TPU v7x, 32 devices: a whole 2x2x4 slice. The times are simulated.
32 devices in a mesh: blk: 4 (over y, x), leaf: 8 (over z, core).
Axes of the slice: x: 2, y: 2, z: 4, core: 2. Of those that a mesh axis runs over, the one named last changes fastest.
Arguments:
- points: bfloat16 [3, 16384], P(None, ('blk', 'leaf')), may hold values from 0 to 1
- test_matrix: bfloat16 [16384, 512], P(('blk', 'leaf')), may hold values from -6 to 6
- near_lists: int32 [64, 5], P(('blk', 'leaf')), may hold values from 0 to 5, as said below
- leaf_pivots: int32 [32, 256], P(('blk', 'leaf')), may hold values from 0 to 511, as said below
- leaf_proj: bfloat16 [16384, 256], P(('blk', 'leaf')), may hold values from -0.25 to 0.25
- merge_pivots: int32 [3, 32, 256], P(None, ('blk', 'leaf')), may hold values from 0 to 511, as said below
- merge_proj: bfloat16 [3, 32, 512, 256], P(None, ('blk', 'leaf')), as said below
Outputs:
- sample: bfloat16 [16384, 512], P(('blk', 'leaf'))
- top_samples: float32 [8192, 512], P(('blk', 'leaf'))
- top_omega: float32 [8192, 512], P(('blk', 'leaf'))
Inputs may be any that keep to these rules, and one draw needn't show every extreme that they name: `near_lists`: the 5 entries of one row are distinct. `leaf_pivots`: the 256 entries of one row are distinct. `merge_pivots`: the 256 entries of one row are distinct; rows [t, n] are equal for all n with the same n // 2^(t+1). `merge_proj`: matrices [t, n] are equal for all n with the same n // 2^(t+1); entries lie within -4 / sqrt(512) to 4 / sqrt(512).
All inputs are finite; a program needn't handle non-finite values.
Results may differ from a plain program's by a relative error of at most 0.0048.
Values may be sent and summed in bfloat16 or wider, within the bound.
No kernel may reach another device: no remote copies, remote signals or barrier semaphores. Data moves between devices by JAX's collectives and lax.ppermute only.
A program may use at most 64 MiB of HBM per device.

v0:
```python
import math

import jax
import jax.numpy as jnp
from jax import lax
from jax.sharding import PartitionSpec as P

SPREAD = 25.0


def shifted(block, axis, distance):
    devices = range(lax.axis_size(axis))
    route = [((i - distance) % len(devices), i) for i in devices]
    return lax.ppermute(block, axis, route)


def swapped(block, axis, stride):
    count = lax.axis_size(axis)
    route = []
    for low in range(count):
        high = low | 1 << stride
        if high != low and high < count:
            route += [(low, high), (high, low)]
    return lax.ppermute(block, axis, route)


def kernel_block(row_points, col_points):
    offsets = row_points[..., :, :, None] - col_points[..., :, None, :]
    return jnp.exp(-SPREAD * jnp.sum(offsets * offsets, axis=-3))


def to_blocks(raw_points, block_count, block_rows):
    return jnp.transpose(
        raw_points.astype(jnp.float32).reshape(3, block_count, block_rows), (1, 0, 2)
    )


def on_device(points, test_matrix, near_lists, leaf_pivots, leaf_proj, merge_pivots, merge_proj):
    row_count = test_matrix.shape[0]
    sample_count = test_matrix.shape[1]
    block_count = near_lists.shape[0]
    slot_count = near_lists.shape[1]
    block_rows = row_count // block_count
    skel_rank = leaf_pivots.shape[1]
    level_count = merge_pivots.shape[0]
    near_amp = 9.0 / math.sqrt(slot_count * block_rows)
    far_amp = 3.0 / math.sqrt(skel_rank)
    highest = lax.Precision.HIGHEST
    own_points = to_blocks(points, block_count, block_rows)
    behind_matrix, behind_points = shifted((test_matrix, points), "blk", 1)
    ahead_matrix, ahead_points = shifted((test_matrix, points), "blk", -1)
    wide_blocks = jnp.concatenate([behind_matrix, test_matrix, ahead_matrix], axis=0).reshape(
        3 * block_count, block_rows, sample_count
    )
    wide_points = jnp.concatenate(
        [
            to_blocks(behind_points, block_count, block_rows),
            own_points,
            to_blocks(ahead_points, block_count, block_rows),
        ],
        axis=0,
    )
    full_sum = jnp.zeros((block_count, block_rows, sample_count), jnp.float32)
    remote_sum = jnp.zeros((block_count, block_rows, sample_count), jnp.float32)
    for entry_slot in range(slot_count):
        candidate = near_lists[:, entry_slot]
        near_block = (
            near_amp * kernel_block(own_points, jnp.take(wide_points, candidate, axis=0))
        ).astype(jnp.bfloat16)
        term_block = jnp.einsum(
            "ipq,iqr->ipr",
            near_block,
            jnp.take(wide_blocks, candidate, axis=0),
            preferred_element_type=jnp.float32,
        )
        is_remote = (candidate // block_count != 1).astype(jnp.float32)[:, None, None]
        full_sum = full_sum + term_block
        remote_sum = remote_sum + is_remote * term_block
    full_sum = full_sum.reshape(row_count, sample_count)
    remote_sum = remote_sum.reshape(row_count, sample_count)
    sample = full_sum.astype(jnp.bfloat16)
    pivots = leaf_pivots[0]
    samples = jnp.take(remote_sum, pivots, axis=0)
    skeleton = jnp.take(points.astype(jnp.float32), pivots, axis=1)
    compressed = lax.dot_general(
        leaf_proj, test_matrix, (((0,), (0,)), ((), ())), preferred_element_type=jnp.float32
    )
    position = lax.axis_index("leaf")
    for tree_level in range(level_count):
        other_samples, other_compressed, other_skeleton = swapped(
            (samples, compressed, skeleton), "leaf", tree_level
        )
        is_left = position >> tree_level & 1 == 0
        left_samples = jnp.where(is_left, samples, other_samples)
        right_samples = jnp.where(is_left, other_samples, samples)
        left_compressed = jnp.where(is_left, compressed, other_compressed)
        right_compressed = jnp.where(is_left, other_compressed, compressed)
        left_skeleton = jnp.where(is_left, skeleton, other_skeleton)
        right_skeleton = jnp.where(is_left, other_skeleton, skeleton)
        coupling = far_amp * kernel_block(left_skeleton, right_skeleton)
        upper_half = left_samples - jnp.dot(coupling, right_compressed, precision=highest)
        lower_half = right_samples - lax.dot_general(
            coupling, left_compressed, (((0,), (0,)), ((), ())), precision=highest
        )
        stacked = jnp.concatenate([upper_half, lower_half], axis=0)
        node_pivots = merge_pivots[tree_level, 0]
        samples = jnp.take(stacked, node_pivots, axis=0)
        skeleton = jnp.take(
            jnp.concatenate([left_skeleton, right_skeleton], axis=1), node_pivots, axis=1
        )
        projection = merge_proj[tree_level, 0].astype(jnp.float32)
        compressed = lax.dot_general(
            projection,
            jnp.concatenate([left_compressed, right_compressed], axis=0),
            (((0,), (0,)), ((), ())),
            precision=highest,
        )
    return (sample, samples, compressed)


def solution(mesh):
    placed = (
        P(None, ("blk", "leaf")),
        P(("blk", "leaf"), None),
        P(("blk", "leaf"), None),
        P(("blk", "leaf"), None),
        P(("blk", "leaf"), None),
        P(None, ("blk", "leaf"), None),
        P(None, ("blk", "leaf"), None, None),
    )
    return jax.shard_map(
        on_device,
        mesh=mesh,
        in_specs=placed,
        out_specs=(P(("blk", "leaf"), None), P(("blk", "leaf"), None), P(("blk", "leaf"), None)),
        check_vma=False,
    )
```

profile of v0, /device:TPU:0, one launch (start us, length us, event | category | flops | bytes accessed | tf_op | source)
XLA Modules:
  0.0 128.7 jit_solution(3302069651075284478)
XLA Ops:
  0.6 3.9 %collective-permute-start.3 = (bf16[512,512]{1,0:T(8,128)(2,1)}, bf16[512,512]{1,0:T(8,128)(2,1)S(1)}, u32[]{:S(2)}, u32[]{:S(2)}) collective-permute-start(bf16[512,512]{1,0:T(8,128)(2,1)} %param.16), channel_id=1, source_target_pairs={{8,0},{16,8},{24,16},{0,24},{9,1},{17,9},{25,17},{1,25},{10,2},{18... | collective-permute-start | bytes 1572872 | tf_op jit(solution)/shard_map/ppermute | solution.py:14
  4.6 2.9 %collective-permute-start.1 = (bf16[3,512]{1,0:T(4,128)(2,1)}, bf16[3,512]{1,0:T(4,128)(2,1)S(1)}, u32[]{:S(2)}, u32[]{:S(2)}) collective-permute-start(bf16[3,512]{1,0:T(4,128)(2,1)} %param.15), channel_id=1, source_target_pairs={{8,0},{16,8},{24,16},{0,24},{9,1},{17,9},{25,17},{1,25},{10,2},{18... | collective-permute-start | bytes 9224 | tf_op jit(solution)/shard_map/ppermute | solution.py:14
  7.5 0.9 copy.68
  8.5 0.7 compare_select_fusion.3
  9.1 0.7 compare_and_fusion.3
  9.9 0.7 gather_fusion.11
  10.8 1.1 slice_reduce_fusion.3
  12.0 0.7 fusion.93
  12.8 0.6 compare_and_fusion
  13.4 1.4 %fusion.94 = f32[256,512]{1,0:T(8,128)S(1)} fusion(bf16[512,256]{1,0:T(8,128)(2,1)S(1)} %copy-done, bf16[512,512]{1,0:T(8,128)(2,1)} %param.16), kind=kOutput, calls=%fused_computation.226 | convolution fusion | flops 134217728 | bytes 1310720 | tf_op jit(solution)/shard_map/dot_general | solution.py:85
  14.9 0.6 collective-permute-start.6
  15.8 11.6 %collective-permute-done.1 = bf16[3,512]{1,0:T(4,128)(2,1)S(1)} collective-permute-done((bf16[3,512]{1,0:T(4,128)(2,1)}, bf16[3,512]{1,0:T(4,128)(2,1)S(1)}, u32[]{:S(2)}, u32[]{:S(2)}) %collective-permute-start.1) | collective-permute-done | bytes 3104 | tf_op jit(solution)/shard_map/ppermute | solution.py:14
  27.4 1.0 collective-permute-done
  28.5 0.6 gather_fusion.2
  29.0 0.6 gather_fusion.4
  29.6 0.6 gather_fusion.6
  30.2 0.6 gather_fusion.8
  30.7 0.6 gather_fusion
  31.3 0.7 gather_fusion.13
  32.1 1.6 %collective-permute-start.8 = (f32[3,256]{0,1:T(8,128)S(1)}, f32[3,256]{0,1:T(8,128)S(1)}, u32[]{:S(2)}, u32[]{:S(2)}) collective-permute-start(f32[3,256]{0,1:T(8,128)S(1)} %select_bitcast_fusion.1), channel_id=1, source_target_pairs={{0,2},{2,0},{1,3},{3,1},{4,6},{6,4},{5,7},{7,5},{8,10},{10,8},{9,1... | collective-permute-start | bytes 9224 | tf_op jit(solution)/shard_map/ppermute | solution.py:24
  34.1 2.3 %multiply_reduce_fusion.3 = (f32[2,256,256]{2,1,0:T(8,128)}, f32[2,256,256]{2,1,0:T(8,128)}, f32[2,256,256]{2,1,0:T(8,128)}, f32[2,256,256]{2,1,0:T(8,128)}, f32[2,256,256]{2,1,0:T(8,128)}) fusion(f32[2,3,256]{2,1,0:T(4,128)S(1)} %broadcast_select_fusion.19, f32[2,3,256]{2,1,0:T(4,128)S(1)} %copy.70, f32[2,3,256]{2,1,0:T(4,128)S(1)} %broadcast_select_fusion.18, ...), kind=kLoop, calls=%fused_computation.21 | loop fusion | flops 5242880 | bytes 2658304 | tf_op jit(solution)/shard_map/reduce_sum | solution.py:29
  36.6 0.5 collective-permute-done.8
  37.5 0.7 gather_fusion.15
  38.2 0.8 select_bitcast_fusion
  39.0 2.6 %collective-permute-start.11 = (f32[3,256]{0,1:T(8,128)}, f32[3,256]{0,1:T(8,128)}, u32[]{:S(2)}, u32[]{:S(2)}) collective-permute-start(f32[3,256]{0,1:T(8,128)} %select_bitcast_fusion), channel_id=1, source_target_pairs={{0,4},{4,0},{1,5},{5,1},{2,6},{6,2},{3,7},{7,3},{8,12},{12,8},{9,1... | collective-permute-start | bytes 9224 | tf_op jit(solution)/shard_map/ppermute | solution.py:24
  41.6 0.8 copy-done.9
  42.4 1.3 %pad_maximum_fusion = bf16[1536,512]{1,0:T(8,128)(2,1)S(1)} fusion(bf16[512,512]{1,0:T(8,128)(2,1)} %copy-done.9, bf16[512,512]{1,0:T(8,128)(2,1)S(1)} %copy-done.6, bf16[512,512]{1,0:T(8,128)(2,1)} %collective-permute-done.2), kind=kLoop, calls=%fused_computation.17 | loop fusion | flops 4718592 | bytes 3145728 | tf_op jit(solution)/shard_map/concatenate | solution.py:52
  43.7 1.4 %gather_fusion.7 = bf16[2,256,512]{2,1,0:T(8,128)(2,1)} fusion(bf16[6,256,512]{2,1,0:T(8,128)(2,1)S(1)} %bitcast.47, s32[1024]{0:T(1024)S(1)} %pad_clamp_fusion.5), kind=kCustom, calls=%fused_computation.10.clone | custom fusion | bytes 1048584 | tf_op jit(solution)/shard_map/jit(_take)/gather | solution.py:73
  45.1 1.4 %gather_fusion.5 = bf16[2,256,512]{2,1,0:T(8,128)(2,1)} fusion(bf16[6,256,512]{2,1,0:T(8,128)(2,1)S(1)} %bitcast.48, s32[1024]{0:T(1024)S(1)} %pad_clamp_fusion.6), kind=kCustom, calls=%fused_computation.9.clone | custom fusion | bytes 1048584 | tf_op jit(solution)/shard_map/jit(_take)/gather | solution.py:73
  46.4 1.4 %gather_fusion.3 = bf16[2,256,512]{2,1,0:T(8,128)(2,1)} fusion(bf16[6,256,512]{2,1,0:T(8,128)(2,1)S(1)} %bitcast.49, s32[1024]{0:T(1024)S(1)} %pad_clamp_fusion.7), kind=kCustom, calls=%fused_computation.8.clone | custom fusion | bytes 1048584 | tf_op jit(solution)/shard_map/jit(_take)/gather | solution.py:73
  47.8 0.6 gather_fusion.1
  48.4 1.4 %gather_fusion.9 = bf16[2,256,512]{2,1,0:T(8,128)(2,1)} fusion(bf16[6,256,512]{2,1,0:T(8,128)(2,1)S(1)} %bitcast.51, s32[1024]{0:T(1024)S(1)} %pad_clamp_fusion.4), kind=kCustom, calls=%fused_computation.11.clone | custom fusion | bytes 1048584 | tf_op jit(solution)/shard_map/jit(_take)/gather | solution.py:73
  49.8 1.7 %fusion.11 = f32[2,256,512]{2,1,0:T(8,128)S(1)} fusion(bf16[2,256,512]{2,1,0:T(8,128)(2,1)} %gather_fusion.7, pred[2]{0:T(512)(128)(4,1)S(1)} %get-tuple-element.56, f32[2,256,256]{2,1,0:T(8,128)} %get-tuple-element.21), kind=kOutput, calls=%fused_computation.45 | convolution fusion | flops 134873088 | bytes 2097154 | tf_op jit(solution)/shard_map/ipq,iqr->ipr/dot_general | solution.py:70
  51.5 0.4 fusion.13
  51.9 0.6 copy-done.1
  53.4 0.6 copy-done.7
  54.2 1.5 %multiply_add_fusion = (f32[2,256,512]{2,1,0:T(8,128)S(1)}, bf16[2,256,512]{2,1,0:T(8,128)(2,1)}) fusion(f32[2,256,512]{2,1,0:T(8,128)S(1)} %fusion.11, f32[2,256,512]{2,1,0:T(8,128)S(1)} %fusion.13, f32[2,256,512]{2,1,0:T(8,128)S(1)} %fusion.15, f32[2,256,512]{2,1,0:T(8,128)S(1)} %fusion.17, f32[2]{0:T(128)S(1)} %get-tuple-element.54, ...), kind=kOutput, calls=%fused_computation.38 | convolution fusion | flops 138543104 | bytes 6815786 | tf_op jit(solution)/shard_map/ipq,iqr->ipr/dot_general | solution.py:70
  55.7 1.0 gather_fusion.10
  57.1 1.1 broadcast_select_fusion.5
  58.2 1.6 %convolution_bitcast_fusion.2 = f32[256,512]{1,0:T(8,128)S(1)} fusion(f32[256,512]{1,0:T(8,128)S(1)} %get-tuple-element.35, f32[256,512]{1,0:T(8,128)S(1)} %get-tuple-element.36, bf16[3,1,512,256]{3,2,1,0:T(8,128)(2,1)} %param.21), kind=kOutput, calls=%fused_computation.25 | convolution fusion | flops 805568512 | bytes 1835008 | tf_op jit(solution)/shard_map/dot_general | solution.py:112
  59.9 1.6 %collective-permute-start.9 = (f32[256,512]{1,0:T(8,128)S(1)}, f32[256,512]{1,0:T(8,128)}, u32[]{:S(2)}, u32[]{:S(2)}) collective-permute-start(f32[256,512]{1,0:T(8,128)S(1)} %convolution_bitcast_fusion.2), channel_id=1, source_target_pairs={{0,2},{2,0},{1,3},{3,1},{4,6},{6,4},{5,7},{7,5},{8,10},{10,8},{9,1... | collective-permute-start | bytes 1572872 | tf_op jit(solution)/shard_map/ppermute | solution.py:24
  61.5 0.7 select_subtract_fusion.4
  62.2 0.7 select_subtract_fusion.5
  62.9 1.0 gather_fusion.12
  64.0 0.5 collective-permute-start.7
  64.5 1.0 broadcast_select_fusion.11
  65.7 9.0 %collective-permute-done.9 = f32[256,512]{1,0:T(8,128)} collective-permute-done((f32[256,512]{1,0:T(8,128)S(1)}, f32[256,512]{1,0:T(8,128)}, u32[]{:S(2)}, u32[]{:S(2)}) %collective-permute-start.9) | collective-permute-done | bytes 524320 | tf_op jit(solution)/shard_map/ppermute | solution.py:24
  74.7 1.1 broadcast_select_fusion.7
  75.9 1.6 %convolution_bitcast_fusion.1 = f32[256,512]{1,0:T(8,128)S(1)} fusion(f32[256,512]{1,0:T(8,128)S(1)} %get-tuple-element.33, f32[256,512]{1,0:T(8,128)S(1)} %get-tuple-element.34, bf16[3,1,512,256]{3,2,1,0:T(8,128)(2,1)} %param.21), kind=kOutput, calls=%fused_computation.24 | convolution fusion | flops 805568512 | bytes 1835008 | tf_op jit(solution)/shard_map/dot_general | solution.py:112
  77.5 0.4 collective-permute-start.12
  77.9 12.4 %collective-permute-done.7 = f32[256,512]{1,0:T(8,128)S(1)} collective-permute-done((f32[256,512]{1,0:T(8,128)S(1)}, f32[256,512]{1,0:T(8,128)S(1)}, u32[]{:S(2)}, u32[]{:S(2)}) %collective-permute-start.7) | collective-permute-done | bytes 524320 | tf_op jit(solution)/shard_map/ppermute | solution.py:24
  90.4 0.7 select_subtract_fusion.2
  91.0 0.7 select_subtract_fusion.3
  91.8 1.0 gather_fusion.14
  92.9 1.7 %collective-permute-start.10 = (f32[256,512]{1,0:T(8,128)S(1)}, f32[256,512]{1,0:T(8,128)S(1)}, u32[]{:S(2)}, u32[]{:S(2)}) collective-permute-start(f32[256,512]{1,0:T(8,128)S(1)} %broadcast_select_fusion.1), channel_id=1, source_target_pairs={{0,4},{4,0},{1,5},{5,1},{2,6},{6,2},{3,7},{7,3},{8,12},{12,8},{9,1... | collective-permute-start | bytes 1572872 | tf_op jit(solution)/shard_map/ppermute | solution.py:24
  94.8 21.1 %collective-permute-done.12 = f32[256,512]{1,0:T(8,128)} collective-permute-done((f32[256,512]{1,0:T(8,128)S(1)}, f32[256,512]{1,0:T(8,128)}, u32[]{:S(2)}, u32[]{:S(2)}) %collective-permute-start.12) | collective-permute-done | bytes 524320 | tf_op jit(solution)/shard_map/ppermute | solution.py:24
  115.9 1.3 %broadcast_select_fusion.9 = (f32[256,512]{1,0:T(8,128)S(1)}, f32[256,512]{1,0:T(8,128)S(1)}) fusion(f32[256,512]{1,0:T(8,128)} %collective-permute-done.12, f32[256,512]{1,0:T(8,128)S(1)} %convolution_bitcast_fusion.1, pred[]{:T(512)S(6)} %eq.9), kind=kLoop, calls=%fused_computation.104 | loop fusion | flops 262144 | bytes 2097153 | tf_op jit(solution)/shard_map/jit(_where)/select_n | solution.py:97
  117.3 1.9 %convolution_bitcast_fusion = f32[256,512]{0,1:T(8,128)S(1)} fusion(f32[256,512]{1,0:T(8,128)S(1)} %get-tuple-element.31, f32[256,512]{1,0:T(8,128)S(1)} %get-tuple-element.32, bf16[3,1,512,256]{3,2,1,0:T(8,128)(2,1)} %param.21), kind=kOutput, calls=%fused_computation.23 | convolution fusion | flops 805568512 | bytes 1835008 | tf_op jit(solution)/shard_map/dot_general | solution.py:112
  119.2 1.0 copy.82
  120.2 5.2 %collective-permute-done.10 = f32[256,512]{1,0:T(8,128)S(1)} collective-permute-done((f32[256,512]{1,0:T(8,128)S(1)}, f32[256,512]{1,0:T(8,128)S(1)}, u32[]{:S(2)}, u32[]{:S(2)}) %collective-permute-start.10) | collective-permute-done | bytes 524320 | tf_op jit(solution)/shard_map/ppermute | solution.py:24
  125.4 0.7 select_subtract_fusion
  126.1 0.7 select_subtract_fusion.1
  126.8 1.0 gather_fusion.16
  127.8 0.9 broadcast_select_fusion
  (88 shorter events, 3.9 us)
Async XLA Ops:
  0.6 12.7 %copy-start = (bf16[512,256]{1,0:T(8,128)(2,1)S(1)}, bf16[512,256]{1,0:T(8,128)(2,1)}, u32[]{:S(2)}) copy-start(bf16[512,256]{1,0:T(8,128)(2,1)} %param.19) | copy-start | bytes 786436
  0.6 40.9 %collective-permute-start.3 = (bf16[512,512]{1,0:T(8,128)(2,1)}, bf16[512,512]{1,0:T(8,128)(2,1)S(1)}, u32[]{:S(2)}, u32[]{:S(2)}) collective-permute-start(bf16[512,512]{1,0:T(8,128)(2,1)} %param.16), channel_id=1, source_target_pairs={{8,0},{16,8},{24,16},{0,24},{9,1},{17,9},{25,17},{1,25},{10,2},{18... | collective-permute-start | bytes 1572872 | tf_op jit(solution)/shard_map/ppermute | solution.py:14
  4.6 37.8 %collective-permute-start.2 = (bf16[512,512]{1,0:T(8,128)(2,1)}, bf16[512,512]{1,0:T(8,128)(2,1)}, u32[]{:S(2)}, u32[]{:S(2)}) collective-permute-start(bf16[512,512]{1,0:T(8,128)(2,1)} %param.16), channel_id=1, source_target_pairs={{24,0},{0,8},{8,16},{16,24},{25,1},{1,9},{9,17},{17,25},{26,2},{2,... | collective-permute-start | bytes 1572872 | tf_op jit(solution)/shard_map/ppermute | solution.py:14
  4.6 22.8 %collective-permute-start.1 = (bf16[3,512]{1,0:T(4,128)(2,1)}, bf16[3,512]{1,0:T(4,128)(2,1)S(1)}, u32[]{:S(2)}, u32[]{:S(2)}) collective-permute-start(bf16[3,512]{1,0:T(4,128)(2,1)} %param.15), channel_id=1, source_target_pairs={{8,0},{16,8},{24,16},{0,24},{9,1},{17,9},{25,17},{1,25},{10,2},{18... | collective-permute-start | bytes 9224 | tf_op jit(solution)/shard_map/ppermute | solution.py:14
  7.5 20.9 %collective-permute-start = (bf16[3,512]{1,0:T(4,128)(2,1)}, bf16[3,512]{1,0:T(4,128)(2,1)S(1)}, u32[]{:S(2)}, u32[]{:S(2)}) collective-permute-start(bf16[3,512]{1,0:T(4,128)(2,1)} %param.15), channel_id=1, source_target_pairs={{24,0},{0,8},{8,16},{16,24},{25,1},{1,9},{9,17},{17,25},{26,2},{2,... | collective-permute-start | bytes 9224 | tf_op jit(solution)/shard_map/ppermute | solution.py:14
  10.7 4.2 %collective-permute-start.5 = (f32[3,256]{0,1:T(8,128)S(1)}, f32[3,256]{0,1:T(8,128)S(1)}, u32[]{:S(2)}, u32[]{:S(2)}) collective-permute-start(f32[3,256]{0,1:T(8,128)S(1)} %select_bitcast_fusion.2), channel_id=1, source_target_pairs={{0,1},{1,0},{2,3},{3,2},{4,5},{5,4},{6,7},{7,6},{8,9},{9,8},{10,11... | collective-permute-start | bytes 9224 | tf_op jit(solution)/shard_map/ppermute | solution.py:24
  12.7 24.5 %copy-start.10 = (pred[256]{0:T(512)(128)(4,1)}, pred[256]{0:T(512)(128)(4,1)S(1)}, u32[]{:S(2)}) copy-start(pred[256]{0:T(512)(128)(4,1)S(1)} %compare_and_fusion.2) | copy-start | bytes 772
  14.9 42.1 %collective-permute-start.6 = (f32[256,512]{1,0:T(8,128)S(1)}, f32[256,512]{1,0:T(8,128)}, u32[]{:S(2)}, u32[]{:S(2)}) collective-permute-start(f32[256,512]{1,0:T(8,128)S(1)} %fusion.94), channel_id=1, source_target_pairs={{0,1},{1,0},{2,3},{3,2},{4,5},{5,4},{6,7},{7,6},{8,9},{9,8},{10,11... | collective-permute-start | bytes 1572872 | tf_op jit(solution)/shard_map/ppermute | solution.py:24
  32.1 5.0 %collective-permute-start.8 = (f32[3,256]{0,1:T(8,128)S(1)}, f32[3,256]{0,1:T(8,128)S(1)}, u32[]{:S(2)}, u32[]{:S(2)}) collective-permute-start(f32[3,256]{0,1:T(8,128)S(1)} %select_bitcast_fusion.1), channel_id=1, source_target_pairs={{0,2},{2,0},{1,3},{3,1},{4,6},{6,4},{5,7},{7,5},{8,10},{10,8},{9,1... | collective-permute-start | bytes 9224 | tf_op jit(solution)/shard_map/ppermute | solution.py:24
  36.5 5.9 %copy-start.6 = (bf16[512,512]{1,0:T(8,128)(2,1)S(1)}, bf16[512,512]{1,0:T(8,128)(2,1)}, u32[]{:S(2)}) copy-start(bf16[512,512]{1,0:T(8,128)(2,1)} %param.16) | copy-start | bytes 1572868
  39.0 25.6 %collective-permute-start.11 = (f32[3,256]{0,1:T(8,128)}, f32[3,256]{0,1:T(8,128)}, u32[]{:S(2)}, u32[]{:S(2)}) collective-permute-start(f32[3,256]{0,1:T(8,128)} %select_bitcast_fusion), channel_id=1, source_target_pairs={{0,4},{4,0},{1,5},{5,1},{2,6},{6,2},{3,7},{7,3},{8,12},{12,8},{9,1... | collective-permute-start | bytes 9224 | tf_op jit(solution)/shard_map/ppermute | solution.py:24
  41.6 0.8 copy-start.9
  49.8 1.7 %copy-start.2 = (bf16[2,256,512]{2,1,0:T(8,128)(2,1)S(1)}, bf16[2,256,512]{2,1,0:T(8,128)(2,1)}, u32[]{:S(2)}) copy-start(bf16[2,256,512]{2,1,0:T(8,128)(2,1)} %gather_fusion.5) | copy-start | bytes 1572868
  49.8 1.7 %copy-start.5 = (f32[2,256,256]{2,1,0:T(8,128)S(1)}, f32[2,256,256]{2,1,0:T(8,128)}, u32[]{:S(2)}) copy-start(f32[2,256,256]{2,1,0:T(8,128)} %get-tuple-element.20) | copy-start | bytes 1572868
  51.4 1.0 copy-start.1
  51.5 1.2 copy-start.4
  51.9 1.2 copy-start.3
  53.0 1.0 copy-start.7
  53.0 1.2 copy-start.8
  56.8 4.7 %collective-permute-start.4 = (f32[256,512]{1,0:T(8,128)S(1)}, f32[256,512]{1,0:T(8,128)S(1)}, u32[]{:S(2)}, u32[]{:S(2)}) collective-permute-start(f32[256,512]{1,0:T(8,128)S(1)} %broadcast_select_fusion.3), channel_id=1, source_target_pairs={{0,1},{1,0},{2,3},{3,2},{4,5},{5,4},{6,7},{7,6},{8,9},{9,8},{10,11... | collective-permute-start | bytes 1572872 | tf_op jit(solution)/shard_map/ppermute | solution.py:24
  59.9 14.9 %collective-permute-start.9 = (f32[256,512]{1,0:T(8,128)S(1)}, f32[256,512]{1,0:T(8,128)}, u32[]{:S(2)}, u32[]{:S(2)}) collective-permute-start(f32[256,512]{1,0:T(8,128)S(1)} %convolution_bitcast_fusion.2), channel_id=1, source_target_pairs={{0,2},{2,0},{1,3},{3,1},{4,6},{6,4},{5,7},{7,5},{8,10},{10,8},{9,1... | collective-permute-start | bytes 1572872 | tf_op jit(solution)/shard_map/ppermute | solution.py:24
  62.9 1.0 copy-start.11
  64.0 26.3 %collective-permute-start.7 = (f32[256,512]{1,0:T(8,128)S(1)}, f32[256,512]{1,0:T(8,128)S(1)}, u32[]{:S(2)}, u32[]{:S(2)}) collective-permute-start(f32[256,512]{1,0:T(8,128)S(1)} %broadcast_select_fusion.2), channel_id=1, source_target_pairs={{0,2},{2,0},{1,3},{3,1},{4,6},{6,4},{5,7},{7,5},{8,10},{10,8},{9,1... | collective-permute-start | bytes 1572872 | tf_op jit(solution)/shard_map/ppermute | solution.py:24
  77.5 38.4 %collective-permute-start.12 = (f32[256,512]{1,0:T(8,128)S(1)}, f32[256,512]{1,0:T(8,128)}, u32[]{:S(2)}, u32[]{:S(2)}) collective-permute-start(f32[256,512]{1,0:T(8,128)S(1)} %convolution_bitcast_fusion.1), channel_id=1, source_target_pairs={{0,4},{4,0},{1,5},{5,1},{2,6},{6,2},{3,7},{7,3},{8,12},{12,8},{9,1... | collective-permute-start | bytes 1572872 | tf_op jit(solution)/shard_map/ppermute | solution.py:24
  92.9 32.5 %collective-permute-start.10 = (f32[256,512]{1,0:T(8,128)S(1)}, f32[256,512]{1,0:T(8,128)S(1)}, u32[]{:S(2)}, u32[]{:S(2)}) collective-permute-start(f32[256,512]{1,0:T(8,128)S(1)} %broadcast_select_fusion.1), channel_id=1, source_target_pairs={{0,4},{4,0},{1,5},{5,1},{2,6},{6,2},{3,7},{7,3},{8,12},{12,8},{9,1... | collective-permute-start | bytes 1572872 | tf_op jit(solution)/shard_map/ppermute | solution.py:24
  126.8 1.0 copy-start.12
where the time goes:
time: 129 us
  waiting for transfers between devices  61 us (47%)
  local copies, waits for them, and re-layouts  21.8 us (17%)
  starting transfers between devices  16.1 us (12%)
  matrix products  14.9 us (12%)
  other arithmetic  13.8 us (11%)
    ppermute x9, waiting for transfers between devices, swapped(): return lax.ppermute(block, axis, route)  48.3 us
    ppermute x4, waiting for transfers between devices, shifted(): return lax.ppermute(block, axis, route)  12.6 us
    ppermute x9, starting transfers between devices, swapped(): return lax.ppermute(block, axis, route)  9.24 us
    ppermute x4, starting transfers between devices, shifted(): return lax.ppermute(block, axis, route)  6.87 us
    gather x5, local copies, waits for them, and re-layouts, on_device(): jnp.take(wide_blocks, candidate, axis=0)  6.08 us
    dot_general x3, matrix products, on_device(): lax.dot_general(projection, jnp.concatenate([left_compressed, right_compr...  5.24 us
    unnamed x28, local copies, waits for them, and re-layouts  4.31 us
    dot_general x5, matrix products, on_device(): jnp.einsum('ipq,iqr->ipr', near_block, jnp.take(wide_blocks, candidate, a...  4.29 us
  transfers between devices with their start and end apart: 13, of which 7 were waited for; matrix products, arithmetic and copies ran while one was open for 35% of the time, Pallas kernels for 0%

commit v1 on v0

v1 whole, which is shorter than its diff:
```python
import functools
import math

import jax
import jax.numpy as jnp
from jax import lax
from jax.experimental import pallas as pl
from jax.experimental.pallas import tpu as pltpu
from jax.sharding import PartitionSpec as P

SPREAD = 25.0
EXPONENT = -SPREAD * math.log2(math.e)
FAR_OFF = 1024.0
HEIGHT = 16
ROW_HI, ROW_LO, MEET, PIVOT = 3, 4, 5, 6
BF16, F32 = jnp.bfloat16, jnp.float32


def call(body, outs, flops, *args):
    specs = [
        pl.BlockSpec(memory_space=pltpu.SMEM if a.dtype == jnp.int32 and a.ndim == 2 and a.shape[1] < 128 else pltpu.VMEM)
        for a in args
    ]
    moved = sum(a.size * a.dtype.itemsize for a in args) + sum(
        math.prod(s) * jnp.dtype(d).itemsize for s, d in outs
    )
    return pl.pallas_call(
        body,
        out_shape=[jax.ShapeDtypeStruct(s, d) for s, d in outs],
        in_specs=specs,
        out_specs=[pl.BlockSpec(memory_space=pltpu.VMEM)] * len(outs),
        compiler_params=pltpu.CompilerParams(vmem_limit_bytes=40 << 20),
        cost_estimate=pl.CostEstimate(flops=flops, bytes_accessed=moved, transcendentals=0),
    )(*args)


def dot(a, b, over_a=1, over_b=0):
    return lax.dot_general(a, b, (((over_a,), (over_b,)), ((), ())), preferred_element_type=F32)


def halves(x):
    hi = x.astype(BF16)
    return hi, (x - hi.astype(F32)).astype(BF16)


def rows_of(entries, width):
    row = lax.broadcasted_iota(jnp.int32, (HEIGHT, width), 0)
    out = jnp.zeros((HEIGHT, width), F32)
    for k, entry in enumerate(entries):
        out = jnp.where(row == k, entry, out)
    return out


def norm_parts(p):
    n = p[0:1] * p[0:1] + p[1:2] * p[1:2] + p[2:3] * p[2:3]
    hi = n.astype(BF16).astype(F32)
    mid = (n - hi).astype(BF16).astype(F32)
    return [hi, mid, n - hi - mid]


def left_features(p, penalties):
    entries = [p[0:1], p[1:2], p[2:3], *norm_parts(p), 1.0, 1.0, 1.0, *penalties]
    return rows_of(entries, p.shape[1]).astype(BF16)


def right_features(p, marks):
    entries = [-2.0 * p[0:1], -2.0 * p[1:2], -2.0 * p[2:3], 1.0, 1.0, 1.0, *norm_parts(p), *marks]
    return rows_of(entries, p.shape[1]).astype(BF16)


def gauss(left, right, amp):
    return jnp.exp2(EXPONENT * dot(left, right, 0, 0)) * amp


def lane_index(width):
    return lax.broadcasted_iota(jnp.int32, (1, width), 1)


def chosen(attributes, index):
    spot = lax.broadcasted_iota(jnp.int32, (attributes.shape[1], index.shape[1]), 0)
    one_hot = jnp.where(spot == index, 1.0, 0.0).astype(BF16)
    return dot(attributes.astype(BF16), one_hot)


def bit_of(value, place):
    return (value >> place) & 1


def describe_body(points_ref, pivots_ref, merges_ref, out_ref):
    p = points_ref[...].astype(F32)
    width = p.shape[1]
    rank = pivots_ref.shape[1]
    spot = lane_index(width)
    attributes = rows_of(
        [p[0:1], p[1:2], p[2:3], (spot // rank).astype(F32), (spot % rank).astype(F32)], width
    )
    skeleton = chosen(attributes, pivots_ref[...])
    row = lax.broadcasted_iota(jnp.int32, skeleton.shape, 0)
    for level in range(merges_ref.shape[0] - 1):
        q = merges_ref[level]
        skeleton = jnp.where(row == PIVOT + 2 * level, (q // rank).astype(F32), skeleton)
        skeleton = jnp.where(row == PIVOT + 2 * level + 1, (q % rank).astype(F32), skeleton)
    out_ref[...] = skeleton.astype(BF16)


def compress_body(proj_ref, matrix_ref, merge_ref, *outs):
    position = lax.axis_index("leaf")
    levels = merge_ref.shape[0]
    rank = proj_ref.shape[1]
    c = dot(proj_ref[...], matrix_ref[...], 0, 0)
    for level in range(levels):
        hi, lo = halves(c)
        outs[0][pl.ds(level * rank, rank), :] = hi
        outs[1][pl.ds(level * rank, rank), :] = lo
        start = pl.multiple_of(bit_of(position, level) * rank, rank)
        m = merge_ref[level, 0, pl.ds(start, rank), :]
        c = dot(m, hi, 0, 0) + dot(m, lo, 0, 0)
    outs[2][...] = c


def tree_body(far_amp, md_ref, merges_ref, hi_ref, lo_ref, top_ref, part_ref):
    position = lax.axis_index("leaf")
    levels = merges_ref.shape[0]
    rank = merges_ref.shape[2]
    nodes = [md_ref[k].astype(F32) for k in range(md_ref.shape[0])]
    pivots = nodes
    row = lax.broadcasted_iota(jnp.int32, (HEIGHT, rank), 0)
    path = []
    for level in range(levels):
        path.append(nodes[0])
        flip = bit_of(position, level)
        merged = []
        for j in range(len(nodes) // 2):
            if level < levels - 1:
                source = pivots[j << level + 1]
                k = PIVOT + 2 * level
                q = (source[k : k + 1] * rank + source[k + 1 : k + 2]).astype(jnp.int32)
            else:
                q = merges_ref[level]
            q = jnp.where(flip == 1, jnp.where(q < rank, q + rank, q - rank), q)
            far = jnp.where(row == MEET, float(level + 1), nodes[2 * j + 1])
            merged.append(chosen(jnp.concatenate([nodes[2 * j], far], axis=1), q))
        nodes = merged
    top = nodes[0]
    top_ref[...] = top
    total = jnp.zeros(part_ref.shape, F32)
    for level in range(levels):
        penalty = jnp.where(top[MEET : MEET + 1] == float(level + 1), 0.0, FAR_OFF)
        block = gauss(left_features(top, [penalty]), right_features(path[level], [1.0]), -far_amp)
        block_hi, block_lo = halves(block)
        hi = hi_ref[pl.ds(level * rank, rank), :]
        lo = lo_ref[pl.ds(level * rank, rank), :]
        total += dot(block_hi, hi) + dot(block_hi, lo) + dot(block_lo, hi)
    part_ref[...] = total


def penalty_table(lists_ref, base, blocks):
    table = []
    for i in range(blocks):
        line = []
        for k in range(blocks):
            listed = lists_ref[i, 0] == base + k
            for slot in range(1, lists_ref.shape[1]):
                listed |= lists_ref[i, slot] == base + k
            line.append(jnp.where(listed, 0.0, FAR_OFF))
        table.append(line)
    return table


def per_block(block_index, values):
    out = jnp.zeros(block_index.shape, F32)
    for i, value in enumerate(values):
        out = jnp.where(block_index == i, value, out)
    return out


def near_body(near_amp, even_ahead, lists_ref, own_ref, first_ref, second_ref, top_ref, matrix_ref, *outs):
    near_first, near_second, top_first, top_second, own_terms = outs
    blocks = lists_ref.shape[0]
    own = own_ref[...].astype(F32)
    width = own.shape[1]
    block_rows = width // blocks
    spot = lane_index(width) // block_rows
    marks = [jnp.where(spot == k, 1.0, 0.0) for k in range(blocks)]
    top = top_ref[...]
    top_block = top[ROW_HI : ROW_HI + 1].astype(jnp.int32)
    top_here = top[MEET : MEET + 1] == 0.0
    if even_ahead:
        odd = lax.axis_index("blk") % 2
        bases = [2 * blocks * (1 - odd), 2 * blocks * odd]
    else:
        bases = [0, 2 * blocks]
    for ref, base, near_ref, part_ref in (
        (first_ref, bases[0], near_first, top_first),
        (second_ref, bases[1], near_second, top_second),
    ):
        table = penalty_table(lists_ref, base, blocks)
        columns = right_features(ref[0:3, :].astype(F32), marks)
        penalties = [per_block(spot, [table[i][k] for i in range(blocks)]) for k in range(blocks)]
        near_ref[...] = gauss(left_features(own, penalties), columns, near_amp).astype(BF16)
        penalties = [
            jnp.where(top_here, per_block(top_block, [table[i][k] for i in range(blocks)]), FAR_OFF)
            for k in range(blocks)
        ]
        part_ref[...] = gauss(left_features(top, penalties), columns, near_amp).astype(BF16)
    table = penalty_table(lists_ref, blocks, blocks)
    penalties = [per_block(spot, [table[i][k] for i in range(blocks)]) for k in range(blocks)]
    near_own = gauss(left_features(own, penalties), right_features(own, marks), near_amp).astype(BF16)
    own_terms[...] = dot(near_own, matrix_ref[...])


def product_body(skip, *refs):
    start_ref, first_ref, second_ref, *chunks, out_ref = refs
    total = start_ref[...]
    per_side = len(chunks) // 2
    for side, left_ref in enumerate((first_ref, second_ref)):
        at = 0
        for k, chunk_ref in enumerate(chunks[side * per_side : (side + 1) * per_side]):
            lead = skip if k == 0 else 0
            count = chunk_ref.shape[0] - lead
            total += dot(left_ref[:, at : at + count], chunk_ref[lead:, :])
            at += count
    out_ref[...] = total.astype(out_ref.dtype)


def permuted(block, axis, route):
    return lax.ppermute(block, axis, [(route(i), i) for i in range(lax.axis_size(axis))])


def swapped(block, distance):
    return permuted(block, "leaf", lambda i: i ^ distance)


def group_sum(part, levels):
    second = bit_of(lax.axis_index("leaf"), 0) == 1
    middle = part.shape[1] // 2
    low, high = part[:, :middle], part[:, middle:]
    kept = jnp.where(second, high, low)
    given = jnp.where(second, low, high).astype(BF16)
    mine = (kept + swapped(given, 1).astype(F32)).astype(BF16)
    total = mine.astype(F32)
    for distance in range(2, 1 << levels, 2):
        total = total + swapped(mine, distance).astype(F32)
    other = swapped(total.astype(BF16), 1).astype(F32)
    return jnp.where(
        second, jnp.concatenate([other, total], axis=1), jnp.concatenate([total, other], axis=1)
    )


def on_device(points, test_matrix, near_lists, leaf_pivots, leaf_proj, merge_pivots, merge_proj):
    row_count, sample_count = test_matrix.shape
    block_count, slot_count = near_lists.shape
    skel_rank = leaf_pivots.shape[1]
    level_count = merge_pivots.shape[0]
    near_amp = 9.0 / math.sqrt(slot_count * (row_count // block_count))
    far_amp = 3.0 / math.sqrt(skel_rank)
    square = 2 * skel_rank * skel_rank * sample_count

    count = lax.axis_size("blk")
    paired = count % 2 == 0 and count > 2
    lead = HEIGHT
    headed = jnp.concatenate([jnp.pad(points, ((0, lead - 3), (0, 0))), test_matrix], axis=0)
    if paired:
        cut = row_count // 4
        edges = [0, lead + cut, lead + 2 * cut, lead + 3 * cut, lead + 4 * cut]
        chunks = [headed[a:b] for a, b in zip(edges[:-1], edges[1:])]
        step = lambda i, by: (i + (by if i % 2 == 0 else -by)) % count
        first = [permuted(c, "blk", lambda i: step(i, 1)) for c in chunks[:3]]
        straight = permuted(chunks[3], "blk", lambda i: step(i, -1))
        first.append(permuted(chunks[3], "blk", lambda i: step(i, 1)))
        second = [permuted(c, "blk", lambda i: step(i, -2)) for c in first[:3]]
        second.append(straight)
    else:
        first = [permuted(headed, "blk", lambda i: (i - 1) % count)]
        second = [permuted(headed, "blk", lambda i: (i + 1) % count)]

    (own_md,) = call(
        describe_body, [((HEIGHT, skel_rank), BF16)], 0, points, leaf_pivots, merge_pivots
    )
    pair = jnp.stack([own_md, swapped(own_md, 1)])
    md = jnp.concatenate([pair] + [swapped(pair, d) for d in range(2, 1 << level_count, 2)], axis=0)

    hi, lo, omega_part = call(
        compress_body,
        [((level_count * skel_rank, sample_count), BF16)] * 2 + [((skel_rank, sample_count), F32)],
        8 * square,
        leaf_proj,
        test_matrix,
        merge_proj,
    )
    top_omega = group_sum(omega_part, level_count)
    top, far_part = call(
        functools.partial(tree_body, far_amp),
        [((HEIGHT, skel_rank), F32), ((skel_rank, sample_count), F32)],
        9 * square,
        md,
        merge_pivots,
        hi,
        lo,
    )
    near_first, near_second, top_first, top_second, own_terms = call(
        functools.partial(near_body, near_amp, paired),
        [((row_count, row_count), BF16)] * 2
        + [((skel_rank, row_count), BF16)] * 2
        + [((row_count, sample_count), F32)],
        8 * square,
        near_lists,
        points,
        first[0],
        second[0],
        top,
        test_matrix,
    )
    product = functools.partial(product_body, lead)
    (samples_part,) = call(
        product, [((skel_rank, sample_count), F32)], 4 * square, far_part, top_first, top_second, *first, *second
    )
    top_samples = group_sum(samples_part, level_count)
    (sample,) = call(
        product, [((row_count, sample_count), BF16)], 8 * square, own_terms, near_first, near_second, *first, *second
    )
    return (sample, top_samples, top_omega)


def solution(mesh):
    placed = (
        P(None, ("blk", "leaf")),
        P(("blk", "leaf"), None),
        P(("blk", "leaf"), None),
        P(("blk", "leaf"), None),
        P(("blk", "leaf"), None),
        P(None, ("blk", "leaf"), None),
        P(None, ("blk", "leaf"), None, None),
    )
    return jax.shard_map(
        on_device,
        mesh=mesh,
        in_specs=placed,
        out_specs=(P(("blk", "leaf"), None), P(("blk", "leaf"), None), P(("blk", "leaf"), None)),
        check_vma=False,
    )
```

time: 129 us -> 66.9 us (0.52)
  waiting for transfers between devices: 61 us -> 24.3 us
  local copies, waits for them, and re-layouts: 21.8 us -> 1.02 us
  matrix products: 14.9 us -> 0 us
  starting transfers between devices: 16.1 us -> 30 us
  other arithmetic: 13.8 us -> 3.03 us
  Pallas kernels: 0 us -> 7.44 us
    ppermute x13 -> x22, waiting for transfers between devices: 61 us -> 24.3 us  [permuted(): lax.ppermute(block, axis, [(route(i), i) for i in range(lax.axis_size(axi...]
    gather x17 -> x0, local copies, waits for them, and re-layouts: 15 us -> none  [the longest x5 6.08 us: on_device(): jnp.take(wide_blocks, candidate, axis=0)]
    dot_general x15 -> x0, matrix products: 14.9 us -> none  [the longest x3 5.24 us: on_device(): lax.dot_general(projection, jnp.concatenate([left_compressed, right_compr...]
    ppermute x13 -> x22, starting transfers between devices: 16.1 us -> 30 us  [permuted(): lax.ppermute(block, axis, [(route(i), i) for i in range(lax.axis_size(axi...]
    pallas_call x0 -> x6, Pallas kernels: none -> 7.44 us  [call(): pl.pallas_call(body, out_shape=[jax.ShapeDtypeStruct(s, d) for s, d in ou...]
    select_n x25 -> x2, other arithmetic: 8.02 us -> 1.68 us  [group_sum(): jnp.where(second, jnp.concatenate([other, total], axis=1), jnp.concatenat...]
    unnamed x28 -> x18, local copies, waits for them, and re-layouts: 4.31 us -> 0.99 us
    reduce_sum x4 -> x0, other arithmetic: 2.81 us -> none  [kernel_block(): return jnp.exp(-SPREAD * jnp.sum(offsets * offsets, axis=-3))]
  transfers between devices with their start and end apart: 13 -> 22, of which waited for: 7 -> 7; matrix products, arithmetic and copies ran while one was open for 35% -> 2% of each run, Pallas kernels for 0% -> 11%
where the time goes in v1:
time: 66.9 us; the launch traced here: 66.7 us
  starting transfers between devices  30 us (45%)
  waiting for transfers between devices  24.3 us (36%)
  Pallas kernels  7.44 us (11%)
  other arithmetic  3.03 us (5%)
  local copies, waits for them, and re-layouts  1.02 us (2%)
  between operations  0.86 us (1%)
    ppermute x22, starting transfers between devices, permuted(): lax.ppermute(block, axis, [(route(i), i) for i in range(lax.axis_size(axi...  30 us
    ppermute x22, waiting for transfers between devices, permuted(): lax.ppermute(block, axis, [(route(i), i) for i in range(lax.axis_size(axi...  24.3 us
    pallas_call x6, Pallas kernels, call(): pl.pallas_call(body, out_shape=[jax.ShapeDtypeStruct(s, d) for s, d in ou...  7.44 us
    select_n x2, other arithmetic, group_sum(): jnp.where(second, jnp.concatenate([other, total], axis=1), jnp.concatenat...  1.68 us
  transfers between devices with their start and end apart: 22, of which 7 were waited for; matrix products, arithmetic and copies ran while one was open for 2% of the time, Pallas kernels for 11%

profile of v1, /device:TPU:0, one launch (start us, length us, event | category | flops | bytes accessed | tf_op | source)
XLA Modules:
  0.0 66.7 jit_solution(8208907227385381364)
XLA Ops:
  0.6 0.0 copy-start.1
  0.6 0.0 copy-start
  0.7 0.0 copy-start.3
  0.7 0.0 copy-start.2
  0.7 0.0 copy-start.4
  0.7 1.0 %fusion.1 = bf16[144,512]{1,0:T(8,128)(2,1)S(1)} fusion(bf16[512,512]{1,0:T(8,128)(2,1)} %matrix_ref.3, bf16[3,512]{1,0:T(4,128)(2,1)} %own_ref.1), kind=kLoop, calls=%fused_computation.10 | loop fusion | flops 516096 | bytes 674816 | tf_op jit(solution)/shard_map/concatenate | solution.py:262
  1.7 3.0 %collective-permute-start = (bf16[144,512]{1,0:T(8,128)(2,1)S(1)}, bf16[144,512]{1,0:T(8,128)(2,1)S(1)}, u32[]{:S(2)}, u32[]{:S(2)}) collective-permute-start(bf16[144,512]{1,0:T(8,128)(2,1)S(1)} %fusion.1), channel_id=1, source_target_pairs={{8,0},{0,8},{24,16},{16,24},{9,1},{1,9},{25,17},{17,25},{10,2},{2,... | collective-permute-start | bytes 442376 | tf_op jit(solution)/shard_map/ppermute | solution.py:227
  4.7 0.0 copy-done.1
  4.7 0.2 shard_map.94
  4.9 0.0 collective-permute-start.2
  4.9 0.1 collective-permute-start.6
  5.0 2.0 %collective-permute-start.7 = (bf16[128,512]{1,0:T(8,128)(2,1)S(1)}, bf16[128,512]{1,0:T(8,128)(2,1)S(1)}, u32[]{:S(2)}, u32[]{:S(2)}) collective-permute-start(bf16[128,512]{1,0:T(8,128)(2,1)S(1)} %get-tuple-element.29), channel_id=1, source_target_pairs={{8,0},{0,8},{24,16},{16,24},{9,1},{1,9},{25,17},{17,25},{10,2},{2,... | collective-permute-start | bytes 393224 | tf_op jit(solution)/shard_map/ppermute | solution.py:227
  7.0 0.1 collective-permute-start.8
  7.1 0.9 %copy-done.5 = bf16[512,256]{1,0:T(8,128)(2,1)S(1)} copy-done((bf16[512,256]{1,0:T(8,128)(2,1)S(1)}, bf16[512,256]{1,0:T(8,128)(2,1)}, u32[]{:S(2)}) %copy-start.5) | copy-done | bytes 262168
  8.1 1.2 %shard_map.95 = (bf16[768,512]{1,0:T(8,128)(2,1)S(1)}, bf16[768,512]{1,0:T(8,128)(2,1)S(1)}, f32[256,512]{1,0:T(8,128)S(1)}) custom-call(bf16[512,256]{1,0:T(8,128)(2,1)S(1)} %copy-done.5, bf16[512,512]{1,0:T(8,128)(2,1)S(1)} %copy-done, bf16[3,1,512,256]{3,2,1,0:T(8,128)(2,1)S(1)} %copy-done.4), custom_call_target="tpu_custom_call" | custom-call | flops 536870912 | bytes 3670016 | tf_op jit(solution)/shard_map/pallas_call | solution.py:27
  9.3 0.0 collective-permute-done.2
  9.3 2.1 %collective-permute-start.3 = (bf16[2,16,256]{2,1,0:T(8,128)(2,1)S(1)}, bf16[2,16,256]{2,1,0:T(8,128)(2,1)S(1)}, u32[]{:S(2)}, u32[]{:S(2)}) collective-permute-start(bf16[2,16,256]{2,1,0:T(8,128)(2,1)S(1)} %pad_maximum_fusion), channel_id=1, source_target_pairs={{2,0},{3,1},{0,2},{1,3},{6,4},{7,5},{4,6},{5,7},{10,8},{11,9},{8,1... | collective-permute-start | bytes 49160 | tf_op jit(solution)/shard_map/ppermute | solution.py:227
  11.4 1.7 %collective-permute-done.3 = bf16[2,16,256]{2,1,0:T(8,128)(2,1)S(1)} collective-permute-done((bf16[2,16,256]{2,1,0:T(8,128)(2,1)S(1)}, bf16[2,16,256]{2,1,0:T(8,128)(2,1)S(1)}, u32[]{:S(2)}, u32[]{:S(2)}) %collective-permute-start.3) | collective-permute-done | bytes 16416 | tf_op jit(solution)/shard_map/ppermute | solution.py:227
  13.1 3.0 %collective-permute-start.4 = (bf16[2,16,256]{2,1,0:T(8,128)(2,1)S(1)}, bf16[2,16,256]{2,1,0:T(8,128)(2,1)S(1)}, u32[]{:S(2)}, u32[]{:S(2)}) collective-permute-start(bf16[2,16,256]{2,1,0:T(8,128)(2,1)S(1)} %pad_maximum_fusion), channel_id=1, source_target_pairs={{4,0},{5,1},{6,2},{7,3},{0,4},{1,5},{2,6},{3,7},{12,8},{13,9},{14,... | collective-permute-start | bytes 49160 | tf_op jit(solution)/shard_map/ppermute | solution.py:227
  16.1 1.7 %collective-permute-done.4 = bf16[2,16,256]{2,1,0:T(8,128)(2,1)S(1)} collective-permute-done((bf16[2,16,256]{2,1,0:T(8,128)(2,1)S(1)}, bf16[2,16,256]{2,1,0:T(8,128)(2,1)S(1)}, u32[]{:S(2)}, u32[]{:S(2)}) %collective-permute-start.4) | collective-permute-done | bytes 16416 | tf_op jit(solution)/shard_map/ppermute | solution.py:227
  17.9 4.0 %collective-permute-start.5 = (bf16[2,16,256]{2,1,0:T(8,128)(2,1)S(1)}, bf16[2,16,256]{2,1,0:T(8,128)(2,1)S(1)}, u32[]{:S(2)}, u32[]{:S(2)}) collective-permute-start(bf16[2,16,256]{2,1,0:T(8,128)(2,1)S(1)} %pad_maximum_fusion), channel_id=1, source_target_pairs={{6,0},{7,1},{4,2},{5,3},{2,4},{3,5},{0,6},{1,7},{14,8},{15,9},{12,... | collective-permute-start | bytes 49160 | tf_op jit(solution)/shard_map/ppermute | solution.py:227
  21.9 1.7 %collective-permute-done.5 = bf16[2,16,256]{2,1,0:T(8,128)(2,1)S(1)} collective-permute-done((bf16[2,16,256]{2,1,0:T(8,128)(2,1)S(1)}, bf16[2,16,256]{2,1,0:T(8,128)(2,1)S(1)}, u32[]{:S(2)}, u32[]{:S(2)}) %collective-permute-start.5) | collective-permute-done | bytes 16416 | tf_op jit(solution)/shard_map/ppermute | solution.py:227
  23.6 2.6 %collective-permute-start.11 = (bf16[128,512]{1,0:T(8,128)(2,1)S(1)}, bf16[128,512]{1,0:T(8,128)(2,1)S(1)}, u32[]{:S(2)}, u32[]{:S(2)}) collective-permute-start(bf16[128,512]{1,0:T(8,128)(2,1)S(1)} %get-tuple-element.27), channel_id=1, source_target_pairs={{24,0},{16,8},{8,16},{0,24},{25,1},{17,9},{9,17},{1,25},{26,2},{18... | collective-permute-start | bytes 393224 | tf_op jit(solution)/shard_map/ppermute | solution.py:227
  26.2 0.0 collective-permute-done.6.refs_4_
  26.2 0.5 collective-permute-start.9
  26.7 0.0 collective-permute-done.7.refs_5_
  26.7 1.5 %collective-permute-start.10 = (bf16[128,512]{1,0:T(8,128)(2,1)S(1)}, bf16[128,512]{1,0:T(8,128)(2,1)S(1)}, u32[]{:S(2)}, u32[]{:S(2)}) collective-permute-start(bf16[128,512]{1,0:T(8,128)(2,1)S(1)} %collective-permute-done.7.refs_5_), channel_id=1, source_target_pairs={{16,0},{24,8},{0,16},{8,24},{17,1},{25,9},{1,17},{9,25},{18,2},{26... | collective-permute-start | bytes 393224 | tf_op jit(solution)/shard_map/ppermute | solution.py:227
  28.2 0.0 collective-permute-done.first_ref.refs_3_
  28.2 0.5 collective-permute-start.1
  28.7 1.8 %shard_map.96 = (f32[16,256]{1,0:T(8,128)S(1)}, f32[256,512]{1,0:T(8,128)S(1)}) custom-call(bf16[8,16,256]{2,1,0:T(8,128)(2,1)S(1)} %constant_dynamic-update-slice_fusion.md_ref, s32[3,1,256]{2,1,0:T(1,128)S(1)} %copy-done.2, bf16[768,512]{1,0:T(8,128)(2,1)S(1)} %get-tuple-element.13.hi_ref, bf16[768,512]{1,0:T(8,128)(2,1)S(1)} %get-tuple-element.14.lo_ref), custom_call_target="tpu_custom_call" | custom-call | flops 603979776 | bytes 2182144 | tf_op jit(solution)/shard_map/pallas_call | solution.py:27
  30.5 0.0 copy-start.6
  30.6 4.9 %collective-permute-done.1.second_ref.refs_7_ = bf16[144,512]{1,0:T(8,128)(2,1)S(1)} collective-permute-done((bf16[144,512]{1,0:T(8,128)(2,1)S(1)}, bf16[144,512]{1,0:T(8,128)(2,1)S(1)}, u32[]{:S(2)}, u32[]{:S(2)}) %collective-permute-start.1) | collective-permute-done | bytes 147488 | tf_op jit(solution)/shard_map/ppermute | solution.py:227
  35.4 0.0 collective-permute-start.17
  35.4 1.6 %shard_map.97 = (bf16[512,512]{1,0:T(8,128)(2,1)S(1)}, bf16[512,512]{1,0:T(8,128)(2,1)S(1)}, bf16[256,512]{1,0:T(8,128)(2,1)S(1)}, bf16[256,512]{1,0:T(8,128)(2,1)S(1)}, f32[512,512]{1,0:T(8,128)S(1)}) custom-call(s32[2,5]{1,0:T(2,128)S(1)} %copy-done.6, bf16[3,512]{1,0:T(4,128)(2,1)S(1)} %copy-done.1, ...), custom_call_target="tpu_custom_call" | custom-call | flops 536870912 | bytes 3460136 | tf_op jit(solution)/shard_map/pallas_call | solution.py:27
  37.1 0.0 collective-permute-done.8.refs_6_
  37.1 0.0 collective-permute-done.11.refs_10_
  37.1 0.0 collective-permute-done.9.refs_8_
  37.1 0.0 collective-permute-done.10.refs_9_
  37.1 0.7 %shard_map.99 = f32[256,512]{1,0:T(8,128)S(1)} custom-call(f32[256,512]{1,0:T(8,128)S(1)} %get-tuple-element.19.refs_0_, bf16[256,512]{1,0:T(8,128)(2,1)S(1)} %get-tuple-element.20.refs_1_, bf16[256,512]{1,0:T(8,128)(2,1)S(1)} %get-tuple-element.21.refs_2_, bf16[144,512]{1,0:T(8,128)(2,1)S(1)} %collective-permute-done.first_ref.refs_3_, ...), custom_call_target="tpu_custom_call" | custom-call | flops 268435456 | bytes 2654208 | tf_op jit(solution)/shard_map/pallas_call | solution.py:27
  37.8 0.6 collective-permute-start.12
  38.4 0.0 collective-permute-done.17
  38.4 0.1 add_convert_fusion
  38.5 3.6 %collective-permute-start.20 = (bf16[256,256]{1,0:T(8,128)(2,1)S(1)}, bf16[256,256]{1,0:T(8,128)(2,1)S(1)}, u32[]{:S(2)}, u32[]{:S(2)}) collective-permute-start(bf16[256,256]{1,0:T(8,128)(2,1)S(1)} %add_convert_fusion), channel_id=1, source_target_pairs={{6,0},{7,1},{4,2},{5,3},{2,4},{3,5},{0,6},{1,7},{14,8},{15,9},{12,... | collective-permute-start | bytes 393224 | tf_op jit(solution)/shard_map/ppermute | solution.py:227
  42.1 0.0 collective-permute-start.19
  42.1 0.8 %collective-permute-start.18 = (bf16[256,256]{1,0:T(8,128)(2,1)S(1)}, bf16[256,256]{1,0:T(8,128)(2,1)S(1)}, u32[]{:S(2)}, u32[]{:S(2)}) collective-permute-start(bf16[256,256]{1,0:T(8,128)(2,1)S(1)} %add_convert_fusion), channel_id=1, source_target_pairs={{2,0},{3,1},{0,2},{1,3},{6,4},{7,5},{4,6},{5,7},{10,8},{11,9},{8,1... | collective-permute-start | bytes 393224 | tf_op jit(solution)/shard_map/ppermute | solution.py:227
  42.9 0.0 collective-permute-done.12
  43.0 3.6 %collective-permute-start.15 = (bf16[256,256]{1,0:T(8,128)(2,1)S(1)}, bf16[256,256]{1,0:T(8,128)(2,1)S(1)}, u32[]{:S(2)}, u32[]{:S(2)}) collective-permute-start(bf16[256,256]{1,0:T(8,128)(2,1)S(1)} %add_convert_fusion.1), channel_id=1, source_target_pairs={{6,0},{7,1},{4,2},{5,3},{2,4},{3,5},{0,6},{1,7},{14,8},{15,9},{12,... | collective-permute-start | bytes 393224 | tf_op jit(solution)/shard_map/ppermute | solution.py:227
  46.6 0.0 collective-permute-start.14
  46.6 0.2 collective-permute-done.20
  46.8 1.6 %collective-permute-start.13 = (bf16[256,256]{1,0:T(8,128)(2,1)S(1)}, bf16[256,256]{1,0:T(8,128)(2,1)S(1)}, u32[]{:S(2)}, u32[]{:S(2)}) collective-permute-start(bf16[256,256]{1,0:T(8,128)(2,1)S(1)} %add_convert_fusion.1), channel_id=1, source_target_pairs={{2,0},{3,1},{0,2},{1,3},{6,4},{7,5},{4,6},{5,7},{10,8},{11,9},{8,1... | collective-permute-start | bytes 393224 | tf_op jit(solution)/shard_map/ppermute | solution.py:227
  48.3 7.8 %collective-permute-done.19 = bf16[256,256]{1,0:T(8,128)(2,1)S(1)} collective-permute-done((bf16[256,256]{1,0:T(8,128)(2,1)S(1)}, bf16[256,256]{1,0:T(8,128)(2,1)S(1)}, u32[]{:S(2)}, u32[]{:S(2)}) %collective-permute-start.19) | collective-permute-done | bytes 131104 | tf_op jit(solution)/shard_map/ppermute | solution.py:227
  56.2 0.0 collective-permute-done.18
  56.2 0.1 fusion.2
  56.3 0.2 collective-permute-start.21
  56.4 0.0 collective-permute-done.15
  56.4 6.2 %collective-permute-done.14 = bf16[256,256]{1,0:T(8,128)(2,1)S(1)} collective-permute-done((bf16[256,256]{1,0:T(8,128)(2,1)S(1)}, bf16[256,256]{1,0:T(8,128)(2,1)S(1)}, u32[]{:S(2)}, u32[]{:S(2)}) %collective-permute-start.14) | collective-permute-done | bytes 131104 | tf_op jit(solution)/shard_map/ppermute | solution.py:227
  62.7 0.0 collective-permute-done.13
  62.7 0.1 fusion.3
  62.8 0.2 collective-permute-start.16
  62.9 2.0 %shard_map.98 = bf16[512,512]{1,0:T(8,128)(2,1)} custom-call(f32[512,512]{1,0:T(8,128)S(1)} %get-tuple-element.16.refs_0_, bf16[512,512]{1,0:T(8,128)(2,1)S(1)} %get-tuple-element.17.refs_1_, bf16[512,512]{1,0:T(8,128)(2,1)S(1)} %get-tuple-element.18.refs_2_, bf16[144,512]{1,0:T(8,128)(2,1)S(1)} %collective-permute-done.first_ref.refs_3_, ...), custom_call_target="tpu_custom_call" | custom-call | flops 536870912 | bytes 3702784 | tf_op jit(solution)/shard_map/pallas_call | solution.py:27
  65.0 0.0 collective-permute-done.21
  65.0 0.8 %maximum_select_fusion.1 = f32[256,512]{1,0:T(8,128)} fusion(f32[256,256]{1,0:T(8,128)S(1)} %get-tuple-element.24, f32[256,256]{1,0:T(8,128)S(1)} %convert_element_type.73, pred[]{:T(512)S(6)} %eq.4), kind=kLoop, calls=%fused_computation.1 | loop fusion | flops 393216 | bytes 1048577 | tf_op jit(solution)/shard_map/jit(_where)/select_n | solution.py:245
  65.8 0.0 collective-permute-done.16
  65.9 0.8 %maximum_select_fusion = f32[256,512]{1,0:T(8,128)} fusion(f32[256,256]{1,0:T(8,128)S(1)} %get-tuple-element.26, f32[256,256]{1,0:T(8,128)S(1)} %convert_element_type.64, pred[]{:T(512)S(6)} %eq.4), kind=kLoop, calls=%fused_computation | loop fusion | flops 393216 | bytes 1048577 | tf_op jit(solution)/shard_map/jit(_where)/select_n | solution.py:245
  (18 shorter events, 0.2 us)
Async XLA Ops:
  0.6 4.1 %copy-start.1 = (bf16[3,512]{1,0:T(4,128)(2,1)S(1)}, bf16[3,512]{1,0:T(4,128)(2,1)}, u32[]{:S(2)}) copy-start(bf16[3,512]{1,0:T(4,128)(2,1)} %own_ref.1) | copy-start | bytes 9220
  0.6 4.2 %copy-start = (bf16[512,512]{1,0:T(8,128)(2,1)S(1)}, bf16[512,512]{1,0:T(8,128)(2,1)}, u32[]{:S(2)}) copy-start(bf16[512,512]{1,0:T(8,128)(2,1)} %matrix_ref.3) | copy-start | bytes 1572868
  0.7 4.1 %copy-start.3 = (s32[1,256]{1,0:T(1,128)S(1)}, s32[1,256]{1,0:T(1,128)}, u32[]{:S(2)}) copy-start(s32[1,256]{1,0:T(1,128)} %pivots_ref.1) | copy-start | bytes 3076
  0.7 4.1 %copy-start.2 = (s32[3,1,256]{2,1,0:T(1,128)S(1)}, s32[3,1,256]{2,1,0:T(1,128)}, u32[]{:S(2)}) copy-start(s32[3,1,256]{2,1,0:T(1,128)} %merges_ref.3) | copy-start | bytes 9220
  0.7 6.4 %copy-start.4 = (bf16[3,1,512,256]{3,2,1,0:T(8,128)(2,1)S(1)}, bf16[3,1,512,256]{3,2,1,0:T(8,128)(2,1)}, u32[]{:S(2)}) copy-start(bf16[3,1,512,256]{3,2,1,0:T(8,128)(2,1)} %merge_ref.1) | copy-start | bytes 2359300
  1.7 26.5 %collective-permute-start = (bf16[144,512]{1,0:T(8,128)(2,1)S(1)}, bf16[144,512]{1,0:T(8,128)(2,1)S(1)}, u32[]{:S(2)}, u32[]{:S(2)}) collective-permute-start(bf16[144,512]{1,0:T(8,128)(2,1)S(1)} %fusion.1), channel_id=1, source_target_pairs={{8,0},{0,8},{24,16},{16,24},{9,1},{1,9},{25,17},{17,25},{10,2},{2,... | collective-permute-start | bytes 442376 | tf_op jit(solution)/shard_map/ppermute | solution.py:227
  4.9 4.4 %collective-permute-start.2 = (bf16[16,256]{1,0:T(8,128)(2,1)S(1)}, bf16[16,256]{1,0:T(8,128)(2,1)S(1)}, u32[]{:S(2)}, u32[]{:S(2)}) collective-permute-start(bf16[16,256]{1,0:T(8,128)(2,1)S(1)} %shard_map.94), channel_id=1, source_target_pairs={{1,0},{0,1},{3,2},{2,3},{5,4},{4,5},{7,6},{6,7},{9,8},{8,9},{11,10... | collective-permute-start | bytes 24584 | tf_op jit(solution)/shard_map/ppermute | solution.py:227
  4.9 21.2 %collective-permute-start.6 = (bf16[128,512]{1,0:T(8,128)(2,1)S(1)}, bf16[128,512]{1,0:T(8,128)(2,1)S(1)}, u32[]{:S(2)}, u32[]{:S(2)}) collective-permute-start(bf16[128,512]{1,0:T(8,128)(2,1)S(1)} %get-tuple-element.28), channel_id=1, source_target_pairs={{8,0},{0,8},{24,16},{16,24},{9,1},{1,9},{25,17},{17,25},{10,2},{2,... | collective-permute-start | bytes 393224 | tf_op jit(solution)/shard_map/ppermute | solution.py:227
  5.0 21.7 %collective-permute-start.7 = (bf16[128,512]{1,0:T(8,128)(2,1)S(1)}, bf16[128,512]{1,0:T(8,128)(2,1)S(1)}, u32[]{:S(2)}, u32[]{:S(2)}) collective-permute-start(bf16[128,512]{1,0:T(8,128)(2,1)S(1)} %get-tuple-element.29), channel_id=1, source_target_pairs={{8,0},{0,8},{24,16},{16,24},{9,1},{1,9},{25,17},{17,25},{10,2},{2,... | collective-permute-start | bytes 393224 | tf_op jit(solution)/shard_map/ppermute | solution.py:227
  7.0 30.0 %collective-permute-start.8 = (bf16[128,512]{1,0:T(8,128)(2,1)S(1)}, bf16[128,512]{1,0:T(8,128)(2,1)S(1)}, u32[]{:S(2)}, u32[]{:S(2)}) collective-permute-start(bf16[128,512]{1,0:T(8,128)(2,1)S(1)} %get-tuple-element.27), channel_id=1, source_target_pairs={{8,0},{0,8},{24,16},{16,24},{9,1},{1,9},{25,17},{17,25},{10,2},{2,... | collective-permute-start | bytes 393224 | tf_op jit(solution)/shard_map/ppermute | solution.py:227
  7.1 1.0 %copy-start.5 = (bf16[512,256]{1,0:T(8,128)(2,1)S(1)}, bf16[512,256]{1,0:T(8,128)(2,1)}, u32[]{:S(2)}) copy-start(bf16[512,256]{1,0:T(8,128)(2,1)} %proj_ref.1) | copy-start | bytes 786436
  9.3 3.8 %collective-permute-start.3 = (bf16[2,16,256]{2,1,0:T(8,128)(2,1)S(1)}, bf16[2,16,256]{2,1,0:T(8,128)(2,1)S(1)}, u32[]{:S(2)}, u32[]{:S(2)}) collective-permute-start(bf16[2,16,256]{2,1,0:T(8,128)(2,1)S(1)} %pad_maximum_fusion), channel_id=1, source_target_pairs={{2,0},{3,1},{0,2},{1,3},{6,4},{7,5},{4,6},{5,7},{10,8},{11,9},{8,1... | collective-permute-start | bytes 49160 | tf_op jit(solution)/shard_map/ppermute | solution.py:227
  13.1 4.7 %collective-permute-start.4 = (bf16[2,16,256]{2,1,0:T(8,128)(2,1)S(1)}, bf16[2,16,256]{2,1,0:T(8,128)(2,1)S(1)}, u32[]{:S(2)}, u32[]{:S(2)}) collective-permute-start(bf16[2,16,256]{2,1,0:T(8,128)(2,1)S(1)} %pad_maximum_fusion), channel_id=1, source_target_pairs={{4,0},{5,1},{6,2},{7,3},{0,4},{1,5},{2,6},{3,7},{12,8},{13,9},{14,... | collective-permute-start | bytes 49160 | tf_op jit(solution)/shard_map/ppermute | solution.py:227
  17.9 5.7 %collective-permute-start.5 = (bf16[2,16,256]{2,1,0:T(8,128)(2,1)S(1)}, bf16[2,16,256]{2,1,0:T(8,128)(2,1)S(1)}, u32[]{:S(2)}, u32[]{:S(2)}) collective-permute-start(bf16[2,16,256]{2,1,0:T(8,128)(2,1)S(1)} %pad_maximum_fusion), channel_id=1, source_target_pairs={{6,0},{7,1},{4,2},{5,3},{2,4},{3,5},{0,6},{1,7},{14,8},{15,9},{12,... | collective-permute-start | bytes 49160 | tf_op jit(solution)/shard_map/ppermute | solution.py:227
  23.6 13.5 %collective-permute-start.11 = (bf16[128,512]{1,0:T(8,128)(2,1)S(1)}, bf16[128,512]{1,0:T(8,128)(2,1)S(1)}, u32[]{:S(2)}, u32[]{:S(2)}) collective-permute-start(bf16[128,512]{1,0:T(8,128)(2,1)S(1)} %get-tuple-element.27), channel_id=1, source_target_pairs={{24,0},{16,8},{8,16},{0,24},{25,1},{17,9},{9,17},{1,25},{26,2},{18... | collective-permute-start | bytes 393224 | tf_op jit(solution)/shard_map/ppermute | solution.py:227
  26.2 10.9 %collective-permute-start.9 = (bf16[128,512]{1,0:T(8,128)(2,1)S(1)}, bf16[128,512]{1,0:T(8,128)(2,1)S(1)}, u32[]{:S(2)}, u32[]{:S(2)}) collective-permute-start(bf16[128,512]{1,0:T(8,128)(2,1)S(1)} %collective-permute-done.6.refs_4_), channel_id=1, source_target_pairs={{16,0},{24,8},{0,16},{8,24},{17,1},{25,9},{1,17},{9,25},{18,2},{26... | collective-permute-start | bytes 393224 | tf_op jit(solution)/shard_map/ppermute | solution.py:227
  26.7 10.4 %collective-permute-start.10 = (bf16[128,512]{1,0:T(8,128)(2,1)S(1)}, bf16[128,512]{1,0:T(8,128)(2,1)S(1)}, u32[]{:S(2)}, u32[]{:S(2)}) collective-permute-start(bf16[128,512]{1,0:T(8,128)(2,1)S(1)} %collective-permute-done.7.refs_5_), channel_id=1, source_target_pairs={{16,0},{24,8},{0,16},{8,24},{17,1},{25,9},{1,17},{9,25},{18,2},{26... | collective-permute-start | bytes 393224 | tf_op jit(solution)/shard_map/ppermute | solution.py:227
  28.2 7.2 %collective-permute-start.1 = (bf16[144,512]{1,0:T(8,128)(2,1)S(1)}, bf16[144,512]{1,0:T(8,128)(2,1)S(1)}, u32[]{:S(2)}, u32[]{:S(2)}) collective-permute-start(bf16[144,512]{1,0:T(8,128)(2,1)S(1)} %collective-permute-done.first_ref.refs_3_), channel_id=1, source_target_pairs={{16,0},{24,8},{0,16},{8,24},{17,1},{25,9},{1,17},{9,25},{18,2},{26... | collective-permute-start | bytes 442376 | tf_op jit(solution)/shard_map/ppermute | solution.py:227
  30.5 4.9 %copy-start.6 = (s32[2,5]{1,0:T(2,128)S(1)}, s32[2,5]{1,0:T(2,128)}, u32[]{:S(2)}) copy-start(s32[2,5]{1,0:T(2,128)} %lists_ref.1) | copy-start | bytes 124
  35.4 3.0 %collective-permute-start.17 = (bf16[256,256]{1,0:T(8,128)(2,1)S(1)}, bf16[256,256]{1,0:T(8,128)(2,1)S(1)}, u32[]{:S(2)}, u32[]{:S(2)}) collective-permute-start(bf16[256,256]{1,0:T(8,128)(2,1)S(1)} %select_convert_fusion), channel_id=1, source_target_pairs={{1,0},{0,1},{3,2},{2,3},{5,4},{4,5},{7,6},{6,7},{9,8},{8,9},{11,10... | collective-permute-start | bytes 393224 | tf_op jit(solution)/shard_map/ppermute | solution.py:227
  37.8 5.1 %collective-permute-start.12 = (bf16[256,256]{1,0:T(8,128)(2,1)S(1)}, bf16[256,256]{1,0:T(8,128)(2,1)S(1)}, u32[]{:S(2)}, u32[]{:S(2)}) collective-permute-start(bf16[256,256]{1,0:T(8,128)(2,1)S(1)} %select_convert_fusion.1), channel_id=1, source_target_pairs={{1,0},{0,1},{3,2},{2,3},{5,4},{4,5},{7,6},{6,7},{9,8},{8,9},{11,10... | collective-permute-start | bytes 393224 | tf_op jit(solution)/shard_map/ppermute | solution.py:227
  38.5 8.3 %collective-permute-start.20 = (bf16[256,256]{1,0:T(8,128)(2,1)S(1)}, bf16[256,256]{1,0:T(8,128)(2,1)S(1)}, u32[]{:S(2)}, u32[]{:S(2)}) collective-permute-start(bf16[256,256]{1,0:T(8,128)(2,1)S(1)} %add_convert_fusion), channel_id=1, source_target_pairs={{6,0},{7,1},{4,2},{5,3},{2,4},{3,5},{0,6},{1,7},{14,8},{15,9},{12,... | collective-permute-start | bytes 393224 | tf_op jit(solution)/shard_map/ppermute | solution.py:227
  42.1 14.1 %collective-permute-start.19 = (bf16[256,256]{1,0:T(8,128)(2,1)S(1)}, bf16[256,256]{1,0:T(8,128)(2,1)S(1)}, u32[]{:S(2)}, u32[]{:S(2)}) collective-permute-start(bf16[256,256]{1,0:T(8,128)(2,1)S(1)} %add_convert_fusion), channel_id=1, source_target_pairs={{4,0},{5,1},{6,2},{7,3},{0,4},{1,5},{2,6},{3,7},{12,8},{13,9},{14,... | collective-permute-start | bytes 393224 | tf_op jit(solution)/shard_map/ppermute | solution.py:227
  42.1 14.1 %collective-permute-start.18 = (bf16[256,256]{1,0:T(8,128)(2,1)S(1)}, bf16[256,256]{1,0:T(8,128)(2,1)S(1)}, u32[]{:S(2)}, u32[]{:S(2)}) collective-permute-start(bf16[256,256]{1,0:T(8,128)(2,1)S(1)} %add_convert_fusion), channel_id=1, source_target_pairs={{2,0},{3,1},{0,2},{1,3},{6,4},{7,5},{4,6},{5,7},{10,8},{11,9},{8,1... | collective-permute-start | bytes 393224 | tf_op jit(solution)/shard_map/ppermute | solution.py:227
  43.0 13.5 %collective-permute-start.15 = (bf16[256,256]{1,0:T(8,128)(2,1)S(1)}, bf16[256,256]{1,0:T(8,128)(2,1)S(1)}, u32[]{:S(2)}, u32[]{:S(2)}) collective-permute-start(bf16[256,256]{1,0:T(8,128)(2,1)S(1)} %add_convert_fusion.1), channel_id=1, source_target_pairs={{6,0},{7,1},{4,2},{5,3},{2,4},{3,5},{0,6},{1,7},{14,8},{15,9},{12,... | collective-permute-start | bytes 393224 | tf_op jit(solution)/shard_map/ppermute | solution.py:227
  46.6 16.1 %collective-permute-start.14 = (bf16[256,256]{1,0:T(8,128)(2,1)S(1)}, bf16[256,256]{1,0:T(8,128)(2,1)S(1)}, u32[]{:S(2)}, u32[]{:S(2)}) collective-permute-start(bf16[256,256]{1,0:T(8,128)(2,1)S(1)} %add_convert_fusion.1), channel_id=1, source_target_pairs={{4,0},{5,1},{6,2},{7,3},{0,4},{1,5},{2,6},{3,7},{12,8},{13,9},{14,... | collective-permute-start | bytes 393224 | tf_op jit(solution)/shard_map/ppermute | solution.py:227
  46.8 15.9 %collective-permute-start.13 = (bf16[256,256]{1,0:T(8,128)(2,1)S(1)}, bf16[256,256]{1,0:T(8,128)(2,1)S(1)}, u32[]{:S(2)}, u32[]{:S(2)}) collective-permute-start(bf16[256,256]{1,0:T(8,128)(2,1)S(1)} %add_convert_fusion.1), channel_id=1, source_target_pairs={{2,0},{3,1},{0,2},{1,3},{6,4},{7,5},{4,6},{5,7},{10,8},{11,9},{8,1... | collective-permute-start | bytes 393224 | tf_op jit(solution)/shard_map/ppermute | solution.py:227
  56.3 8.7 %collective-permute-start.21 = (bf16[256,256]{1,0:T(8,128)(2,1)S(1)}, bf16[256,256]{1,0:T(8,128)(2,1)S(1)}, u32[]{:S(2)}, u32[]{:S(2)}) collective-permute-start(bf16[256,256]{1,0:T(8,128)(2,1)S(1)} %get-tuple-element.23), channel_id=1, source_target_pairs={{1,0},{0,1},{3,2},{2,3},{5,4},{4,5},{7,6},{6,7},{9,8},{8,9},{11,10... | collective-permute-start | bytes 393224 | tf_op jit(solution)/shard_map/ppermute | solution.py:227
  62.8 3.1 %collective-permute-start.16 = (bf16[256,256]{1,0:T(8,128)(2,1)S(1)}, bf16[256,256]{1,0:T(8,128)(2,1)S(1)}, u32[]{:S(2)}, u32[]{:S(2)}) collective-permute-start(bf16[256,256]{1,0:T(8,128)(2,1)S(1)} %get-tuple-element.25), channel_id=1, source_target_pairs={{1,0},{0,1},{3,2},{2,3},{5,4},{4,5},{7,6},{6,7},{9,8},{8,9},{11,10... | collective-permute-start | bytes 393224 | tf_op jit(solution)/shard_map/ppermute | solution.py:227

commit v2 on v1

v2 whole, which is shorter than its diff:
```python
import functools
import math

import jax
import jax.numpy as jnp
from jax import lax
from jax.experimental import pallas as pl
from jax.experimental.pallas import tpu as pltpu
from jax.sharding import PartitionSpec as P

SPREAD = 25.0
EXPONENT = -SPREAD * math.log2(math.e)
FAR_OFF = 1024.0
HEIGHT = 16
ROW_HI, ROW_LO, MEET, PIVOT = 3, 4, 5, 6
BF16, F32 = jnp.bfloat16, jnp.float32


def call(body, outs, flops, *args):
    specs = [
        pl.BlockSpec(memory_space=pltpu.SMEM if a.dtype == jnp.int32 and a.ndim == 2 and a.shape[1] < 128 else pltpu.VMEM)
        for a in args
    ]
    moved = sum(a.size * a.dtype.itemsize for a in args) + sum(
        math.prod(s) * jnp.dtype(d).itemsize for s, d in outs
    )
    return pl.pallas_call(
        body,
        out_shape=[jax.ShapeDtypeStruct(s, d) for s, d in outs],
        in_specs=specs,
        out_specs=[pl.BlockSpec(memory_space=pltpu.VMEM)] * len(outs),
        compiler_params=pltpu.CompilerParams(vmem_limit_bytes=40 << 20),
        cost_estimate=pl.CostEstimate(flops=flops, bytes_accessed=moved, transcendentals=0),
    )(*args)


def dot(a, b, over_a=1, over_b=0):
    return lax.dot_general(a, b, (((over_a,), (over_b,)), ((), ())), preferred_element_type=F32)


def halves(x):
    hi = x.astype(BF16)
    return hi, (x - hi.astype(F32)).astype(BF16)


def rows_of(entries, width):
    row = lax.broadcasted_iota(jnp.int32, (HEIGHT, width), 0)
    out = jnp.zeros((HEIGHT, width), F32)
    for k, entry in enumerate(entries):
        out = jnp.where(row == k, entry, out)
    return out


def norm_parts(p):
    n = p[0:1] * p[0:1] + p[1:2] * p[1:2] + p[2:3] * p[2:3]
    hi = n.astype(BF16).astype(F32)
    mid = (n - hi).astype(BF16).astype(F32)
    return [hi, mid, n - hi - mid]


def left_features(p, penalties):
    entries = [p[0:1], p[1:2], p[2:3], *norm_parts(p), 1.0, 1.0, 1.0, *penalties]
    return rows_of(entries, p.shape[1]).astype(BF16)


def right_features(p, marks):
    entries = [-2.0 * p[0:1], -2.0 * p[1:2], -2.0 * p[2:3], 1.0, 1.0, 1.0, *norm_parts(p), *marks]
    return rows_of(entries, p.shape[1]).astype(BF16)


def gauss(left, right, amp):
    return jnp.exp2(EXPONENT * dot(left, right, 0, 0)) * amp


def lane_index(width):
    return lax.broadcasted_iota(jnp.int32, (1, width), 1)


def chosen(attributes, index):
    spot = lax.broadcasted_iota(jnp.int32, (attributes.shape[1], index.shape[1]), 0)
    one_hot = jnp.where(spot == index, 1.0, 0.0).astype(BF16)
    return dot(attributes.astype(BF16), one_hot)


def bit_of(value, place):
    return (value >> place) & 1


def bit_of(value, place):
    return (value >> place) & 1


def describe_body(points_ref, pivots_ref, merges_ref, proj_ref, matrix_ref, merge_ref, *outs):
    given_ref, kept_ref, hi_ref, lo_ref = outs
    p = points_ref[...].astype(F32)
    width = p.shape[1]
    rank = pivots_ref.shape[1]
    levels = merge_ref.shape[0]
    position = lax.axis_index("leaf")
    spot = lane_index(width)
    attributes = rows_of(
        [p[0:1], p[1:2], p[2:3], (spot // rank).astype(F32), (spot % rank).astype(F32)], width
    )
    skeleton = chosen(attributes, pivots_ref[...])
    row = lax.broadcasted_iota(jnp.int32, skeleton.shape, 0)
    for level in range(levels - 1):
        q = merges_ref[level]
        skeleton = jnp.where(row == PIVOT + 2 * level, (q // rank).astype(F32), skeleton)
        skeleton = jnp.where(row == PIVOT + 2 * level + 1, (q % rank).astype(F32), skeleton)
    given_ref[0:HEIGHT, :] = skeleton.astype(BF16)
    c = dot(proj_ref[...], matrix_ref[...], 0, 0)
    for level in range(levels):
        hi, lo = halves(c)
        hi_ref[pl.ds(level * rank, rank), :] = hi
        lo_ref[pl.ds(level * rank, rank), :] = lo
        start = pl.multiple_of(bit_of(position, level) * rank, rank)
        m = merge_ref[level, 0, pl.ds(start, rank), :]
        c = dot(m, hi, 0, 0) + dot(m, lo, 0, 0)
    second = bit_of(position, 0) == 1
    middle = c.shape[1] // 2
    low, high = c[:, :middle], c[:, middle:]
    kept_ref[...] = jnp.where(second, high, low)
    given_ref[HEIGHT:, :] = jnp.where(second, low, high).astype(BF16)


def scatter_body(kept_ref, sent_ref, got_ref, mine_ref, *message_refs):
    chip = (lax.axis_index("leaf") >> 1) % (len(message_refs) + 1)
    count = mine_ref.shape[0]
    for k, ref in enumerate((mine_ref, *message_refs)):
        start = pl.multiple_of((chip ^ k) * count, count)
        other = got_ref[pl.ds(pl.multiple_of(HEIGHT + start, HEIGHT), count), :]
        piece = kept_ref[pl.ds(start, count), :] + other.astype(F32)
        if k == 0:
            ref[...] = piece
        else:
            ref[0:HEIGHT, :] = sent_ref[0:HEIGHT, :]
            ref[HEIGHT : 2 * HEIGHT, :] = got_ref[0:HEIGHT, :]
            ref[2 * HEIGHT :, :] = piece.astype(BF16)


def tree_body(far_amp, near_amp, even_ahead, lists_ref, *refs):
    *messages, sent_ref, got_ref, mine_ref, merges_ref, hi_ref, lo_ref, first_ref, second_ref = refs[:-4]
    top_first, top_second, part_ref, piece_ref = refs[-4:]
    piece = mine_ref[...]
    for ref in messages:
        piece += ref[2 * HEIGHT :, :].astype(F32)
    piece_ref[...] = piece.astype(BF16)
    position = lax.axis_index("leaf")
    levels = merges_ref.shape[0]
    rank = merges_ref.shape[2]
    nodes = [sent_ref[0:HEIGHT, :].astype(F32), got_ref[0:HEIGHT, :].astype(F32)]
    for ref in messages:
        nodes += [ref[0:HEIGHT, :].astype(F32), ref[HEIGHT : 2 * HEIGHT, :].astype(F32)]
    pivots = nodes
    row = lax.broadcasted_iota(jnp.int32, (HEIGHT, rank), 0)
    path = []
    for level in range(levels):
        path.append(nodes[0])
        flip = bit_of(position, level)
        merged = []
        for j in range(len(nodes) // 2):
            if level < levels - 1:
                source = pivots[j << level + 1]
                k = PIVOT + 2 * level
                q = (source[k : k + 1] * rank + source[k + 1 : k + 2]).astype(jnp.int32)
            else:
                q = merges_ref[level]
            q = jnp.where(flip == 1, jnp.where(q < rank, q + rank, q - rank), q)
            far = jnp.where(row == MEET, float(level + 1), nodes[2 * j + 1])
            merged.append(chosen(jnp.concatenate([nodes[2 * j], far], axis=1), q))
        nodes = merged
    top = nodes[0]
    blocks = lists_ref.shape[0]
    width = first_ref.shape[1]
    marks = block_marks(width, blocks)
    top_block = top[ROW_HI : ROW_HI + 1].astype(jnp.int32)
    top_here = top[MEET : MEET + 1] == 0.0
    for ref, base, near_ref in zip((first_ref, second_ref), bases_of(even_ahead, blocks), (top_first, top_second)):
        table = penalty_table(lists_ref, base, blocks)
        penalties = [
            jnp.where(top_here, per_block(top_block, [table[i][k] for i in range(blocks)]), FAR_OFF)
            for k in range(blocks)
        ]
        columns = right_features(ref[0:3, :].astype(F32), marks)
        near_ref[...] = gauss(left_features(top, penalties), columns, near_amp).astype(BF16)
    total = jnp.zeros(part_ref.shape, F32)
    for level in range(levels):
        penalty = jnp.where(top[MEET : MEET + 1] == float(level + 1), 0.0, FAR_OFF)
        block = gauss(left_features(top, [penalty]), right_features(path[level], [1.0]), -far_amp)
        block_hi, block_lo = halves(block)
        hi = hi_ref[pl.ds(level * rank, rank), :]
        lo = lo_ref[pl.ds(level * rank, rank), :]
        total += dot(block_hi, hi) + dot(block_hi, lo) + dot(block_lo, hi)
    part_ref[...] = total


def penalty_table(lists_ref, base, blocks):
    table = []
    for i in range(blocks):
        line = []
        for k in range(blocks):
            listed = lists_ref[i, 0] == base + k
            for slot in range(1, lists_ref.shape[1]):
                listed |= lists_ref[i, slot] == base + k
            line.append(jnp.where(listed, 0.0, FAR_OFF))
        table.append(line)
    return table


def per_block(block_index, values):
    out = jnp.zeros(block_index.shape, F32)
    for i, value in enumerate(values):
        out = jnp.where(block_index == i, value, out)
    return out


def block_marks(width, blocks):
    spot = lane_index(width) // (width // blocks)
    return [jnp.where(spot == k, 1.0, 0.0) for k in range(blocks)]


def bases_of(even_ahead, blocks):
    if not even_ahead:
        return [0, 2 * blocks]
    odd = lax.axis_index("blk") % 2
    return [2 * blocks * (1 - odd), 2 * blocks * odd]


def near_body(near_amp, even_ahead, lists_ref, own_ref, first_ref, second_ref, matrix_ref, *outs):
    near_first, near_second, own_terms = outs
    blocks = lists_ref.shape[0]
    own = own_ref[...].astype(F32)
    width = own.shape[1]
    spot = lane_index(width) // (width // blocks)
    marks = block_marks(width, blocks)

    def near(base, columns):
        table = penalty_table(lists_ref, base, blocks)
        penalties = [per_block(spot, [table[i][k] for i in range(blocks)]) for k in range(blocks)]
        return gauss(left_features(own, penalties), right_features(columns, marks), near_amp).astype(BF16)

    bases = bases_of(even_ahead, blocks)
    near_first[...] = near(bases[0], first_ref[0:3, :].astype(F32))
    near_second[...] = near(bases[1], second_ref[0:3, :].astype(F32))
    own_terms[...] = dot(near(blocks, own), matrix_ref[...])


def near_product(start_ref, first_ref, second_ref, *chunks):
    total = start_ref[...]
    per_side = len(chunks) // 2
    for side, left_ref in enumerate((first_ref, second_ref)):
        at = 0
        for k, chunk_ref in enumerate(chunks[side * per_side : (side + 1) * per_side]):
            lead = 0 if k else HEIGHT
            count = chunk_ref.shape[0] - lead
            total += dot(left_ref[:, at : at + count], chunk_ref[lead:, :])
            at += count
    return total


def sample_body(*refs):
    refs[-1][...] = near_product(*refs[:-1]).astype(BF16)


def share_body(*refs):
    *ins, kept_ref, given_ref = refs
    total = near_product(*ins)
    second = bit_of(lax.axis_index("leaf"), 0) == 1
    middle = total.shape[1] // 2
    low, high = total[:, :middle], total[:, middle:]
    kept_ref[...] = jnp.where(second, high, low)
    given_ref[...] = jnp.where(second, low, high).astype(BF16)


def pair_body(kept_ref, got_ref, piece_ref, out_ref):
    rank = kept_ref.shape[0]
    out_ref[0:rank, :] = (kept_ref[...] + got_ref[...].astype(F32)).astype(BF16)
    out_ref[rank:, :] = piece_ref[...]


def total_body(*refs):
    *messages, out_ref = refs
    rank = out_ref.shape[0] // 2
    count = rank // len(messages)
    chip = (lax.axis_index("leaf") >> 1) % len(messages)
    total = messages[0][0:rank, :].astype(F32)
    for ref in messages[1:]:
        total += ref[0:rank, :].astype(F32)
    out_ref[0:rank, :] = total.astype(BF16)
    for k, ref in enumerate(messages):
        start = pl.multiple_of(rank + (chip ^ k) * count, count)
        out_ref[pl.ds(start, count), :] = ref[rank:, :]


def join_body(own_ref, other_ref, samples_ref, omega_ref):
    second = bit_of(lax.axis_index("leaf"), 0) == 1
    rank, middle = samples_ref.shape[0], own_ref.shape[1]
    own, other = own_ref[...].astype(F32), other_ref[...].astype(F32)
    low, high = jnp.where(second, other, own), jnp.where(second, own, other)
    for ref, at in ((samples_ref, 0), (omega_ref, rank)):
        ref[:, :middle] = low[at : at + rank]
        ref[:, middle:] = high[at : at + rank]


def permuted(block, axis, route):
    return lax.ppermute(block, axis, [(route(i), i) for i in range(lax.axis_size(axis))])


def swapped(block, distance):
    return permuted(block, "leaf", lambda i: i ^ distance)


def on_device(points, test_matrix, near_lists, leaf_pivots, leaf_proj, merge_pivots, merge_proj):
    row_count, sample_count = test_matrix.shape
    block_count, slot_count = near_lists.shape
    skel_rank = leaf_pivots.shape[1]
    level_count = merge_pivots.shape[0]
    near_amp = 9.0 / math.sqrt(slot_count * (row_count // block_count))
    far_amp = 3.0 / math.sqrt(skel_rank)
    square = 2 * skel_rank * skel_rank * sample_count

    middle = sample_count // 2
    chips = 1 << level_count - 1
    piece = skel_rank // chips

    count = lax.axis_size("blk")
    paired = count % 2 == 0 and count > 2
    if paired:
        step = lambda i, by: (i + (by if i % 2 == 0 else -by)) % count
        routes = [lambda i: step(i, 1), lambda i: step(i, -1), lambda i: step(i, -2)]
    else:
        routes = [lambda i: (i - 1) % count, lambda i: (i + 1) % count]
    header = jnp.pad(points, ((0, HEIGHT - points.shape[0]), (0, 0)))
    chunks = [
        jnp.concatenate([header, test_matrix[: row_count // 2]], axis=0),
        test_matrix[row_count // 2 :],
    ]
    first = [permuted(c, "blk", routes[0]) for c in chunks]
    onward = list(first if paired else chunks)

    given, kept, hi, lo = call(
        describe_body,
        [((HEIGHT + skel_rank, middle), BF16), ((skel_rank, middle), F32)]
        + [((level_count * skel_rank, sample_count), BF16)] * 2,
        8 * square,
        points,
        leaf_pivots,
        merge_pivots,
        leaf_proj,
        test_matrix,
        merge_proj,
    )
    got = swapped(given, 1)
    mine, *messages = call(
        scatter_body,
        [((piece, middle), F32)] + [((2 * HEIGHT + piece, middle), BF16)] * (chips - 1),
        0,
        kept,
        given,
        got,
    )
    messages = [swapped(m, 2 * k + 2) for k, m in enumerate(messages)]
    onward[0], messages[0] = lax.optimization_barrier((onward[0], messages[0]))
    second = [permuted(onward[0], "blk", routes[-1])]
    first_points, second_points = first[0], second[0]
    near_first, near_second, own_terms = call(
        functools.partial(near_body, near_amp, paired),
        [((row_count, row_count), BF16)] * 2 + [((row_count, sample_count), F32)],
        6 * square,
        near_lists,
        points,
        first_points,
        second_points,
        test_matrix,
    )
    onward[1], messages = lax.optimization_barrier((onward[1], messages))
    second.append(permuted(onward[1], "blk", routes[-1]))
    top_first, top_second, far_part, omega_piece = call(
        functools.partial(tree_body, far_amp, near_amp, paired),
        [((skel_rank, row_count), BF16)] * 2
        + [((skel_rank, sample_count), F32), ((piece, middle), BF16)],
        9 * square,
        near_lists,
        *messages,
        given,
        got,
        mine,
        merge_pivots,
        hi,
        lo,
        first_points,
        second_points,
    )
    kept, given = call(
        share_body,
        [((skel_rank, middle), F32), ((skel_rank, middle), BF16)],
        4 * square,
        far_part,
        top_first,
        top_second,
        *first,
        *second,
    )
    got = swapped(given, 1)
    (message,) = call(pair_body, [((skel_rank + piece, middle), BF16)], 0, kept, got, omega_piece)
    messages = [message] + [swapped(message, 2 * k) for k in range(1, chips)]
    (sample,) = call(
        sample_body,
        [((row_count, sample_count), BF16)],
        8 * square,
        own_terms,
        near_first,
        near_second,
        *first,
        *second,
    )
    (total,) = call(total_body, [((2 * skel_rank, middle), BF16)], 0, *messages)
    total, sample = lax.optimization_barrier((total, sample))
    other = swapped(total, 1)
    top_samples, top_omega = call(
        join_body, [((skel_rank, sample_count), F32)] * 2, 0, total, other
    )
    return (sample, top_samples, top_omega)


def solution(mesh):
    placed = (
        P(None, ("blk", "leaf")),
        P(("blk", "leaf"), None),
        P(("blk", "leaf"), None),
        P(("blk", "leaf"), None),
        P(("blk", "leaf"), None),
        P(None, ("blk", "leaf"), None),
        P(None, ("blk", "leaf"), None, None),
    )
    return jax.shard_map(
        on_device,
        mesh=mesh,
        in_specs=placed,
        out_specs=(P(("blk", "leaf"), None), P(("blk", "leaf"), None), P(("blk", "leaf"), None)),
        check_vma=False,
    )
```

time: 66.9 us -> 49.8 us (0.74)
  starting transfers between devices: 30 us -> 16.4 us
  other arithmetic: 3.03 us -> 0.02 us
  waiting for transfers between devices: 24.3 us -> 21.8 us
  Pallas kernels: 7.44 us -> 8.29 us
  local copies, waits for them, and re-layouts: 1.02 us -> 1.86 us
    ppermute x22 -> x13, starting transfers between devices: 30 us -> 16.4 us  [permuted(): lax.ppermute(block, axis, [(route(i), i) for i in range(lax.axis_size(axi...]
    ppermute x22 -> x13, waiting for transfers between devices: 24.3 us -> 21.8 us  [permuted(): lax.ppermute(block, axis, [(route(i), i) for i in range(lax.axis_size(axi...]
    select_n x2 -> x0, other arithmetic: 1.68 us -> none  [group_sum(): jnp.where(second, jnp.concatenate([other, total], axis=1), jnp.concatenat...]
    slice x1, local copies, waits for them, and re-layouts: 0.03 us -> 1.15 us  [on_device(): test_matrix[:row_count // 2]]
    concatenate x1, other arithmetic: 1.02 us -> 0.02 us  [on_device(): jnp.concatenate([header, test_matrix[:row_count // 2]], axis=0)]
    pallas_call x6 -> x9, Pallas kernels: 7.44 us -> 8.29 us  [call(): pl.pallas_call(body, out_shape=[jax.ShapeDtypeStruct(s, d) for s, d in ou...]
  transfers between devices with their start and end apart: 22 -> 13, of which waited for: 7 -> 10; matrix products, arithmetic and copies ran while one was open for 2% -> 0% of each run, Pallas kernels for 11% -> 14%
where the time goes in v2:
time: 49.8 us; the launch traced here: 49.1 us
  waiting for transfers between devices  21.8 us (44%)
  starting transfers between devices  16.4 us (33%)
  Pallas kernels  8.29 us (17%)
  local copies, waits for them, and re-layouts  1.86 us (4%)
  between operations  0.79 us (2%)
    ppermute x13, waiting for transfers between devices, permuted(): lax.ppermute(block, axis, [(route(i), i) for i in range(lax.axis_size(axi...  21.8 us
    ppermute x13, starting transfers between devices, permuted(): lax.ppermute(block, axis, [(route(i), i) for i in range(lax.axis_size(axi...  16.4 us
    pallas_call x9, Pallas kernels, call(): pl.pallas_call(body, out_shape=[jax.ShapeDtypeStruct(s, d) for s, d in ou...  8.29 us
    slice x1, local copies, waits for them, and re-layouts, on_device(): test_matrix[:row_count // 2]  1.15 us
  transfers between devices with their start and end apart: 13, of which 10 were waited for; matrix products, arithmetic and copies ran while one was open for 0% of the time, Pallas kernels for 14%

profile of v2, /device:TPU:0, one launch (start us, length us, event | category | flops | bytes accessed | tf_op | source)
XLA Modules:
  0.0 49.1 jit_solution(7043451044542102384)
XLA Ops:
  0.6 0.0 copy-start.4
  0.6 0.0 copy-start.1
  0.7 0.0 copy-start.5
  0.7 1.1 %fusion.2 = (bf16[256,512]{1,0:T(8,128)(2,1)S(1)}, bf16[256,512]{1,0:T(8,128)(2,1)S(1)}) fusion(bf16[512,512]{1,0:T(8,128)(2,1)} %matrix_ref.3), kind=kLoop, calls=%fused_computation.3 | loop fusion | bytes 1048576 | tf_op jit(solution)/shard_map/slice | solution.py:335
  1.8 0.0 copy-start
  1.8 0.0 copy-done.1
  1.8 0.0 copy-start.2
  1.9 0.0 copy-start.6
  1.9 3.0 %collective-permute-start.1 = (bf16[272,512]{1,0:T(8,128)(2,1)S(1)}, bf16[272,512]{1,0:T(8,128)(2,1)S(1)}, u32[]{:S(2)}, u32[]{:S(2)}) collective-permute-start(bf16[272,512]{1,0:T(8,128)(2,1)S(1)} %fusion.1), channel_id=1, source_target_pairs={{8,0},{0,8},{24,16},{16,24},{9,1},{1,9},{25,17},{17,25},{10,2},{2,... | collective-permute-start | bytes 835592 | tf_op jit(solution)/shard_map/ppermute | solution.py:306
  4.9 0.1 collective-permute-start
  5.0 0.0 copy-done.4
  5.0 0.0 copy-done.5
  5.0 0.0 copy-done
  5.0 0.0 copy-done.2
  5.0 0.0 copy-done.6
  5.0 1.2 %shard_map.94 = (bf16[272,256]{1,0:T(8,128)(2,1)S(1)}, f32[256,256]{1,0:T(8,128)S(1)}, bf16[768,512]{1,0:T(8,128)(2,1)S(1)}, bf16[768,512]{1,0:T(8,128)(2,1)S(1)}) custom-call(bf16[3,512]{1,0:T(4,128)(2,1)S(1)} %copy-done.1, s32[1,256]{1,0:T(1,128)S(1)} %copy-done.6, s32[3,1,256]{2,1,0:T(1,128)S(1)} %copy-done.2, bf16[512,256]{1,0:T(8,128)(2,1)S(1)} %copy-done.5, ...), custom_call_target="tpu_custom_call" | custom-call | flops 536870912 | bytes 3554304 | tf_op jit(solution)/shard_map/pallas_call | solution.py:27
  6.2 0.1 collective-permute-start.2
  6.3 1.3 %collective-permute-done.2.got_ref.refs_4_ = bf16[272,256]{1,0:T(8,128)(2,1)S(1)} collective-permute-done((bf16[272,256]{1,0:T(8,128)(2,1)S(1)}, bf16[272,256]{1,0:T(8,128)(2,1)S(1)}, u32[]{:S(2)}, u32[]{:S(2)}) %collective-permute-start.2) | collective-permute-done | bytes 139296 | tf_op jit(solution)/shard_map/ppermute | solution.py:306
  7.7 2.1 %collective-permute-start.3 = (bf16[96,256]{1,0:T(8,128)(2,1)S(1)}, bf16[96,256]{1,0:T(8,128)(2,1)S(1)}, u32[]{:S(2)}, u32[]{:S(2)}) collective-permute-start(bf16[96,256]{1,0:T(8,128)(2,1)S(1)} %get-tuple-element.32), channel_id=1, source_target_pairs={{2,0},{3,1},{0,2},{1,3},{6,4},{7,5},{4,6},{5,7},{10,8},{11,9},{8,1... | collective-permute-start | bytes 147464 | tf_op jit(solution)/shard_map/ppermute | solution.py:306
  9.8 2.1 %collective-permute-done.3.refs_0_ = bf16[96,256]{1,0:T(8,128)(2,1)S(1)} collective-permute-done((bf16[96,256]{1,0:T(8,128)(2,1)S(1)}, bf16[96,256]{1,0:T(8,128)(2,1)S(1)}, u32[]{:S(2)}, u32[]{:S(2)}) %collective-permute-start.3) | collective-permute-done | bytes 49184 | tf_op jit(solution)/shard_map/ppermute | solution.py:306
  11.8 0.6 %collective-permute-done.1.refs_9_.refs_3_.first_ref = bf16[272,512]{1,0:T(8,128)(2,1)S(1)} collective-permute-done((bf16[272,512]{1,0:T(8,128)(2,1)S(1)}, bf16[272,512]{1,0:T(8,128)(2,1)S(1)}, u32[]{:S(2)}, u32[]{:S(2)}) %collective-permute-start.1) | collective-permute-done | bytes 278560 | tf_op jit(solution)/shard_map/ppermute | solution.py:306
  12.4 2.1 %collective-permute-start.6 = (bf16[272,512]{1,0:T(8,128)(2,1)S(1)}, bf16[272,512]{1,0:T(8,128)(2,1)S(1)}, u32[]{:S(2)}, u32[]{:S(2)}) collective-permute-start(bf16[272,512]{1,0:T(8,128)(2,1)S(1)} %collective-permute-done.1.refs_9_.refs_3_.first_ref), channel_id=1, source_target_pairs={{16,0},{24,8},{0,16},{8,24},{17,1},{25,9},{1,17},{9,25},{18,2},{26... | collective-permute-start | bytes 835592 | tf_op jit(solution)/shard_map/ppermute | solution.py:306
  14.5 2.6 %collective-permute-start.4 = (bf16[96,256]{1,0:T(8,128)(2,1)S(1)}, bf16[96,256]{1,0:T(8,128)(2,1)S(1)}, u32[]{:S(2)}, u32[]{:S(2)}) collective-permute-start(bf16[96,256]{1,0:T(8,128)(2,1)S(1)} %get-tuple-element.34), channel_id=1, source_target_pairs={{4,0},{5,1},{6,2},{7,3},{0,4},{1,5},{2,6},{3,7},{12,8},{13,9},{14,... | collective-permute-start | bytes 147464 | tf_op jit(solution)/shard_map/ppermute | solution.py:306
  17.1 1.3 %collective-permute-start.5 = (bf16[96,256]{1,0:T(8,128)(2,1)S(1)}, bf16[96,256]{1,0:T(8,128)(2,1)S(1)}, u32[]{:S(2)}, u32[]{:S(2)}) collective-permute-start(bf16[96,256]{1,0:T(8,128)(2,1)S(1)} %get-tuple-element.35), channel_id=1, source_target_pairs={{6,0},{7,1},{4,2},{5,3},{2,4},{3,5},{0,6},{1,7},{14,8},{15,9},{12,... | collective-permute-start | bytes 147464 | tf_op jit(solution)/shard_map/ppermute | solution.py:306
  18.4 2.4 %collective-permute-done.4.refs_1_ = bf16[96,256]{1,0:T(8,128)(2,1)S(1)} collective-permute-done((bf16[96,256]{1,0:T(8,128)(2,1)S(1)}, bf16[96,256]{1,0:T(8,128)(2,1)S(1)}, u32[]{:S(2)}, u32[]{:S(2)}) %collective-permute-start.4) | collective-permute-done | bytes 49184 | tf_op jit(solution)/shard_map/ppermute | solution.py:306
  20.8 2.1 %collective-permute-done.5.refs_2_ = bf16[96,256]{1,0:T(8,128)(2,1)S(1)} collective-permute-done((bf16[96,256]{1,0:T(8,128)(2,1)S(1)}, bf16[96,256]{1,0:T(8,128)(2,1)S(1)}, u32[]{:S(2)}, u32[]{:S(2)}) %collective-permute-start.5) | collective-permute-done | bytes 49184 | tf_op jit(solution)/shard_map/ppermute | solution.py:306
  22.9 0.0 collective-permute-done.refs_4_
  22.9 0.5 %collective-permute-start.7 = (bf16[256,512]{1,0:T(8,128)(2,1)S(1)}, bf16[256,512]{1,0:T(8,128)(2,1)S(1)}, u32[]{:S(2)}, u32[]{:S(2)}) collective-permute-start(bf16[256,512]{1,0:T(8,128)(2,1)S(1)} %collective-permute-done.refs_4_), channel_id=1, source_target_pairs={{16,0},{24,8},{0,16},{8,24},{17,1},{25,9},{1,17},{9,25},{18,2},{26... | collective-permute-start | bytes 786440 | tf_op jit(solution)/shard_map/ppermute | solution.py:306
  23.5 0.0 collective-permute-done.6.refs_10_.refs_5_.second_ref
  23.5 0.0 copy-start.3
  23.5 0.7 %copy-done.3 = s32[2,5]{1,0:T(2,128)S(1)} copy-done((s32[2,5]{1,0:T(2,128)S(1)}, s32[2,5]{1,0:T(2,128)}, u32[]{:S(2)}) %copy-start.3) | copy-done | bytes 64
  24.1 2.5 %shard_map.96 = (bf16[256,512]{1,0:T(8,128)(2,1)S(1)}, bf16[256,512]{1,0:T(8,128)(2,1)S(1)}, f32[256,512]{1,0:T(8,128)S(1)}, bf16[64,256]{1,0:T(8,128)(2,1)S(1)}) custom-call(s32[2,5]{1,0:T(2,128)S(1)} %copy-done.3, bf16[96,256]{1,0:T(8,128)(2,1)S(1)} %collective-permute-done.3.refs_0_, bf16[96,256]{1,0:T(8,128)(2,1)S(1)} %collective-permute-done.4.refs_1_, ...), custom_call_target="tpu_custom_call" | custom-call | flops 603979776 | bytes 3705896 | tf_op jit(solution)/shard_map/pallas_call | solution.py:27
  26.7 2.7 %collective-permute-done.7.refs_6_ = bf16[256,512]{1,0:T(8,128)(2,1)S(1)} collective-permute-done((bf16[256,512]{1,0:T(8,128)(2,1)S(1)}, bf16[256,512]{1,0:T(8,128)(2,1)S(1)}, u32[]{:S(2)}, u32[]{:S(2)}) %collective-permute-start.7) | collective-permute-done | bytes 262176 | tf_op jit(solution)/shard_map/ppermute | solution.py:306
  29.3 0.4 shard_map.97
  29.8 0.1 collective-permute-start.8
  29.8 1.3 %collective-permute-done.8.got_ref = bf16[256,256]{1,0:T(8,128)(2,1)S(1)} collective-permute-done((bf16[256,256]{1,0:T(8,128)(2,1)S(1)}, bf16[256,256]{1,0:T(8,128)(2,1)S(1)}, u32[]{:S(2)}, u32[]{:S(2)}) %collective-permute-start.8) | collective-permute-done | bytes 131104 | tf_op jit(solution)/shard_map/ppermute | solution.py:306
  31.2 0.1 collective-permute-start.9
  31.3 2.0 %collective-permute-start.10 = (bf16[320,256]{1,0:T(8,128)(2,1)S(1)}, bf16[320,256]{1,0:T(8,128)(2,1)S(1)}, u32[]{:S(2)}, u32[]{:S(2)}) collective-permute-start(bf16[320,256]{1,0:T(8,128)(2,1)S(1)} %shard_map.98.refs_0_), channel_id=1, source_target_pairs={{4,0},{5,1},{6,2},{7,3},{0,4},{1,5},{2,6},{3,7},{12,8},{13,9},{14,... | collective-permute-start | bytes 491528 | tf_op jit(solution)/shard_map/ppermute | solution.py:306
  33.3 2.4 %collective-permute-start.11 = (bf16[320,256]{1,0:T(8,128)(2,1)S(1)}, bf16[320,256]{1,0:T(8,128)(2,1)S(1)}, u32[]{:S(2)}, u32[]{:S(2)}) collective-permute-start(bf16[320,256]{1,0:T(8,128)(2,1)S(1)} %shard_map.98.refs_0_), channel_id=1, source_target_pairs={{6,0},{7,1},{4,2},{5,3},{2,4},{3,5},{0,6},{1,7},{14,8},{15,9},{12,... | collective-permute-start | bytes 491528 | tf_op jit(solution)/shard_map/ppermute | solution.py:306
  35.7 1.5 %shard_map.100 = (bf16[512,512]{1,0:T(8,128)(2,1)S(1)}, bf16[512,512]{1,0:T(8,128)(2,1)S(1)}, f32[512,512]{1,0:T(8,128)S(1)}) custom-call(s32[2,5]{1,0:T(2,128)S(1)} %copy-done.3, bf16[3,512]{1,0:T(4,128)(2,1)S(1)} %copy-done.1, bf16[272,512]{1,0:T(8,128)(2,1)S(1)} %collective-permute-done.1.refs_9_.refs_3_.first_ref, ...), custom_call_target="tpu_custom_call" | custom-call | flops 402653184 | bytes 3181608 | tf_op jit(solution)/shard_map/pallas_call | solution.py:27
  37.1 1.5 %shard_map.101 = bf16[512,512]{1,0:T(8,128)(2,1)} custom-call(f32[512,512]{1,0:T(8,128)S(1)} %get-tuple-element.50.refs_0_, bf16[512,512]{1,0:T(8,128)(2,1)S(1)} %get-tuple-element.51.refs_1_, bf16[512,512]{1,0:T(8,128)(2,1)S(1)} %get-tuple-element.52.refs_2_, bf16[272,512]{1,0:T(8,128)(2,1)S(1)} %collective-permute-done.1.refs_9_.refs_3_.first_ref, ...), custom_call_target="tpu_custom_call" | custom-call | flops 536870912 | bytes 3702784 | tf_op jit(solution)/shard_map/pallas_call | solution.py:27
  38.6 1.6 %collective-permute-done.9.refs_1_ = bf16[320,256]{1,0:T(8,128)(2,1)S(1)} collective-permute-done((bf16[320,256]{1,0:T(8,128)(2,1)S(1)}, bf16[320,256]{1,0:T(8,128)(2,1)S(1)}, u32[]{:S(2)}, u32[]{:S(2)}) %collective-permute-start.9) | collective-permute-done | bytes 163872 | tf_op jit(solution)/shard_map/ppermute | solution.py:306
  40.2 6.1 %collective-permute-done.10.refs_2_ = bf16[320,256]{1,0:T(8,128)(2,1)S(1)} collective-permute-done((bf16[320,256]{1,0:T(8,128)(2,1)S(1)}, bf16[320,256]{1,0:T(8,128)(2,1)S(1)}, u32[]{:S(2)}, u32[]{:S(2)}) %collective-permute-start.10) | collective-permute-done | bytes 163872 | tf_op jit(solution)/shard_map/ppermute | solution.py:306
  46.4 0.0 collective-permute-done.11.refs_3_
  46.4 0.1 shard_map.99.own_ref
  46.5 0.1 collective-permute-start.12
  46.5 1.5 %collective-permute-done.12.other_ref = bf16[512,256]{1,0:T(8,128)(2,1)S(1)} collective-permute-done((bf16[512,256]{1,0:T(8,128)(2,1)S(1)}, bf16[512,256]{1,0:T(8,128)(2,1)S(1)}, u32[]{:S(2)}, u32[]{:S(2)}) %collective-permute-start.12) | collective-permute-done | bytes 262176 | tf_op jit(solution)/shard_map/ppermute | solution.py:306
  48.1 1.0 %shard_map.102 = (f32[256,512]{1,0:T(8,128)}, f32[256,512]{1,0:T(8,128)}) custom-call(bf16[512,256]{1,0:T(8,128)(2,1)S(1)} %shard_map.99.own_ref, bf16[512,256]{1,0:T(8,128)(2,1)S(1)} %collective-permute-done.12.other_ref), custom_call_target="tpu_custom_call" | custom-call | bytes 1572864 | tf_op jit(solution)/shard_map/pallas_call | solution.py:27
  (3 shorter events, 0.1 us)
Async XLA Ops:
  0.6 4.3 %copy-start.4 = (bf16[3,1,512,256]{3,2,1,0:T(8,128)(2,1)S(1)}, bf16[3,1,512,256]{3,2,1,0:T(8,128)(2,1)}, u32[]{:S(2)}) copy-start(bf16[3,1,512,256]{3,2,1,0:T(8,128)(2,1)} %merge_ref.1) | copy-start | bytes 2359300
  0.6 1.2 %copy-start.1 = (bf16[3,512]{1,0:T(4,128)(2,1)S(1)}, bf16[3,512]{1,0:T(4,128)(2,1)}, u32[]{:S(2)}) copy-start(bf16[3,512]{1,0:T(4,128)(2,1)} %own_ref.1) | copy-start | bytes 9220
  0.7 4.3 %copy-start.5 = (bf16[512,256]{1,0:T(8,128)(2,1)S(1)}, bf16[512,256]{1,0:T(8,128)(2,1)}, u32[]{:S(2)}) copy-start(bf16[512,256]{1,0:T(8,128)(2,1)} %proj_ref.1) | copy-start | bytes 786436
  1.8 3.2 %copy-start = (bf16[512,512]{1,0:T(8,128)(2,1)S(1)}, bf16[512,512]{1,0:T(8,128)(2,1)}, u32[]{:S(2)}) copy-start(bf16[512,512]{1,0:T(8,128)(2,1)} %matrix_ref.3) | copy-start | bytes 1572868
  1.8 3.1 %copy-start.2 = (s32[3,1,256]{2,1,0:T(1,128)S(1)}, s32[3,1,256]{2,1,0:T(1,128)}, u32[]{:S(2)}) copy-start(s32[3,1,256]{2,1,0:T(1,128)} %refs_6_.1) | copy-start | bytes 9220
  1.9 3.1 %copy-start.6 = (s32[1,256]{1,0:T(1,128)S(1)}, s32[1,256]{1,0:T(1,128)}, u32[]{:S(2)}) copy-start(s32[1,256]{1,0:T(1,128)} %pivots_ref.1) | copy-start | bytes 3076
  1.9 10.5 %collective-permute-start.1 = (bf16[272,512]{1,0:T(8,128)(2,1)S(1)}, bf16[272,512]{1,0:T(8,128)(2,1)S(1)}, u32[]{:S(2)}, u32[]{:S(2)}) collective-permute-start(bf16[272,512]{1,0:T(8,128)(2,1)S(1)} %fusion.1), channel_id=1, source_target_pairs={{8,0},{0,8},{24,16},{16,24},{9,1},{1,9},{25,17},{17,25},{10,2},{2,... | collective-permute-start | bytes 835592 | tf_op jit(solution)/shard_map/ppermute | solution.py:306
  4.9 18.1 %collective-permute-start = (bf16[256,512]{1,0:T(8,128)(2,1)S(1)}, bf16[256,512]{1,0:T(8,128)(2,1)S(1)}, u32[]{:S(2)}, u32[]{:S(2)}) collective-permute-start(bf16[256,512]{1,0:T(8,128)(2,1)S(1)} %get-tuple-element.58), channel_id=1, source_target_pairs={{8,0},{0,8},{24,16},{16,24},{9,1},{1,9},{25,17},{17,25},{10,2},{2,... | collective-permute-start | bytes 786440 | tf_op jit(solution)/shard_map/ppermute | solution.py:306
  6.2 1.4 %collective-permute-start.2 = (bf16[272,256]{1,0:T(8,128)(2,1)S(1)}, bf16[272,256]{1,0:T(8,128)(2,1)S(1)}, u32[]{:S(2)}, u32[]{:S(2)}) collective-permute-start(bf16[272,256]{1,0:T(8,128)(2,1)S(1)} %get-tuple-element.31.sent_ref.refs_3_), channel_id=1, source_target_pairs={{1,0},{0,1},{3,2},{2,3},{5,4},{4,5},{7,6},{6,7},{9,8},{8,9},{11,10... | collective-permute-start | bytes 417800 | tf_op jit(solution)/shard_map/ppermute | solution.py:306
  7.7 4.2 %collective-permute-start.3 = (bf16[96,256]{1,0:T(8,128)(2,1)S(1)}, bf16[96,256]{1,0:T(8,128)(2,1)S(1)}, u32[]{:S(2)}, u32[]{:S(2)}) collective-permute-start(bf16[96,256]{1,0:T(8,128)(2,1)S(1)} %get-tuple-element.32), channel_id=1, source_target_pairs={{2,0},{3,1},{0,2},{1,3},{6,4},{7,5},{4,6},{5,7},{10,8},{11,9},{8,1... | collective-permute-start | bytes 147464 | tf_op jit(solution)/shard_map/ppermute | solution.py:306
  12.4 11.1 %collective-permute-start.6 = (bf16[272,512]{1,0:T(8,128)(2,1)S(1)}, bf16[272,512]{1,0:T(8,128)(2,1)S(1)}, u32[]{:S(2)}, u32[]{:S(2)}) collective-permute-start(bf16[272,512]{1,0:T(8,128)(2,1)S(1)} %collective-permute-done.1.refs_9_.refs_3_.first_ref), channel_id=1, source_target_pairs={{16,0},{24,8},{0,16},{8,24},{17,1},{25,9},{1,17},{9,25},{18,2},{26... | collective-permute-start | bytes 835592 | tf_op jit(solution)/shard_map/ppermute | solution.py:306
  14.5 6.4 %collective-permute-start.4 = (bf16[96,256]{1,0:T(8,128)(2,1)S(1)}, bf16[96,256]{1,0:T(8,128)(2,1)S(1)}, u32[]{:S(2)}, u32[]{:S(2)}) collective-permute-start(bf16[96,256]{1,0:T(8,128)(2,1)S(1)} %get-tuple-element.34), channel_id=1, source_target_pairs={{4,0},{5,1},{6,2},{7,3},{0,4},{1,5},{2,6},{3,7},{12,8},{13,9},{14,... | collective-permute-start | bytes 147464 | tf_op jit(solution)/shard_map/ppermute | solution.py:306
  17.1 5.9 %collective-permute-start.5 = (bf16[96,256]{1,0:T(8,128)(2,1)S(1)}, bf16[96,256]{1,0:T(8,128)(2,1)S(1)}, u32[]{:S(2)}, u32[]{:S(2)}) collective-permute-start(bf16[96,256]{1,0:T(8,128)(2,1)S(1)} %get-tuple-element.35), channel_id=1, source_target_pairs={{6,0},{7,1},{4,2},{5,3},{2,4},{3,5},{0,6},{1,7},{14,8},{15,9},{12,... | collective-permute-start | bytes 147464 | tf_op jit(solution)/shard_map/ppermute | solution.py:306
  22.9 6.4 %collective-permute-start.7 = (bf16[256,512]{1,0:T(8,128)(2,1)S(1)}, bf16[256,512]{1,0:T(8,128)(2,1)S(1)}, u32[]{:S(2)}, u32[]{:S(2)}) collective-permute-start(bf16[256,512]{1,0:T(8,128)(2,1)S(1)} %collective-permute-done.refs_4_), channel_id=1, source_target_pairs={{16,0},{24,8},{0,16},{8,24},{17,1},{25,9},{1,17},{9,25},{18,2},{26... | collective-permute-start | bytes 786440 | tf_op jit(solution)/shard_map/ppermute | solution.py:306
  23.5 0.7 %copy-start.3 = (s32[2,5]{1,0:T(2,128)S(1)}, s32[2,5]{1,0:T(2,128)}, u32[]{:S(2)}) copy-start(s32[2,5]{1,0:T(2,128)} %lists_ref.3) | copy-start | bytes 124
  29.8 1.4 %collective-permute-start.8 = (bf16[256,256]{1,0:T(8,128)(2,1)S(1)}, bf16[256,256]{1,0:T(8,128)(2,1)S(1)}, u32[]{:S(2)}, u32[]{:S(2)}) collective-permute-start(bf16[256,256]{1,0:T(8,128)(2,1)S(1)} %get-tuple-element.48), channel_id=1, source_target_pairs={{1,0},{0,1},{3,2},{2,3},{5,4},{4,5},{7,6},{6,7},{9,8},{8,9},{11,10... | collective-permute-start | bytes 393224 | tf_op jit(solution)/shard_map/ppermute | solution.py:306
  31.2 9.0 %collective-permute-start.9 = (bf16[320,256]{1,0:T(8,128)(2,1)S(1)}, bf16[320,256]{1,0:T(8,128)(2,1)S(1)}, u32[]{:S(2)}, u32[]{:S(2)}) collective-permute-start(bf16[320,256]{1,0:T(8,128)(2,1)S(1)} %shard_map.98.refs_0_), channel_id=1, source_target_pairs={{2,0},{3,1},{0,2},{1,3},{6,4},{7,5},{4,6},{5,7},{10,8},{11,9},{8,1... | collective-permute-start | bytes 491528 | tf_op jit(solution)/shard_map/ppermute | solution.py:306
  31.3 15.1 %collective-permute-start.10 = (bf16[320,256]{1,0:T(8,128)(2,1)S(1)}, bf16[320,256]{1,0:T(8,128)(2,1)S(1)}, u32[]{:S(2)}, u32[]{:S(2)}) collective-permute-start(bf16[320,256]{1,0:T(8,128)(2,1)S(1)} %shard_map.98.refs_0_), channel_id=1, source_target_pairs={{4,0},{5,1},{6,2},{7,3},{0,4},{1,5},{2,6},{3,7},{12,8},{13,9},{14,... | collective-permute-start | bytes 491528 | tf_op jit(solution)/shard_map/ppermute | solution.py:306
  33.3 13.1 %collective-permute-start.11 = (bf16[320,256]{1,0:T(8,128)(2,1)S(1)}, bf16[320,256]{1,0:T(8,128)(2,1)S(1)}, u32[]{:S(2)}, u32[]{:S(2)}) collective-permute-start(bf16[320,256]{1,0:T(8,128)(2,1)S(1)} %shard_map.98.refs_0_), channel_id=1, source_target_pairs={{6,0},{7,1},{4,2},{5,3},{2,4},{3,5},{0,6},{1,7},{14,8},{15,9},{12,... | collective-permute-start | bytes 491528 | tf_op jit(solution)/shard_map/ppermute | solution.py:306
  46.5 1.6 %collective-permute-start.12 = (bf16[512,256]{1,0:T(8,128)(2,1)S(1)}, bf16[512,256]{1,0:T(8,128)(2,1)S(1)}, u32[]{:S(2)}, u32[]{:S(2)}) collective-permute-start(bf16[512,256]{1,0:T(8,128)(2,1)S(1)} %shard_map.99.own_ref), channel_id=1, source_target_pairs={{1,0},{0,1},{3,2},{2,3},{5,4},{4,5},{7,6},{6,7},{9,8},{8,9},{11,10... | collective-permute-start | bytes 786440 | tf_op jit(solution)/shard_map/ppermute | solution.py:306

commit v3 on v2

v3 whole, which is shorter than its diff:
```python
import functools
import math

import jax
import jax.numpy as jnp
from jax import lax
from jax.experimental import pallas as pl
from jax.experimental.pallas import tpu as pltpu
from jax.sharding import PartitionSpec as P

SPREAD = 25.0
EXPONENT = -SPREAD * math.log2(math.e)
FAR_OFF = 1024.0
LANES = 128
HEADED = 0
HEIGHT = 16
ROW_HI, ROW_LO, MEET, PIVOT = 3, 4, 5, 6
BF16, F32 = jnp.bfloat16, jnp.float32


def call(body, outs, *args):
    return pl.pallas_call(
        body,
        out_shape=[jax.ShapeDtypeStruct(s, d) for s, d in outs],
        in_specs=[pl.BlockSpec(memory_space=pltpu.VMEM)] * len(args),
        out_specs=[pl.BlockSpec(memory_space=pltpu.VMEM)] * len(outs),
        compiler_params=pltpu.CompilerParams(vmem_limit_bytes=40 << 20),
        cost_estimate=pl.CostEstimate(flops=0, bytes_accessed=0, transcendentals=0),
    )(*args)


def dot(a, b, over_a=1, over_b=0):
    return lax.dot_general(a, b, (((over_a,), (over_b,)), ((), ())), preferred_element_type=F32)


def halves(x):
    hi = x.astype(BF16)
    return hi, (x - hi.astype(F32)).astype(BF16)


def rows_of(entries, width):
    row = lax.broadcasted_iota(jnp.int32, (HEIGHT, width), 0)
    out = jnp.zeros((HEIGHT, width), F32)
    for k, entry in enumerate(entries):
        out = jnp.where(row == k, entry, out)
    return out


def norm_parts(p):
    n = p[0:1] * p[0:1] + p[1:2] * p[1:2] + p[2:3] * p[2:3]
    hi = n.astype(BF16).astype(F32)
    mid = (n - hi).astype(BF16).astype(F32)
    return [hi, mid, n - hi - mid]


def left_features(p, penalties):
    entries = [p[0:1], p[1:2], p[2:3], *norm_parts(p), 1.0, 1.0, 1.0, *penalties]
    return rows_of(entries, p.shape[1]).astype(BF16)


def right_features(p, marks):
    entries = [-2.0 * p[0:1], -2.0 * p[1:2], -2.0 * p[2:3], 1.0, 1.0, 1.0, *norm_parts(p), *marks]
    return rows_of(entries, p.shape[1]).astype(BF16)


def gauss(left, right, amp):
    return jnp.exp2(EXPONENT * dot(left, right, 0, 0)) * amp


def lane_index(width):
    return lax.broadcasted_iota(jnp.int32, (1, width), 1)


def chosen(attributes, index):
    spot = lax.broadcasted_iota(jnp.int32, (attributes.shape[1], index.shape[1]), 0)
    one_hot = jnp.where(spot == index, 1.0, 0.0).astype(BF16)
    return dot(attributes.astype(BF16), one_hot)


def bit_of(value, place):
    return (value >> place) & 1


def bit_of(value, place):
    return (value >> place) & 1


def describe_body(*refs):
    sources, outs, held, sems = refs[:7], refs[7:13], refs[13:20], refs[20]
    given_ref, kept_ref, hi_ref, lo_ref, top_pivots_ref, table_ref = outs
    lists_ref, points_ref, pivots_ref, merges_ref, proj_ref, matrix_ref, merge_ref = held
    levels, rank = merge_ref.shape[:2]
    position = lax.axis_index("leaf")
    copies = [
        pltpu.make_async_copy(a, b, sems.at[k]) for k, (a, b) in enumerate(zip(sources[:6], held[:6]))
    ]
    for level in range(levels):
        start = pl.multiple_of(bit_of(position, level) * rank, rank)
        source = sources[6].at[level, 0, pl.ds(start, rank), :]
        copies.append(pltpu.make_async_copy(source, merge_ref.at[level], sems.at[6 + level]))
    for copy in copies:
        copy.start()
    for copy in copies[:4]:
        copy.wait()
    lists = lists_ref[...]
    blocks = lists.shape[0]
    for c in range(3 * blocks):
        listed = jnp.max(jnp.where(lists == c, 1.0, 0.0), axis=1, keepdims=True)
        for i in range(blocks):
            row = c * blocks + i
            table_ref[row : row + 1, :] = jnp.broadcast_to(FAR_OFF * (1.0 - listed[i : i + 1]), (1, LANES))
    top_pivots_ref[...] = merges_ref[merges_ref.shape[0] - 1]
    p = points_ref[...].astype(F32)
    width = p.shape[1]
    spot = lane_index(width)
    attributes = rows_of(
        [p[0:1], p[1:2], p[2:3], (spot // rank).astype(F32), (spot % rank).astype(F32)], width
    )
    skeleton = chosen(attributes, pivots_ref[...])
    row = lax.broadcasted_iota(jnp.int32, skeleton.shape, 0)
    for level in range(levels - 1):
        q = merges_ref[level]
        skeleton = jnp.where(row == PIVOT + 2 * level, (q // rank).astype(F32), skeleton)
        skeleton = jnp.where(row == PIVOT + 2 * level + 1, (q % rank).astype(F32), skeleton)
    given_ref[0:HEIGHT, :] = skeleton.astype(BF16)
    for copy in copies[4:]:
        copy.wait()
    c = dot(proj_ref[...], matrix_ref[...], 0)
    for level in range(levels):
        hi, lo = halves(c)
        hi_ref[pl.ds(level * rank, rank), :] = hi
        lo_ref[pl.ds(level * rank, rank), :] = lo
        m = merge_ref[level]
        c = dot(m, hi, 0, 0) + dot(m, lo, 0, 0)
    second = bit_of(position, 0) == 1
    middle = c.shape[1] // 2
    low, high = c[:, :middle], c[:, middle:]
    kept_ref[...] = jnp.where(second, high, low)
    given_ref[HEIGHT:, :] = jnp.where(second, low, high).astype(BF16)


def scatter_body(kept_ref, sent_ref, got_ref, mine_ref, *message_refs):
    chip = (lax.axis_index("leaf") >> 1) % (len(message_refs) + 1)
    count = mine_ref.shape[0]
    for k, ref in enumerate((mine_ref, *message_refs)):
        start = pl.multiple_of((chip ^ k) * count, count)
        other = got_ref[pl.ds(pl.multiple_of(HEIGHT + start, HEIGHT), count), :]
        piece = kept_ref[pl.ds(start, count), :] + other.astype(F32)
        if k == 0:
            ref[...] = piece
        else:
            ref[0:HEIGHT, :] = sent_ref[0:HEIGHT, :]
            ref[HEIGHT : 2 * HEIGHT, :] = got_ref[0:HEIGHT, :]
            ref[2 * HEIGHT :, :] = piece.astype(BF16)


def piece_body(*refs):
    mine_ref, *messages, out_ref = refs
    piece = mine_ref[...]
    for ref in messages:
        piece += ref[2 * HEIGHT :, :].astype(F32)
    out_ref[...] = piece.astype(BF16)


def tree_body(far_amp, *refs):
    *messages, sent_ref, got_ref, top_pivots_ref, hi_ref, lo_ref, top_ref, part_ref = refs
    position = lax.axis_index("leaf")
    rank = top_pivots_ref.shape[1]
    levels = hi_ref.shape[0] // rank
    nodes = [sent_ref[0:HEIGHT, :].astype(F32), got_ref[0:HEIGHT, :].astype(F32)]
    for ref in messages:
        nodes += [ref[0:HEIGHT, :].astype(F32), ref[HEIGHT : 2 * HEIGHT, :].astype(F32)]
    pivots = nodes
    row = lax.broadcasted_iota(jnp.int32, (HEIGHT, rank), 0)
    path = []
    for level in range(levels):
        path.append(nodes[0])
        flip = bit_of(position, level)
        merged = []
        for j in range(len(nodes) // 2):
            if level < levels - 1:
                source = pivots[j << level + 1]
                k = PIVOT + 2 * level
                q = (source[k : k + 1] * rank + source[k + 1 : k + 2]).astype(jnp.int32)
            else:
                q = top_pivots_ref[...]
            q = jnp.where(flip == 1, jnp.where(q < rank, q + rank, q - rank), q)
            far = jnp.where(row == MEET, float(level + 1), nodes[2 * j + 1])
            merged.append(chosen(jnp.concatenate([nodes[2 * j], far], axis=1), q))
        nodes = merged
    top = nodes[0]
    top_ref[...] = top
    total = jnp.zeros(part_ref.shape, F32)
    for level in range(levels):
        penalty = jnp.where(top[MEET : MEET + 1] == float(level + 1), 0.0, FAR_OFF)
        block = gauss(left_features(top, [penalty]), right_features(path[level], [1.0]), -far_amp)
        block_hi, block_lo = halves(block)
        hi = hi_ref[pl.ds(level * rank, rank), :]
        lo = lo_ref[pl.ds(level * rank, rank), :]
        total += dot(block_hi, hi) + dot(block_hi, lo) + dot(block_lo, hi)
    part_ref[...] = total


def top_near_body(near_amp, even_ahead, table_ref, top_ref, first_ref, second_ref, top_first, top_second):
    top = top_ref[...]
    blocks = block_count_of(table_ref)
    width = first_ref.shape[1]
    marks = block_marks(width, blocks)
    top_block = top[ROW_HI : ROW_HI + 1].astype(jnp.int32)
    top_here = top[MEET : MEET + 1] == 0.0
    for ref, base, near_ref in zip((first_ref, second_ref), bases_of(even_ahead, blocks), (top_first, top_second)):
        table = penalty_table(table_ref, base, blocks)
        penalties = [
            jnp.where(top_here, per_block(top_block, [table[i][k] for i in range(blocks)]), FAR_OFF)
            for k in range(blocks)
        ]
        columns = right_features(ref[0:3, :].astype(F32), marks)
        near_ref[...] = gauss(left_features(top, penalties), columns, near_amp).astype(BF16)


def block_count_of(table_ref):
    return math.isqrt(table_ref.shape[0] // 3)


def penalty_table(table_ref, base, blocks):
    return [
        [table_ref[pl.ds((base + k) * blocks + i, 1), 0:1] for k in range(blocks)] for i in range(blocks)
    ]


def per_block(block_index, values):
    out = jnp.zeros(block_index.shape, F32)
    for i, value in enumerate(values):
        out = jnp.where(block_index == i, value, out)
    return out


def block_marks(width, blocks):
    spot = lane_index(width) // (width // blocks)
    return [jnp.where(spot == k, 1.0, 0.0) for k in range(blocks)]


def bases_of(even_ahead, blocks):
    if not even_ahead:
        return [0, 2 * blocks]
    odd = lax.axis_index("blk") % 2
    return [2 * blocks * (1 - odd), 2 * blocks * odd]


def near_body(near_amp, even_ahead, table_ref, own_ref, first_ref, second_ref, matrix_ref, *outs):
    near_first, near_second, own_terms = outs
    blocks = block_count_of(table_ref)
    own = own_ref[...].astype(F32)
    width = own.shape[1]
    spot = lane_index(width) // (width // blocks)
    marks = block_marks(width, blocks)

    def near(base, columns):
        table = penalty_table(table_ref, base, blocks)
        penalties = [per_block(spot, [table[i][k] for i in range(blocks)]) for k in range(blocks)]
        return gauss(left_features(own, penalties), right_features(columns, marks), near_amp).astype(BF16)

    bases = bases_of(even_ahead, blocks)
    near_first[...] = near(bases[0], first_ref[0:3, :].astype(F32))
    near_second[...] = near(bases[1], second_ref[0:3, :].astype(F32))
    own_terms[...] = dot(near(blocks, own), matrix_ref[...])


def near_product(start_ref, first_ref, second_ref, *chunks):
    total = start_ref[...]
    per_side = len(chunks) // 2
    for side, left_ref in enumerate((first_ref, second_ref)):
        at = 0
        for k, chunk_ref in enumerate(chunks[side * per_side : (side + 1) * per_side]):
            lead = HEIGHT if k == HEADED else 0
            count = chunk_ref.shape[0] - lead
            total += dot(left_ref[:, at : at + count], chunk_ref[lead:, :])
            at += count
    return total


def sample_body(*refs):
    refs[-1][...] = near_product(*refs[:-1]).astype(BF16)


def share_body(*refs):
    *ins, kept_ref, given_ref = refs
    total = near_product(*ins)
    second = bit_of(lax.axis_index("leaf"), 0) == 1
    middle = total.shape[1] // 2
    low, high = total[:, :middle], total[:, middle:]
    kept_ref[...] = jnp.where(second, high, low)
    given_ref[...] = jnp.where(second, low, high).astype(BF16)


def pair_body(kept_ref, got_ref, out_ref):
    out_ref[...] = (kept_ref[...] + got_ref[...].astype(F32)).astype(BF16)


def total_body(*refs):
    *messages, out_ref = refs
    total = messages[0][...].astype(F32)
    for ref in messages[1:]:
        total += ref[...].astype(F32)
    out_ref[...] = total.astype(BF16)


def gather_body(*refs):
    *messages, out_ref = refs
    count = messages[0].shape[0]
    chip = (lax.axis_index("leaf") >> 1) % len(messages)
    for k, ref in enumerate(messages):
        out_ref[pl.ds(pl.multiple_of((chip ^ k) * count, count), count), :] = ref[...]


def join_body(own_ref, other_ref, out_ref):
    second = bit_of(lax.axis_index("leaf"), 0) == 1
    middle = own_ref.shape[1]
    own, other = own_ref[...].astype(F32), other_ref[...].astype(F32)
    out_ref[:, :middle] = jnp.where(second, other, own)
    out_ref[:, middle:] = jnp.where(second, own, other)


def permuted(block, axis, route):
    return lax.ppermute(block, axis, [(route(i), i) for i in range(lax.axis_size(axis))])


def swapped(block, distance):
    return permuted(block, "leaf", lambda i: i ^ distance)


def on_device(points, test_matrix, near_lists, leaf_pivots, leaf_proj, merge_pivots, merge_proj):
    row_count, sample_count = test_matrix.shape
    block_count, slot_count = near_lists.shape
    skel_rank = leaf_pivots.shape[1]
    level_count = merge_pivots.shape[0]
    near_amp = 9.0 / math.sqrt(slot_count * (row_count // block_count))
    far_amp = 3.0 / math.sqrt(skel_rank)

    middle = sample_count // 2
    chips = 1 << level_count - 1
    piece = skel_rank // chips

    count = lax.axis_size("blk")
    paired = count % 2 == 0 and count > 2
    if paired:
        step = lambda i, by: (i + (by if i % 2 == 0 else -by)) % count
        routes = [lambda i: step(i, 1), lambda i: step(i, -1), lambda i: step(i, -2)]
    else:
        routes = [lambda i: (i - 1) % count, lambda i: (i + 1) % count]
    header = jnp.pad(points, ((0, HEIGHT - points.shape[0]), (0, 0)))
    unit = row_count // 8
    edges = [0, 4 * unit, 8 * unit]
    chunks = [test_matrix[a:b] for a, b in zip(edges[:-1], edges[1:])]
    chunks[HEADED] = jnp.concatenate([header, chunks[HEADED]], axis=0)
    first = [permuted(c, "blk", routes[0]) for c in chunks]
    onward = list(first if paired else chunks)

    inputs = [near_lists, points, leaf_pivots, merge_pivots, leaf_proj, test_matrix, merge_proj]
    held = [(x.shape, x.dtype) for x in inputs[:6]] + [((level_count, skel_rank, skel_rank), BF16)]
    given, kept, hi, lo, top_pivots, table = pl.pallas_call(
        describe_body,
        out_shape=[
            jax.ShapeDtypeStruct((HEIGHT + skel_rank, middle), BF16),
            jax.ShapeDtypeStruct((skel_rank, middle), F32),
            jax.ShapeDtypeStruct((level_count * skel_rank, sample_count), BF16),
            jax.ShapeDtypeStruct((level_count * skel_rank, sample_count), BF16),
            jax.ShapeDtypeStruct((1, skel_rank), jnp.int32),
            jax.ShapeDtypeStruct((3 * block_count * block_count, LANES), F32),
        ],
        in_specs=[pl.BlockSpec(memory_space=pltpu.HBM)] * 7,
        out_specs=[pl.BlockSpec(memory_space=pltpu.VMEM)] * 6,
        scratch_shapes=[pltpu.VMEM(*h) for h in held] + [pltpu.SemaphoreType.DMA((6 + level_count,))],
        compiler_params=pltpu.CompilerParams(vmem_limit_bytes=40 << 20),
        cost_estimate=pl.CostEstimate(flops=0, bytes_accessed=0, transcendentals=0),
    )(*[pltpu.with_memory_space_constraint(x, pltpu.HBM) for x in inputs])
    got = swapped(given, 1)
    mine, *messages = call(
        scatter_body,
        [((piece, middle), F32)] + [((2 * HEIGHT + piece, middle), BF16)] * (chips - 1),
        kept,
        given,
        got,
    )
    messages = [swapped(m, 2 * k + 2) for k, m in enumerate(messages)]
    onward[0], messages[0] = lax.optimization_barrier((onward[0], messages[0]))
    second = [permuted(onward[0], "blk", routes[-1])]
    onward[1], messages = lax.optimization_barrier((onward[1], messages))
    second += [permuted(c, "blk", routes[-1]) for c in onward[1:]]
    (omega_piece,) = call(piece_body, [((piece, middle), BF16)], mine, *messages)
    omega_pieces = [omega_piece] + [swapped(omega_piece, 2 * k) for k in range(1, chips)]
    top, far_part = call(
        functools.partial(tree_body, far_amp),
        [((HEIGHT, skel_rank), F32), ((skel_rank, sample_count), F32)],
        *messages,
        given,
        got,
        top_pivots,
        hi,
        lo,
    )
    near_first, near_second, own_terms = call(
        functools.partial(near_body, near_amp, paired),
        [((row_count, row_count), BF16)] * 2 + [((row_count, sample_count), F32)],
        table,
        points,
        first[HEADED],
        second[HEADED],
        test_matrix,
    )
    top_first, top_second = call(
        functools.partial(top_near_body, near_amp, paired),
        [((skel_rank, row_count), BF16)] * 2,
        table,
        top,
        first[HEADED],
        second[HEADED],
    )
    second[-1], omega_pieces = lax.optimization_barrier((second[-1], omega_pieces))
    kept, given = call(
        share_body,
        [((skel_rank, middle), F32), ((skel_rank, middle), BF16)],
        far_part,
        top_first,
        top_second,
        *first,
        *second,
    )
    got = swapped(given, 1)
    (message,) = call(pair_body, [((skel_rank, middle), BF16)], kept, got)
    messages = [message] + [swapped(message, 2 * k) for k in range(1, chips)]
    (omega,) = call(gather_body, [((skel_rank, middle), BF16)], *omega_pieces)
    (top_omega,) = call(join_body, [((skel_rank, sample_count), F32)], omega, swapped(omega, 1))
    (sample,) = call(
        sample_body,
        [((row_count, sample_count), BF16)],
        own_terms,
        near_first,
        near_second,
        *first,
        *second,
    )
    (total,) = call(total_body, [((skel_rank, middle), BF16)], *messages)
    total, sample, top_omega = lax.optimization_barrier((total, sample, top_omega))
    (top_samples,) = call(join_body, [((skel_rank, sample_count), F32)], total, swapped(total, 1))
    return (sample, top_samples, top_omega)


def solution(mesh):
    placed = (
        P(None, ("blk", "leaf")),
        P(("blk", "leaf"), None),
        P(("blk", "leaf"), None),
        P(("blk", "leaf"), None),
        P(("blk", "leaf"), None),
        P(None, ("blk", "leaf"), None),
        P(None, ("blk", "leaf"), None, None),
    )
    return jax.shard_map(
        on_device,
        mesh=mesh,
        in_specs=placed,
        out_specs=(P(("blk", "leaf"), None), P(("blk", "leaf"), None), P(("blk", "leaf"), None)),
        check_vma=False,
    )
```

time: 49.8 us -> 46.7 us (0.938); the launches traced: 49.1 us -> 46.5 us
  waiting for transfers between devices: 21.8 us -> 14.4 us
  starting transfers between devices: 16.4 us -> 20.7 us
  Pallas kernels: 8.29 us -> 9.56 us
  local copies, waits for them, and re-layouts: 1.86 us -> 1.09 us
    ppermute x13 -> x17, waiting for transfers between devices: 21.8 us -> 14.4 us  [permuted(): lax.ppermute(block, axis, [(route(i), i) for i in range(lax.axis_size(axi...]
    ppermute x13 -> x17, starting transfers between devices: 16.4 us -> 20.7 us  [permuted(): lax.ppermute(block, axis, [(route(i), i) for i in range(lax.axis_size(axi...]
    pallas_call x0 -> x1, Pallas kernels: none -> 2.53 us  [on_device(): pl.pallas_call(describe_body, out_shape=[jax.ShapeDtypeStruct((HEIGHT + s...]
    pallas_call x9 -> x12, Pallas kernels: 8.29 us -> 7.03 us  [call(): pl.pallas_call(body, out_shape=[jax.ShapeDtypeStruct(s, d) for s, d in ou...]
    unnamed x14 -> x6, local copies, waits for them, and re-layouts: 0.71 us -> 0.02 us
  transfers between devices with their start and end apart: 13 -> 17, of which waited for: 10 -> 8; matrix products, arithmetic and copies ran while one was open for 0% -> 0% of each run, Pallas kernels for 14% -> 17%
where the time goes in v3:
time: 46.7 us; the launch traced here: 46.5 us
  starting transfers between devices  20.7 us (44%)
  waiting for transfers between devices  14.4 us (31%)
  Pallas kernels  9.56 us (20%)
  local copies, waits for them, and re-layouts  1.09 us (2%)
  between operations  0.8 us (2%)
    ppermute x17, starting transfers between devices, permuted(): lax.ppermute(block, axis, [(route(i), i) for i in range(lax.axis_size(axi...  20.7 us
    ppermute x17, waiting for transfers between devices, permuted(): lax.ppermute(block, axis, [(route(i), i) for i in range(lax.axis_size(axi...  14.4 us
    pallas_call x12, Pallas kernels, call(): pl.pallas_call(body, out_shape=[jax.ShapeDtypeStruct(s, d) for s, d in ou...  7.03 us
    pallas_call x1, Pallas kernels, on_device(): pl.pallas_call(describe_body, out_shape=[jax.ShapeDtypeStruct((HEIGHT + s...  2.53 us
    slice x1, local copies, waits for them, and re-layouts, on_device(): chunks = [test_matrix[a:b] for a, b in zip(edges[:-1], edges[1:])]  1.07 us
  transfers between devices with their start and end apart: 17, of which 8 were waited for; matrix products, arithmetic and copies ran while one was open for 0% of the time, Pallas kernels for 17%

profile of v3, /device:TPU:0, one launch (start us, length us, event | category | flops | bytes accessed | tf_op | source)
XLA Modules:
  0.0 46.5 jit_solution(18296241509969919815)
XLA Ops:
  0.6 0.0 copy-start.1
  0.6 1.1 %fusion.2 = (bf16[256,512]{1,0:T(8,128)(2,1)S(1)}, bf16[256,512]{1,0:T(8,128)(2,1)S(1)}) fusion(bf16[512,512]{1,0:T(8,128)(2,1)} %matrix_ref.1), kind=kLoop, calls=%fused_computation.3 | loop fusion | bytes 1048576 | tf_op jit(solution)/shard_map/slice | solution.py:354
  1.7 0.0 copy-done.1
  1.8 3.0 %collective-permute-start.1 = (bf16[272,512]{1,0:T(8,128)(2,1)S(1)}, bf16[272,512]{1,0:T(8,128)(2,1)S(1)}, u32[]{:S(2)}, u32[]{:S(2)}) collective-permute-start(bf16[272,512]{1,0:T(8,128)(2,1)S(1)} %fusion.1), channel_id=1, source_target_pairs={{8,0},{0,8},{24,16},{16,24},{9,1},{1,9},{25,17},{17,25},{10,2},{2,... | collective-permute-start | bytes 835592 | tf_op jit(solution)/shard_map/ppermute | solution.py:325
  4.8 0.1 collective-permute-start
  4.8 2.5 %shard_map.94 = (bf16[272,256]{1,0:T(8,128)(2,1)S(1)}, f32[256,256]{1,0:T(8,128)S(1)}, bf16[768,512]{1,0:T(8,128)(2,1)S(1)}, bf16[768,512]{1,0:T(8,128)(2,1)S(1)...) custom-call(s32[2,5]{1,0:T(2,128)} %refs_0_.1, bf16[3,512]{1,0:T(4,128)(2,1)} %own_ref.1, s32[1,256]{1,0:T(1,128)} %refs_2_.1, ...), custom_call_target="tpu_custom_call" | custom-call | tf_op jit(solution)/shard_map/pallas_call | solution.py:361
  7.4 0.1 collective-permute-start.2
  7.5 1.3 %collective-permute-done.2.got_ref.refs_4_ = bf16[272,256]{1,0:T(8,128)(2,1)S(1)} collective-permute-done((bf16[272,256]{1,0:T(8,128)(2,1)S(1)}, bf16[272,256]{1,0:T(8,128)(2,1)S(1)}, u32[]{:S(2)}, u32[]{:S(2)}) %collective-permute-start.2) | collective-permute-done | bytes 139296 | tf_op jit(solution)/shard_map/ppermute | solution.py:325
  8.8 2.1 %collective-permute-start.3 = (bf16[96,256]{1,0:T(8,128)(2,1)S(1)}, bf16[96,256]{1,0:T(8,128)(2,1)S(1)}, u32[]{:S(2)}, u32[]{:S(2)}) collective-permute-start(bf16[96,256]{1,0:T(8,128)(2,1)S(1)} %get-tuple-element.38), channel_id=1, source_target_pairs={{2,0},{3,1},{0,2},{1,3},{6,4},{7,5},{4,6},{5,7},{10,8},{11,9},{8,1... | collective-permute-start | bytes 147464 | tf_op jit(solution)/shard_map/ppermute | solution.py:325
  10.9 2.6 %collective-permute-start.4 = (bf16[96,256]{1,0:T(8,128)(2,1)S(1)}, bf16[96,256]{1,0:T(8,128)(2,1)S(1)}, u32[]{:S(2)}, u32[]{:S(2)}) collective-permute-start(bf16[96,256]{1,0:T(8,128)(2,1)S(1)} %get-tuple-element.40), channel_id=1, source_target_pairs={{4,0},{5,1},{6,2},{7,3},{0,4},{1,5},{2,6},{3,7},{12,8},{13,9},{14,... | collective-permute-start | bytes 147464 | tf_op jit(solution)/shard_map/ppermute | solution.py:325
  13.5 0.0 collective-permute-start.5
  13.5 0.0 collective-permute-done.3.refs_0_.refs_1_
  13.5 0.0 collective-permute-done.1.first_ref.refs_3_
  13.5 1.7 %collective-permute-start.6 = (bf16[272,512]{1,0:T(8,128)(2,1)S(1)}, bf16[272,512]{1,0:T(8,128)(2,1)S(1)}, u32[]{:S(2)}, u32[]{:S(2)}) collective-permute-start(bf16[272,512]{1,0:T(8,128)(2,1)S(1)} %collective-permute-done.1.first_ref.refs_3_), channel_id=1, source_target_pairs={{16,0},{24,8},{0,16},{8,24},{17,1},{25,9},{1,17},{9,25},{18,2},{26... | collective-permute-start | bytes 835592 | tf_op jit(solution)/shard_map/ppermute | solution.py:325
  15.3 1.5 %collective-permute-done.4.refs_1_.refs_2_ = bf16[96,256]{1,0:T(8,128)(2,1)S(1)} collective-permute-done((bf16[96,256]{1,0:T(8,128)(2,1)S(1)}, bf16[96,256]{1,0:T(8,128)(2,1)S(1)}, u32[]{:S(2)}, u32[]{:S(2)}) %collective-permute-start.4) | collective-permute-done | bytes 49184 | tf_op jit(solution)/shard_map/ppermute | solution.py:325
  16.8 2.6 %collective-permute-done.5.refs_2_.refs_3_ = bf16[96,256]{1,0:T(8,128)(2,1)S(1)} collective-permute-done((bf16[96,256]{1,0:T(8,128)(2,1)S(1)}, bf16[96,256]{1,0:T(8,128)(2,1)S(1)}, u32[]{:S(2)}, u32[]{:S(2)}) %collective-permute-start.5) | collective-permute-done | bytes 49184 | tf_op jit(solution)/shard_map/ppermute | solution.py:325
  19.4 0.0 collective-permute-done.refs_4_
  19.4 1.5 %collective-permute-start.7 = (bf16[256,512]{1,0:T(8,128)(2,1)S(1)}, bf16[256,512]{1,0:T(8,128)(2,1)S(1)}, u32[]{:S(2)}, u32[]{:S(2)}) collective-permute-start(bf16[256,512]{1,0:T(8,128)(2,1)S(1)} %collective-permute-done.refs_4_), channel_id=1, source_target_pairs={{16,0},{24,8},{0,16},{8,24},{17,1},{25,9},{1,17},{9,25},{18,2},{26... | collective-permute-start | bytes 786440 | tf_op jit(solution)/shard_map/ppermute | solution.py:325
  20.9 0.1 collective-permute-start.8
  21.0 2.0 %collective-permute-start.9 = (bf16[64,256]{1,0:T(8,128)(2,1)S(1)}, bf16[64,256]{1,0:T(8,128)(2,1)S(1)}, u32[]{:S(2)}, u32[]{:S(2)}) collective-permute-start(bf16[64,256]{1,0:T(8,128)(2,1)S(1)} %shard_map.98.refs_0_), channel_id=1, source_target_pairs={{4,0},{5,1},{6,2},{7,3},{0,4},{1,5},{2,6},{3,7},{12,8},{13,9},{14,... | collective-permute-start | bytes 98312 | tf_op jit(solution)/shard_map/ppermute | solution.py:325
  23.1 2.3 %collective-permute-start.10 = (bf16[64,256]{1,0:T(8,128)(2,1)S(1)}, bf16[64,256]{1,0:T(8,128)(2,1)S(1)}, u32[]{:S(2)}, u32[]{:S(2)}) collective-permute-start(bf16[64,256]{1,0:T(8,128)(2,1)S(1)} %shard_map.98.refs_0_), channel_id=1, source_target_pairs={{6,0},{7,1},{4,2},{5,3},{2,4},{3,5},{0,6},{1,7},{14,8},{15,9},{12,... | collective-permute-start | bytes 98312 | tf_op jit(solution)/shard_map/ppermute | solution.py:325
  25.4 1.8 %shard_map.96 = (f32[16,256]{1,0:T(8,128)S(1)}, f32[256,512]{1,0:T(8,128)S(1)}) custom-call(bf16[96,256]{1,0:T(8,128)(2,1)S(1)} %collective-permute-done.3.refs_0_.refs_1_, bf16[96,256]{1,0:T(8,128)(2,1)S(1)} %collective-permute-done.4.refs_1_.refs_2_, bf16[96,256]{1,0:T(8,128)(2,1)S(1)} %collective-permute-done.5.refs_2_.refs_3_, ...), custom_call_target="tpu_custom_call" | custom-call | tf_op jit(solution)/shard_map/pallas_call | solution.py:22
  27.2 0.0 collective-permute-done.8.refs_1_
  27.2 0.0 collective-permute-done.9.refs_2_
  27.3 1.5 %collective-permute-done.10.refs_3_ = bf16[64,256]{1,0:T(8,128)(2,1)S(1)} collective-permute-done((bf16[64,256]{1,0:T(8,128)(2,1)S(1)}, bf16[64,256]{1,0:T(8,128)(2,1)S(1)}, u32[]{:S(2)}, u32[]{:S(2)}) %collective-permute-start.10) | collective-permute-done | bytes 32800 | tf_op jit(solution)/shard_map/ppermute | solution.py:325
  28.8 0.0 collective-permute-done.7.refs_6_
  28.8 0.0 collective-permute-done.6.second_ref.refs_5_
  28.8 0.4 shard_map.97
  29.2 0.4 shard_map.99
  29.6 0.0 copy-start
  29.7 0.1 collective-permute-start.11
  29.8 0.5 %collective-permute-start.15 = (bf16[256,256]{1,0:T(8,128)(2,1)S(1)}, bf16[256,256]{1,0:T(8,128)(2,1)S(1)}, u32[]{:S(2)}, u32[]{:S(2)}) collective-permute-start(bf16[256,256]{1,0:T(8,128)(2,1)S(1)} %shard_map.104.own_ref), channel_id=1, source_target_pairs={{1,0},{0,1},{3,2},{2,3},{5,4},{4,5},{7,6},{6,7},{9,8},{8,9},{11,10... | collective-permute-start | bytes 393224 | tf_op jit(solution)/shard_map/ppermute | solution.py:325
  30.3 0.8 %collective-permute-done.11.got_ref = bf16[256,256]{1,0:T(8,128)(2,1)S(1)} collective-permute-done((bf16[256,256]{1,0:T(8,128)(2,1)S(1)}, bf16[256,256]{1,0:T(8,128)(2,1)S(1)}, u32[]{:S(2)}, u32[]{:S(2)}) %collective-permute-start.11) | collective-permute-done | bytes 131104 | tf_op jit(solution)/shard_map/ppermute | solution.py:325
  31.1 0.0 copy-start.2
  31.1 0.1 collective-permute-start.12
  31.2 2.9 %collective-permute-start.13 = (bf16[256,256]{1,0:T(8,128)(2,1)S(1)}, bf16[256,256]{1,0:T(8,128)(2,1)S(1)}, u32[]{:S(2)}, u32[]{:S(2)}) collective-permute-start(bf16[256,256]{1,0:T(8,128)(2,1)S(1)} %shard_map.100.refs_0_), channel_id=1, source_target_pairs={{4,0},{5,1},{6,2},{7,3},{0,4},{1,5},{2,6},{3,7},{12,8},{13,9},{14,... | collective-permute-start | bytes 393224 | tf_op jit(solution)/shard_map/ppermute | solution.py:325
  34.1 1.5 %collective-permute-start.14 = (bf16[256,256]{1,0:T(8,128)(2,1)S(1)}, bf16[256,256]{1,0:T(8,128)(2,1)S(1)}, u32[]{:S(2)}, u32[]{:S(2)}) collective-permute-start(bf16[256,256]{1,0:T(8,128)(2,1)S(1)} %shard_map.100.refs_0_), channel_id=1, source_target_pairs={{6,0},{7,1},{4,2},{5,3},{2,4},{3,5},{0,6},{1,7},{14,8},{15,9},{12,... | collective-permute-start | bytes 393224 | tf_op jit(solution)/shard_map/ppermute | solution.py:325
  35.6 0.0 copy-done
  35.6 0.0 copy-done.2
  35.6 1.0 %shard_map.102 = (bf16[512,512]{1,0:T(8,128)(2,1)S(1)}, bf16[512,512]{1,0:T(8,128)(2,1)S(1)}, f32[512,512]{1,0:T(8,128)S(1)}) custom-call(f32[12,128]{1,0:T(8,128)S(1)} %get-tuple-element.49.table_ref, bf16[3,512]{1,0:T(4,128)(2,1)S(1)} %copy-done.2, bf16[272,512]{1,0:T(8,128)(2,1)S(1)} %collective-permute-done.1.first_ref.refs_3_, ...), custom_call_target="tpu_custom_call" | custom-call | tf_op jit(solution)/shard_map/pallas_call | solution.py:22
  36.5 1.5 %shard_map.103 = bf16[512,512]{1,0:T(8,128)(2,1)} custom-call(f32[512,512]{1,0:T(8,128)S(1)} %get-tuple-element.59.refs_0_, bf16[512,512]{1,0:T(8,128)(2,1)S(1)} %get-tuple-element.60.refs_1_, bf16[512,512]{1,0:T(8,128)(2,1)S(1)} %get-tuple-element.61.refs_2_, bf16[272,512]{1,0:T(8,128)(2,1)S(1)} %collective-permute-done.1.first_ref.refs_3_, ...), custom_call_target="tpu_custom_call" | custom-call | tf_op jit(solution)/shard_map/pallas_call | solution.py:22
  38.0 0.0 collective-permute-done.15.other_ref
  38.0 0.9 %shard_map.105 = f32[256,512]{1,0:T(8,128)} custom-call(bf16[256,256]{1,0:T(8,128)(2,1)S(1)} %shard_map.104.own_ref, bf16[256,256]{1,0:T(8,128)(2,1)S(1)} %collective-permute-done.15.other_ref), custom_call_target="tpu_custom_call" | custom-call | tf_op jit(solution)/shard_map/pallas_call | solution.py:22
  38.9 0.1 collective-permute-done.12.refs_1_
  39.0 5.2 %collective-permute-done.13.refs_2_ = bf16[256,256]{1,0:T(8,128)(2,1)S(1)} collective-permute-done((bf16[256,256]{1,0:T(8,128)(2,1)S(1)}, bf16[256,256]{1,0:T(8,128)(2,1)S(1)}, u32[]{:S(2)}, u32[]{:S(2)}) %collective-permute-start.13) | collective-permute-done | bytes 131104 | tf_op jit(solution)/shard_map/ppermute | solution.py:325
  44.2 0.0 collective-permute-done.14.refs_3_
  44.2 0.1 shard_map.101.own_ref
  44.2 0.1 collective-permute-start.16
  44.3 1.3 %collective-permute-done.16.other_ref = bf16[256,256]{1,0:T(8,128)(2,1)S(1)} collective-permute-done((bf16[256,256]{1,0:T(8,128)(2,1)S(1)}, bf16[256,256]{1,0:T(8,128)(2,1)S(1)}, u32[]{:S(2)}, u32[]{:S(2)}) %collective-permute-start.16) | collective-permute-done | bytes 131104 | tf_op jit(solution)/shard_map/ppermute | solution.py:325
  45.6 0.9 %shard_map.106 = f32[256,512]{1,0:T(8,128)} custom-call(bf16[256,256]{1,0:T(8,128)(2,1)S(1)} %shard_map.101.own_ref, bf16[256,256]{1,0:T(8,128)(2,1)S(1)} %collective-permute-done.16.other_ref), custom_call_target="tpu_custom_call" | custom-call | tf_op jit(solution)/shard_map/pallas_call | solution.py:22
  (5 shorter events, 0.1 us)
Async XLA Ops:
  0.6 1.1 %copy-start.1 = (bf16[3,512]{1,0:T(4,128)(2,1)S(1)}, bf16[3,512]{1,0:T(4,128)(2,1)}, u32[]{:S(2)}) copy-start(bf16[3,512]{1,0:T(4,128)(2,1)} %own_ref.1) | copy-start | bytes 9220
  1.8 11.8 %collective-permute-start.1 = (bf16[272,512]{1,0:T(8,128)(2,1)S(1)}, bf16[272,512]{1,0:T(8,128)(2,1)S(1)}, u32[]{:S(2)}, u32[]{:S(2)}) collective-permute-start(bf16[272,512]{1,0:T(8,128)(2,1)S(1)} %fusion.1), channel_id=1, source_target_pairs={{8,0},{0,8},{24,16},{16,24},{9,1},{1,9},{25,17},{17,25},{10,2},{2,... | collective-permute-start | bytes 835592 | tf_op jit(solution)/shard_map/ppermute | solution.py:325
  4.8 14.6 %collective-permute-start = (bf16[256,512]{1,0:T(8,128)(2,1)S(1)}, bf16[256,512]{1,0:T(8,128)(2,1)S(1)}, u32[]{:S(2)}, u32[]{:S(2)}) collective-permute-start(bf16[256,512]{1,0:T(8,128)(2,1)S(1)} %get-tuple-element.70), channel_id=1, source_target_pairs={{8,0},{0,8},{24,16},{16,24},{9,1},{1,9},{25,17},{17,25},{10,2},{2,... | collective-permute-start | bytes 786440 | tf_op jit(solution)/shard_map/ppermute | solution.py:325
  7.4 1.4 %collective-permute-start.2 = (bf16[272,256]{1,0:T(8,128)(2,1)S(1)}, bf16[272,256]{1,0:T(8,128)(2,1)S(1)}, u32[]{:S(2)}, u32[]{:S(2)}) collective-permute-start(bf16[272,256]{1,0:T(8,128)(2,1)S(1)} %get-tuple-element.37.sent_ref.refs_3_), channel_id=1, source_target_pairs={{1,0},{0,1},{3,2},{2,3},{5,4},{4,5},{7,6},{6,7},{9,8},{8,9},{11,10... | collective-permute-start | bytes 417800 | tf_op jit(solution)/shard_map/ppermute | solution.py:325
  8.8 4.7 %collective-permute-start.3 = (bf16[96,256]{1,0:T(8,128)(2,1)S(1)}, bf16[96,256]{1,0:T(8,128)(2,1)S(1)}, u32[]{:S(2)}, u32[]{:S(2)}) collective-permute-start(bf16[96,256]{1,0:T(8,128)(2,1)S(1)} %get-tuple-element.38), channel_id=1, source_target_pairs={{2,0},{3,1},{0,2},{1,3},{6,4},{7,5},{4,6},{5,7},{10,8},{11,9},{8,1... | collective-permute-start | bytes 147464 | tf_op jit(solution)/shard_map/ppermute | solution.py:325
  10.9 5.9 %collective-permute-start.4 = (bf16[96,256]{1,0:T(8,128)(2,1)S(1)}, bf16[96,256]{1,0:T(8,128)(2,1)S(1)}, u32[]{:S(2)}, u32[]{:S(2)}) collective-permute-start(bf16[96,256]{1,0:T(8,128)(2,1)S(1)} %get-tuple-element.40), channel_id=1, source_target_pairs={{4,0},{5,1},{6,2},{7,3},{0,4},{1,5},{2,6},{3,7},{12,8},{13,9},{14,... | collective-permute-start | bytes 147464 | tf_op jit(solution)/shard_map/ppermute | solution.py:325
  13.5 5.9 %collective-permute-start.5 = (bf16[96,256]{1,0:T(8,128)(2,1)S(1)}, bf16[96,256]{1,0:T(8,128)(2,1)S(1)}, u32[]{:S(2)}, u32[]{:S(2)}) collective-permute-start(bf16[96,256]{1,0:T(8,128)(2,1)S(1)} %get-tuple-element.41), channel_id=1, source_target_pairs={{6,0},{7,1},{4,2},{5,3},{2,4},{3,5},{0,6},{1,7},{14,8},{15,9},{12,... | collective-permute-start | bytes 147464 | tf_op jit(solution)/shard_map/ppermute | solution.py:325
  13.5 15.2 %collective-permute-start.6 = (bf16[272,512]{1,0:T(8,128)(2,1)S(1)}, bf16[272,512]{1,0:T(8,128)(2,1)S(1)}, u32[]{:S(2)}, u32[]{:S(2)}) collective-permute-start(bf16[272,512]{1,0:T(8,128)(2,1)S(1)} %collective-permute-done.1.first_ref.refs_3_), channel_id=1, source_target_pairs={{16,0},{24,8},{0,16},{8,24},{17,1},{25,9},{1,17},{9,25},{18,2},{26... | collective-permute-start | bytes 835592 | tf_op jit(solution)/shard_map/ppermute | solution.py:325
  19.4 9.4 %collective-permute-start.7 = (bf16[256,512]{1,0:T(8,128)(2,1)S(1)}, bf16[256,512]{1,0:T(8,128)(2,1)S(1)}, u32[]{:S(2)}, u32[]{:S(2)}) collective-permute-start(bf16[256,512]{1,0:T(8,128)(2,1)S(1)} %collective-permute-done.refs_4_), channel_id=1, source_target_pairs={{16,0},{24,8},{0,16},{8,24},{17,1},{25,9},{1,17},{9,25},{18,2},{26... | collective-permute-start | bytes 786440 | tf_op jit(solution)/shard_map/ppermute | solution.py:325
  20.9 6.3 %collective-permute-start.8 = (bf16[64,256]{1,0:T(8,128)(2,1)S(1)}, bf16[64,256]{1,0:T(8,128)(2,1)S(1)}, u32[]{:S(2)}, u32[]{:S(2)}) collective-permute-start(bf16[64,256]{1,0:T(8,128)(2,1)S(1)} %shard_map.98.refs_0_), channel_id=1, source_target_pairs={{2,0},{3,1},{0,2},{1,3},{6,4},{7,5},{4,6},{5,7},{10,8},{11,9},{8,1... | collective-permute-start | bytes 98312 | tf_op jit(solution)/shard_map/ppermute | solution.py:325
  21.0 6.2 %collective-permute-start.9 = (bf16[64,256]{1,0:T(8,128)(2,1)S(1)}, bf16[64,256]{1,0:T(8,128)(2,1)S(1)}, u32[]{:S(2)}, u32[]{:S(2)}) collective-permute-start(bf16[64,256]{1,0:T(8,128)(2,1)S(1)} %shard_map.98.refs_0_), channel_id=1, source_target_pairs={{4,0},{5,1},{6,2},{7,3},{0,4},{1,5},{2,6},{3,7},{12,8},{13,9},{14,... | collective-permute-start | bytes 98312 | tf_op jit(solution)/shard_map/ppermute | solution.py:325
  23.1 5.7 %collective-permute-start.10 = (bf16[64,256]{1,0:T(8,128)(2,1)S(1)}, bf16[64,256]{1,0:T(8,128)(2,1)S(1)}, u32[]{:S(2)}, u32[]{:S(2)}) collective-permute-start(bf16[64,256]{1,0:T(8,128)(2,1)S(1)} %shard_map.98.refs_0_), channel_id=1, source_target_pairs={{6,0},{7,1},{4,2},{5,3},{2,4},{3,5},{0,6},{1,7},{14,8},{15,9},{12,... | collective-permute-start | bytes 98312 | tf_op jit(solution)/shard_map/ppermute | solution.py:325
  29.6 5.9 %copy-start = (bf16[512,512]{1,0:T(8,128)(2,1)S(1)}, bf16[512,512]{1,0:T(8,128)(2,1)}, u32[]{:S(2)}) copy-start(bf16[512,512]{1,0:T(8,128)(2,1)} %matrix_ref.1) | copy-start | bytes 1572868
  29.7 1.4 %collective-permute-start.11 = (bf16[256,256]{1,0:T(8,128)(2,1)S(1)}, bf16[256,256]{1,0:T(8,128)(2,1)S(1)}, u32[]{:S(2)}, u32[]{:S(2)}) collective-permute-start(bf16[256,256]{1,0:T(8,128)(2,1)S(1)} %get-tuple-element.58), channel_id=1, source_target_pairs={{1,0},{0,1},{3,2},{2,3},{5,4},{4,5},{7,6},{6,7},{9,8},{8,9},{11,10... | collective-permute-start | bytes 393224 | tf_op jit(solution)/shard_map/ppermute | solution.py:325
  29.8 8.3 %collective-permute-start.15 = (bf16[256,256]{1,0:T(8,128)(2,1)S(1)}, bf16[256,256]{1,0:T(8,128)(2,1)S(1)}, u32[]{:S(2)}, u32[]{:S(2)}) collective-permute-start(bf16[256,256]{1,0:T(8,128)(2,1)S(1)} %shard_map.104.own_ref), channel_id=1, source_target_pairs={{1,0},{0,1},{3,2},{2,3},{5,4},{4,5},{7,6},{6,7},{9,8},{8,9},{11,10... | collective-permute-start | bytes 393224 | tf_op jit(solution)/shard_map/ppermute | solution.py:325
  31.1 4.5 %copy-start.2 = (bf16[3,512]{1,0:T(4,128)(2,1)S(1)}, bf16[3,512]{1,0:T(4,128)(2,1)}, u32[]{:S(2)}) copy-start(bf16[3,512]{1,0:T(4,128)(2,1)} %own_ref.1) | copy-start | bytes 9220
  31.1 7.9 %collective-permute-start.12 = (bf16[256,256]{1,0:T(8,128)(2,1)S(1)}, bf16[256,256]{1,0:T(8,128)(2,1)S(1)}, u32[]{:S(2)}, u32[]{:S(2)}) collective-permute-start(bf16[256,256]{1,0:T(8,128)(2,1)S(1)} %shard_map.100.refs_0_), channel_id=1, source_target_pairs={{2,0},{3,1},{0,2},{1,3},{6,4},{7,5},{4,6},{5,7},{10,8},{11,9},{8,1... | collective-permute-start | bytes 393224 | tf_op jit(solution)/shard_map/ppermute | solution.py:325
  31.2 13.0 %collective-permute-start.13 = (bf16[256,256]{1,0:T(8,128)(2,1)S(1)}, bf16[256,256]{1,0:T(8,128)(2,1)S(1)}, u32[]{:S(2)}, u32[]{:S(2)}) collective-permute-start(bf16[256,256]{1,0:T(8,128)(2,1)S(1)} %shard_map.100.refs_0_), channel_id=1, source_target_pairs={{4,0},{5,1},{6,2},{7,3},{0,4},{1,5},{2,6},{3,7},{12,8},{13,9},{14,... | collective-permute-start | bytes 393224 | tf_op jit(solution)/shard_map/ppermute | solution.py:325
  34.1 10.1 %collective-permute-start.14 = (bf16[256,256]{1,0:T(8,128)(2,1)S(1)}, bf16[256,256]{1,0:T(8,128)(2,1)S(1)}, u32[]{:S(2)}, u32[]{:S(2)}) collective-permute-start(bf16[256,256]{1,0:T(8,128)(2,1)S(1)} %shard_map.100.refs_0_), channel_id=1, source_target_pairs={{6,0},{7,1},{4,2},{5,3},{2,4},{3,5},{0,6},{1,7},{14,8},{15,9},{12,... | collective-permute-start | bytes 393224 | tf_op jit(solution)/shard_map/ppermute | solution.py:325
  44.2 1.4 %collective-permute-start.16 = (bf16[256,256]{1,0:T(8,128)(2,1)S(1)}, bf16[256,256]{1,0:T(8,128)(2,1)S(1)}, u32[]{:S(2)}, u32[]{:S(2)}) collective-permute-start(bf16[256,256]{1,0:T(8,128)(2,1)S(1)} %shard_map.101.own_ref), channel_id=1, source_target_pairs={{1,0},{0,1},{3,2},{2,3},{5,4},{4,5},{7,6},{6,7},{9,8},{8,9},{11,10... | collective-permute-start | bytes 393224 | tf_op jit(solution)/shard_map/ppermute | solution.py:325

commit v4 on v3

--- a/solution.py
+++ b/solution.py
@@ -85,23 +85,38 @@
     return (value >> place) & 1
 
 
-def describe_body(*refs):
-    sources, outs, held, sems = refs[:7], refs[7:13], refs[13:20], refs[20]
-    given_ref, kept_ref, hi_ref, lo_ref, top_pivots_ref, table_ref = outs
-    lists_ref, points_ref, pivots_ref, merges_ref, proj_ref, matrix_ref, merge_ref = held
+def load_body(*refs):
+    points_hbm, matrix_hbm, merge_hbm, *others = refs[:7]
+    first_ref, second_ref, merge_ref, *other_refs = refs[7:14]
+    points_ref, sems = refs[14:]
+    position = lax.axis_index("leaf")
     levels, rank = merge_ref.shape[:2]
-    position = lax.axis_index("leaf")
-    copies = [
-        pltpu.make_async_copy(a, b, sems.at[k]) for k, (a, b) in enumerate(zip(sources[:6], held[:6]))
+    rows = second_ref.shape[0]
+    pairs = [
+        (points_hbm, points_ref),
+        (matrix_hbm.at[pl.ds(0, rows), :], first_ref.at[pl.ds(HEIGHT, rows), :]),
+        (matrix_hbm.at[pl.ds(rows, rows), :], second_ref),
+        *zip(others, other_refs),
     ]
     for level in range(levels):
         start = pl.multiple_of(bit_of(position, level) * rank, rank)
-        source = sources[6].at[level, 0, pl.ds(start, rank), :]
-        copies.append(pltpu.make_async_copy(source, merge_ref.at[level], sems.at[6 + level]))
+        pairs.append((merge_hbm.at[level, 0, pl.ds(start, rank), :], merge_ref.at[level]))
+    copies = [pltpu.make_async_copy(a, b, sems.at[k]) for k, (a, b) in enumerate(pairs)]
     for copy in copies:
         copy.start()
-    for copy in copies[:4]:
+    copies[0].wait()
+    held = points_ref[...]
+    blank = jnp.zeros((HEIGHT - held.shape[0], held.shape[1]), BF16)
+    first_ref[0:HEIGHT, :] = jnp.concatenate([held, blank], axis=0)
+    for copy in copies[1:]:
         copy.wait()
+
+
+def describe_body(*refs):
+    first_ref, second_ref, merge_ref, lists_ref, pivots_ref, merges_ref, proj_ref = refs[:7]
+    given_ref, kept_ref, hi_ref, lo_ref, top_pivots_ref, table_ref = refs[7:]
+    levels, rank = merge_ref.shape[:2]
+    position = lax.axis_index("leaf")
     lists = lists_ref[...]
     blocks = lists.shape[0]
     for c in range(3 * blocks):
@@ -110,7 +125,7 @@
             row = c * blocks + i
             table_ref[row : row + 1, :] = jnp.broadcast_to(FAR_OFF * (1.0 - listed[i : i + 1]), (1, LANES))
     top_pivots_ref[...] = merges_ref[merges_ref.shape[0] - 1]
-    p = points_ref[...].astype(F32)
+    p = first_ref[0:3, :].astype(F32)
     width = p.shape[1]
     spot = lane_index(width)
     attributes = rows_of(
@@ -123,9 +138,8 @@
         skeleton = jnp.where(row == PIVOT + 2 * level, (q // rank).astype(F32), skeleton)
         skeleton = jnp.where(row == PIVOT + 2 * level + 1, (q % rank).astype(F32), skeleton)
     given_ref[0:HEIGHT, :] = skeleton.astype(BF16)
-    for copy in copies[4:]:
-        copy.wait()
-    c = dot(proj_ref[...], matrix_ref[...], 0)
+    rows = second_ref.shape[0]
+    c = dot(proj_ref[0:rows, :], first_ref[HEIGHT:, :], 0) + dot(proj_ref[rows:, :], second_ref[...], 0)
     for level in range(levels):
         hi, lo = halves(c)
         hi_ref[pl.ds(level * rank, rank), :] = hi
@@ -247,10 +261,10 @@
     return [2 * blocks * (1 - odd), 2 * blocks * odd]
 
 
-def near_body(near_amp, even_ahead, table_ref, own_ref, first_ref, second_ref, matrix_ref, *outs):
+def near_body(near_amp, even_ahead, table_ref, first_ref, second_ref, own_ref, own_late_ref, *outs):
     near_first, near_second, own_terms = outs
     blocks = block_count_of(table_ref)
-    own = own_ref[...].astype(F32)
+    own = own_ref[0:3, :].astype(F32)
     width = own.shape[1]
     spot = lane_index(width) // (width // blocks)
     marks = block_marks(width, blocks)
@@ -263,7 +277,8 @@
     bases = bases_of(even_ahead, blocks)
     near_first[...] = near(bases[0], first_ref[0:3, :].astype(F32))
     near_second[...] = near(bases[1], second_ref[0:3, :].astype(F32))
-    own_terms[...] = dot(near(blocks, own), matrix_ref[...])
+    near_own, rows = near(blocks, own), own_late_ref.shape[0]
+    own_terms[...] = dot(near_own[:, :rows], own_ref[HEIGHT:, :]) + dot(near_own[:, rows:], own_late_ref[...])
 
 
 def near_product(start_ref, first_ref, second_ref, *chunks):
@@ -348,32 +363,33 @@
         routes = [lambda i: step(i, 1), lambda i: step(i, -1), lambda i: step(i, -2)]
     else:
         routes = [lambda i: (i - 1) % count, lambda i: (i + 1) % count]
-    header = jnp.pad(points, ((0, HEIGHT - points.shape[0]), (0, 0)))
-    unit = row_count // 8
-    edges = [0, 4 * unit, 8 * unit]
-    chunks = [test_matrix[a:b] for a, b in zip(edges[:-1], edges[1:])]
-    chunks[HEADED] = jnp.concatenate([header, chunks[HEADED]], axis=0)
-    first = [permuted(c, "blk", routes[0]) for c in chunks]
-    onward = list(first if paired else chunks)
-
-    inputs = [near_lists, points, leaf_pivots, merge_pivots, leaf_proj, test_matrix, merge_proj]
-    held = [(x.shape, x.dtype) for x in inputs[:6]] + [((level_count, skel_rank, skel_rank), BF16)]
-    given, kept, hi, lo, top_pivots, table = pl.pallas_call(
-        describe_body,
+    half = row_count // 2
+    inputs = [points, test_matrix, merge_proj, near_lists, leaf_pivots, merge_pivots, leaf_proj]
+    loaded = pl.pallas_call(
+        load_body,
         out_shape=[
-            jax.ShapeDtypeStruct((HEIGHT + skel_rank, middle), BF16),
-            jax.ShapeDtypeStruct((skel_rank, middle), F32),
-            jax.ShapeDtypeStruct((level_count * skel_rank, sample_count), BF16),
-            jax.ShapeDtypeStruct((level_count * skel_rank, sample_count), BF16),
-            jax.ShapeDtypeStruct((1, skel_rank), jnp.int32),
-            jax.ShapeDtypeStruct((3 * block_count * block_count, LANES), F32),
-        ],
+            jax.ShapeDtypeStruct((HEIGHT + half, sample_count), BF16),
+            jax.ShapeDtypeStruct((half, sample_count), BF16),
+            jax.ShapeDtypeStruct((level_count, skel_rank, skel_rank), BF16),
+        ]
+        + [jax.ShapeDtypeStruct(x.shape, x.dtype) for x in inputs[3:]],
         in_specs=[pl.BlockSpec(memory_space=pltpu.HBM)] * 7,
-        out_specs=[pl.BlockSpec(memory_space=pltpu.VMEM)] * 6,
-        scratch_shapes=[pltpu.VMEM(*h) for h in held] + [pltpu.SemaphoreType.DMA((6 + level_count,))],
+        out_specs=[pl.BlockSpec(memory_space=pltpu.VMEM)] * 7,
+        scratch_shapes=[pltpu.VMEM(points.shape, BF16), pltpu.SemaphoreType.DMA((7 + level_count,))],
         compiler_params=pltpu.CompilerParams(vmem_limit_bytes=40 << 20),
         cost_estimate=pl.CostEstimate(flops=0, bytes_accessed=0, transcendentals=0),
     )(*[pltpu.with_memory_space_constraint(x, pltpu.HBM) for x in inputs])
+    chunks = loaded[:2]
+    first = [permuted(c, "blk", routes[0]) for c in chunks]
+    onward = list(first if paired else chunks)
+
+    given, kept, hi, lo, top_pivots, table = call(
+        describe_body,
+        [((HEIGHT + skel_rank, middle), BF16), ((skel_rank, middle), F32)]
+        + [((level_count * skel_rank, sample_count), BF16)] * 2
+        + [((1, skel_rank), jnp.int32), ((3 * block_count * block_count, LANES), F32)],
+        *loaded,
+    )
     got = swapped(given, 1)
     mine, *messages = call(
         scatter_body,
@@ -388,7 +404,7 @@
     onward[1], messages = lax.optimization_barrier((onward[1], messages))
     second += [permuted(c, "blk", routes[-1]) for c in onward[1:]]
     (omega_piece,) = call(piece_body, [((piece, middle), BF16)], mine, *messages)
-    omega_pieces = [omega_piece] + [swapped(omega_piece, 2 * k) for k in range(1, chips)]
+    omega_pieces = [omega_piece] + [swapped(omega_piece, 2 * k) for k in range(chips - 1, 0, -1)][::-1]
     top, far_part = call(
         functools.partial(tree_body, far_amp),
         [((HEIGHT, skel_rank), F32), ((skel_rank, sample_count), F32)],
@@ -403,10 +419,9 @@
         functools.partial(near_body, near_amp, paired),
         [((row_count, row_count), BF16)] * 2 + [((row_count, sample_count), F32)],
         table,
-        points,
         first[HEADED],
         second[HEADED],
-        test_matrix,
+        *chunks,
     )
     top_first, top_second = call(
         functools.partial(top_near_body, near_amp, paired),
@@ -416,7 +431,8 @@
         first[HEADED],
         second[HEADED],
     )
-    second[-1], omega_pieces = lax.optimization_barrier((second[-1], omega_pieces))
+    second[-1], omega_pieces = lax.optimization_barrier((second[-1], omega_pieces[::-1]))
+    omega_pieces = omega_pieces[::-1]
     kept, given = call(
         share_body,
         [((skel_rank, middle), F32), ((skel_rank, middle), BF16)],

time: 46.7 us -> 46 us (0.985)
  local copies, waits for them, and re-layouts: 1.09 us -> 0 us
    pallas_call x12 -> x13, Pallas kernels: 7.03 us -> 8.2 us  [call(): pl.pallas_call(body, out_shape=[jax.ShapeDtypeStruct(s, d) for s, d in ou...]
    pallas_call x1, Pallas kernels: 2.53 us -> 1.37 us  [on_device(): pl.pallas_call(load_body, out_shape=[jax.ShapeDtypeStruct((HEIGHT + half,...]
    slice x1 -> x0, local copies, waits for them, and re-layouts: 1.07 us -> none  [on_device(): chunks = [test_matrix[a:b] for a, b in zip(edges[:-1], edges[1:])]]
  transfers between devices with their start and end apart: 17 -> 17, of which waited for: 8 -> 9; matrix products, arithmetic and copies ran while one was open for 0% -> 0% of each run, Pallas kernels for 17% -> 14%
where the time goes in v4:
time: 46 us; the launch traced here: 45.9 us
  starting transfers between devices  21 us (46%)
  waiting for transfers between devices  14.5 us (32%)
  Pallas kernels  9.57 us (21%)
  between operations  0.75 us (2%)
    ppermute x17, starting transfers between devices, permuted(): lax.ppermute(block, axis, [(route(i), i) for i in range(lax.axis_size(axi...  21 us
    ppermute x17, waiting for transfers between devices, permuted(): lax.ppermute(block, axis, [(route(i), i) for i in range(lax.axis_size(axi...  14.5 us
    pallas_call x13, Pallas kernels, call(): pl.pallas_call(body, out_shape=[jax.ShapeDtypeStruct(s, d) for s, d in ou...  8.2 us
    pallas_call x1, Pallas kernels, on_device(): pl.pallas_call(load_body, out_shape=[jax.ShapeDtypeStruct((HEIGHT + half,...  1.37 us
  transfers between devices with their start and end apart: 17, of which 9 were waited for; matrix products, arithmetic and copies ran while one was open for 0% of the time, Pallas kernels for 14%

profile of v4, /device:TPU:0, one launch (start us, length us, event | category | flops | bytes accessed | tf_op | source)
XLA Modules:
  0.0 45.9 jit_solution(5413508233418232029)
XLA Ops:
  0.6 1.4 %shard_map.94 = (bf16[272,512]{1,0:T(8,128)(2,1)S(1)}, bf16[256,512]{1,0:T(8,128)(2,1)S(1)}, bf16[3,256,256]{2,1,0:T(8,128)(2,1)S(1)}, s32[2,5]{1,0:T(2,128)S(1)...) custom-call(bf16[3,512]{1,0:T(4,128)(2,1)} %refs_0_.1, bf16[512,512]{1,0:T(8,128)(2,1)} %refs_1_.1, ...), custom_call_target="tpu_custom_call" | custom-call | tf_op jit(solution)/shard_map/pallas_call | solution.py:368
  2.0 3.0 %collective-permute-start.1 = (bf16[272,512]{1,0:T(8,128)(2,1)S(1)}, bf16[272,512]{1,0:T(8,128)(2,1)S(1)}, u32[]{:S(2)}, u32[]{:S(2)}) collective-permute-start(bf16[272,512]{1,0:T(8,128)(2,1)S(1)} %get-tuple-element.44.refs_0_.own_ref), channel_id=1, source_target_pairs={{8,0},{0,8},{24,16},{16,24},{9,1},{1,9},{25,17},{17,25},{10,2},{2,... | collective-permute-start | bytes 835592 | tf_op jit(solution)/shard_map/ppermute | solution.py:340
  5.0 0.1 collective-permute-start
  5.1 1.2 %shard_map.95 = (bf16[272,256]{1,0:T(8,128)(2,1)S(1)}, f32[256,256]{1,0:T(8,128)S(1)}, bf16[768,512]{1,0:T(8,128)(2,1)S(1)}, bf16[768,512]{1,0:T(8,128)(2,1)S(1)...) custom-call(bf16[272,512]{1,0:T(8,128)(2,1)S(1)} %get-tuple-element.44.refs_0_.own_ref, ...), custom_call_target="tpu_custom_call" | custom-call | tf_op jit(solution)/shard_map/pallas_call | solution.py:22
  6.3 0.1 collective-permute-start.2
  6.4 1.3 %collective-permute-done.2.got_ref.refs_4_ = bf16[272,256]{1,0:T(8,128)(2,1)S(1)} collective-permute-done((bf16[272,256]{1,0:T(8,128)(2,1)S(1)}, bf16[272,256]{1,0:T(8,128)(2,1)S(1)}, u32[]{:S(2)}, u32[]{:S(2)}) %collective-permute-start.2) | collective-permute-done | bytes 139296 | tf_op jit(solution)/shard_map/ppermute | solution.py:340
  7.7 2.1 %collective-permute-start.3 = (bf16[96,256]{1,0:T(8,128)(2,1)S(1)}, bf16[96,256]{1,0:T(8,128)(2,1)S(1)}, u32[]{:S(2)}, u32[]{:S(2)}) collective-permute-start(bf16[96,256]{1,0:T(8,128)(2,1)S(1)} %get-tuple-element.52), channel_id=1, source_target_pairs={{2,0},{3,1},{0,2},{1,3},{6,4},{7,5},{4,6},{5,7},{10,8},{11,9},{8,1... | collective-permute-start | bytes 147464 | tf_op jit(solution)/shard_map/ppermute | solution.py:340
  9.8 2.6 %collective-permute-start.4 = (bf16[96,256]{1,0:T(8,128)(2,1)S(1)}, bf16[96,256]{1,0:T(8,128)(2,1)S(1)}, u32[]{:S(2)}, u32[]{:S(2)}) collective-permute-start(bf16[96,256]{1,0:T(8,128)(2,1)S(1)} %get-tuple-element.54), channel_id=1, source_target_pairs={{4,0},{5,1},{6,2},{7,3},{0,4},{1,5},{2,6},{3,7},{12,8},{13,9},{14,... | collective-permute-start | bytes 147464 | tf_op jit(solution)/shard_map/ppermute | solution.py:340
  12.4 0.0 collective-permute-start.5
  12.4 0.0 collective-permute-done.3.refs_0_.refs_1_
  12.4 0.1 collective-permute-done.1.first_ref.refs_3_
  12.5 2.1 %collective-permute-start.6 = (bf16[272,512]{1,0:T(8,128)(2,1)S(1)}, bf16[272,512]{1,0:T(8,128)(2,1)S(1)}, u32[]{:S(2)}, u32[]{:S(2)}) collective-permute-start(bf16[272,512]{1,0:T(8,128)(2,1)S(1)} %collective-permute-done.1.first_ref.refs_3_), channel_id=1, source_target_pairs={{16,0},{24,8},{0,16},{8,24},{17,1},{25,9},{1,17},{9,25},{18,2},{26... | collective-permute-start | bytes 835592 | tf_op jit(solution)/shard_map/ppermute | solution.py:340
  14.6 1.1 %collective-permute-done.4.refs_1_.refs_2_ = bf16[96,256]{1,0:T(8,128)(2,1)S(1)} collective-permute-done((bf16[96,256]{1,0:T(8,128)(2,1)S(1)}, bf16[96,256]{1,0:T(8,128)(2,1)S(1)}, u32[]{:S(2)}, u32[]{:S(2)}) %collective-permute-start.4) | collective-permute-done | bytes 49184 | tf_op jit(solution)/shard_map/ppermute | solution.py:340
  15.7 2.6 %collective-permute-done.5.refs_2_.refs_3_ = bf16[96,256]{1,0:T(8,128)(2,1)S(1)} collective-permute-done((bf16[96,256]{1,0:T(8,128)(2,1)S(1)}, bf16[96,256]{1,0:T(8,128)(2,1)S(1)}, u32[]{:S(2)}, u32[]{:S(2)}) %collective-permute-start.5) | collective-permute-done | bytes 49184 | tf_op jit(solution)/shard_map/ppermute | solution.py:340
  18.3 0.0 collective-permute-done.refs_4_
  18.3 1.5 %collective-permute-start.7 = (bf16[256,512]{1,0:T(8,128)(2,1)S(1)}, bf16[256,512]{1,0:T(8,128)(2,1)S(1)}, u32[]{:S(2)}, u32[]{:S(2)}) collective-permute-start(bf16[256,512]{1,0:T(8,128)(2,1)S(1)} %collective-permute-done.refs_4_), channel_id=1, source_target_pairs={{16,0},{24,8},{0,16},{8,24},{17,1},{25,9},{1,17},{9,25},{18,2},{26... | collective-permute-start | bytes 786440 | tf_op jit(solution)/shard_map/ppermute | solution.py:340
  19.9 2.9 %collective-permute-start.8 = (bf16[64,256]{1,0:T(8,128)(2,1)S(1)}, bf16[64,256]{1,0:T(8,128)(2,1)S(1)}, u32[]{:S(2)}, u32[]{:S(2)}) collective-permute-start(bf16[64,256]{1,0:T(8,128)(2,1)S(1)} %shard_map.99.refs_0_), channel_id=1, source_target_pairs={{6,0},{7,1},{4,2},{5,3},{2,4},{3,5},{0,6},{1,7},{14,8},{15,9},{12,... | collective-permute-start | bytes 98312 | tf_op jit(solution)/shard_map/ppermute | solution.py:340
  22.7 0.0 collective-permute-start.9
  22.8 1.6 %collective-permute-start.10 = (bf16[64,256]{1,0:T(8,128)(2,1)S(1)}, bf16[64,256]{1,0:T(8,128)(2,1)S(1)}, u32[]{:S(2)}, u32[]{:S(2)}) collective-permute-start(bf16[64,256]{1,0:T(8,128)(2,1)S(1)} %shard_map.99.refs_0_), channel_id=1, source_target_pairs={{2,0},{3,1},{0,2},{1,3},{6,4},{7,5},{4,6},{5,7},{10,8},{11,9},{8,1... | collective-permute-start | bytes 98312 | tf_op jit(solution)/shard_map/ppermute | solution.py:340
  24.3 1.8 %shard_map.97 = (f32[16,256]{1,0:T(8,128)S(1)}, f32[256,512]{1,0:T(8,128)S(1)}) custom-call(bf16[96,256]{1,0:T(8,128)(2,1)S(1)} %collective-permute-done.3.refs_0_.refs_1_, bf16[96,256]{1,0:T(8,128)(2,1)S(1)} %collective-permute-done.4.refs_1_.refs_2_, bf16[96,256]{1,0:T(8,128)(2,1)S(1)} %collective-permute-done.5.refs_2_.refs_3_, ...), custom_call_target="tpu_custom_call" | custom-call | tf_op jit(solution)/shard_map/pallas_call | solution.py:22
  26.1 0.0 collective-permute-done.8.refs_3_
  26.1 1.4 %collective-permute-done.9.refs_2_ = bf16[64,256]{1,0:T(8,128)(2,1)S(1)} collective-permute-done((bf16[64,256]{1,0:T(8,128)(2,1)S(1)}, bf16[64,256]{1,0:T(8,128)(2,1)S(1)}, u32[]{:S(2)}, u32[]{:S(2)}) %collective-permute-start.9) | collective-permute-done | bytes 32800 | tf_op jit(solution)/shard_map/ppermute | solution.py:340
  27.6 0.0 collective-permute-done.10.refs_1_
  27.6 0.0 collective-permute-done.7.refs_6_
  27.6 0.0 collective-permute-done.6.second_ref.refs_5_
  27.6 0.4 shard_map.98
  28.0 0.4 shard_map.100
  28.4 0.1 collective-permute-start.11
  28.6 0.5 %collective-permute-start.15 = (bf16[256,256]{1,0:T(8,128)(2,1)S(1)}, bf16[256,256]{1,0:T(8,128)(2,1)S(1)}, u32[]{:S(2)}, u32[]{:S(2)}) collective-permute-start(bf16[256,256]{1,0:T(8,128)(2,1)S(1)} %shard_map.105.own_ref), channel_id=1, source_target_pairs={{1,0},{0,1},{3,2},{2,3},{5,4},{4,5},{7,6},{6,7},{9,8},{8,9},{11,10... | collective-permute-start | bytes 393224 | tf_op jit(solution)/shard_map/ppermute | solution.py:340
  29.1 0.8 %collective-permute-done.11.got_ref = bf16[256,256]{1,0:T(8,128)(2,1)S(1)} collective-permute-done((bf16[256,256]{1,0:T(8,128)(2,1)S(1)}, bf16[256,256]{1,0:T(8,128)(2,1)S(1)}, u32[]{:S(2)}, u32[]{:S(2)}) %collective-permute-start.11) | collective-permute-done | bytes 131104 | tf_op jit(solution)/shard_map/ppermute | solution.py:340
  29.9 0.7 %collective-permute-start.12 = (bf16[256,256]{1,0:T(8,128)(2,1)S(1)}, bf16[256,256]{1,0:T(8,128)(2,1)S(1)}, u32[]{:S(2)}, u32[]{:S(2)}) collective-permute-start(bf16[256,256]{1,0:T(8,128)(2,1)S(1)} %shard_map.101.refs_0_), channel_id=1, source_target_pairs={{2,0},{3,1},{0,2},{1,3},{6,4},{7,5},{4,6},{5,7},{10,8},{11,9},{8,1... | collective-permute-start | bytes 393224 | tf_op jit(solution)/shard_map/ppermute | solution.py:340
  30.6 2.1 %collective-permute-start.13 = (bf16[256,256]{1,0:T(8,128)(2,1)S(1)}, bf16[256,256]{1,0:T(8,128)(2,1)S(1)}, u32[]{:S(2)}, u32[]{:S(2)}) collective-permute-start(bf16[256,256]{1,0:T(8,128)(2,1)S(1)} %shard_map.101.refs_0_), channel_id=1, source_target_pairs={{4,0},{5,1},{6,2},{7,3},{0,4},{1,5},{2,6},{3,7},{12,8},{13,9},{14,... | collective-permute-start | bytes 393224 | tf_op jit(solution)/shard_map/ppermute | solution.py:340
  32.7 1.7 %collective-permute-start.14 = (bf16[256,256]{1,0:T(8,128)(2,1)S(1)}, bf16[256,256]{1,0:T(8,128)(2,1)S(1)}, u32[]{:S(2)}, u32[]{:S(2)}) collective-permute-start(bf16[256,256]{1,0:T(8,128)(2,1)S(1)} %shard_map.101.refs_0_), channel_id=1, source_target_pairs={{6,0},{7,1},{4,2},{5,3},{2,4},{3,5},{0,6},{1,7},{14,8},{15,9},{12,... | collective-permute-start | bytes 393224 | tf_op jit(solution)/shard_map/ppermute | solution.py:340
  34.3 1.0 %shard_map.103 = (bf16[512,512]{1,0:T(8,128)(2,1)S(1)}, bf16[512,512]{1,0:T(8,128)(2,1)S(1)}, f32[512,512]{1,0:T(8,128)S(1)}) custom-call(f32[12,128]{1,0:T(8,128)S(1)} %get-tuple-element.63.table_ref, bf16[272,512]{1,0:T(8,128)(2,1)S(1)} %collective-permute-done.1.first_ref.refs_3_, bf16[272,512]{1,0:T(8,128)(2,1)S(1)} %collective-permute-done.6.second_ref.refs_5_, ...), custom_call_target="tpu_custom_call" | custom-call | tf_op jit(solution)/shard_map/pallas_call | solution.py:22
  35.3 1.5 %shard_map.104 = bf16[512,512]{1,0:T(8,128)(2,1)} custom-call(f32[512,512]{1,0:T(8,128)S(1)} %get-tuple-element.73.refs_0_, bf16[512,512]{1,0:T(8,128)(2,1)S(1)} %get-tuple-element.74.refs_1_, bf16[512,512]{1,0:T(8,128)(2,1)S(1)} %get-tuple-element.75.refs_2_, bf16[272,512]{1,0:T(8,128)(2,1)S(1)} %collective-permute-done.1.first_ref.refs_3_, ...), custom_call_target="tpu_custom_call" | custom-call | tf_op jit(solution)/shard_map/pallas_call | solution.py:22
  36.8 0.0 collective-permute-done.15.other_ref
  36.8 0.9 %shard_map.106 = f32[256,512]{1,0:T(8,128)} custom-call(bf16[256,256]{1,0:T(8,128)(2,1)S(1)} %shard_map.105.own_ref, bf16[256,256]{1,0:T(8,128)(2,1)S(1)} %collective-permute-done.15.other_ref), custom_call_target="tpu_custom_call" | custom-call | tf_op jit(solution)/shard_map/pallas_call | solution.py:22
  37.7 0.2 collective-permute-done.12.refs_1_
  37.9 5.6 %collective-permute-done.13.refs_2_ = bf16[256,256]{1,0:T(8,128)(2,1)S(1)} collective-permute-done((bf16[256,256]{1,0:T(8,128)(2,1)S(1)}, bf16[256,256]{1,0:T(8,128)(2,1)S(1)}, u32[]{:S(2)}, u32[]{:S(2)}) %collective-permute-start.13) | collective-permute-done | bytes 131104 | tf_op jit(solution)/shard_map/ppermute | solution.py:340
  43.5 0.0 collective-permute-done.14.refs_3_
  43.5 0.1 shard_map.102.own_ref
  43.6 0.1 collective-permute-start.16
  43.7 1.3 %collective-permute-done.16.other_ref = bf16[256,256]{1,0:T(8,128)(2,1)S(1)} collective-permute-done((bf16[256,256]{1,0:T(8,128)(2,1)S(1)}, bf16[256,256]{1,0:T(8,128)(2,1)S(1)}, u32[]{:S(2)}, u32[]{:S(2)}) %collective-permute-start.16) | collective-permute-done | bytes 131104 | tf_op jit(solution)/shard_map/ppermute | solution.py:340
  45.0 0.9 %shard_map.107 = f32[256,512]{1,0:T(8,128)} custom-call(bf16[256,256]{1,0:T(8,128)(2,1)S(1)} %shard_map.102.own_ref, bf16[256,256]{1,0:T(8,128)(2,1)S(1)} %collective-permute-done.16.other_ref), custom_call_target="tpu_custom_call" | custom-call | tf_op jit(solution)/shard_map/pallas_call | solution.py:22
  (4 shorter events, 0.1 us)
Async XLA Ops:
  2.0 10.5 %collective-permute-start.1 = (bf16[272,512]{1,0:T(8,128)(2,1)S(1)}, bf16[272,512]{1,0:T(8,128)(2,1)S(1)}, u32[]{:S(2)}, u32[]{:S(2)}) collective-permute-start(bf16[272,512]{1,0:T(8,128)(2,1)S(1)} %get-tuple-element.44.refs_0_.own_ref), channel_id=1, source_target_pairs={{8,0},{0,8},{24,16},{16,24},{9,1},{1,9},{25,17},{17,25},{10,2},{2,... | collective-permute-start | bytes 835592 | tf_op jit(solution)/shard_map/ppermute | solution.py:340
  5.0 13.3 %collective-permute-start = (bf16[256,512]{1,0:T(8,128)(2,1)S(1)}, bf16[256,512]{1,0:T(8,128)(2,1)S(1)}, u32[]{:S(2)}, u32[]{:S(2)}) collective-permute-start(bf16[256,512]{1,0:T(8,128)(2,1)S(1)} %get-tuple-element.43.refs_1_.own_late_ref), channel_id=1, source_target_pairs={{8,0},{0,8},{24,16},{16,24},{9,1},{1,9},{25,17},{17,25},{10,2},{2,... | collective-permute-start | bytes 786440 | tf_op jit(solution)/shard_map/ppermute | solution.py:340
  6.3 1.4 %collective-permute-start.2 = (bf16[272,256]{1,0:T(8,128)(2,1)S(1)}, bf16[272,256]{1,0:T(8,128)(2,1)S(1)}, u32[]{:S(2)}, u32[]{:S(2)}) collective-permute-start(bf16[272,256]{1,0:T(8,128)(2,1)S(1)} %get-tuple-element.51.sent_ref.refs_3_), channel_id=1, source_target_pairs={{1,0},{0,1},{3,2},{2,3},{5,4},{4,5},{7,6},{6,7},{9,8},{8,9},{11,10... | collective-permute-start | bytes 417800 | tf_op jit(solution)/shard_map/ppermute | solution.py:340
  7.7 4.7 %collective-permute-start.3 = (bf16[96,256]{1,0:T(8,128)(2,1)S(1)}, bf16[96,256]{1,0:T(8,128)(2,1)S(1)}, u32[]{:S(2)}, u32[]{:S(2)}) collective-permute-start(bf16[96,256]{1,0:T(8,128)(2,1)S(1)} %get-tuple-element.52), channel_id=1, source_target_pairs={{2,0},{3,1},{0,2},{1,3},{6,4},{7,5},{4,6},{5,7},{10,8},{11,9},{8,1... | collective-permute-start | bytes 147464 | tf_op jit(solution)/shard_map/ppermute | solution.py:340
  9.8 5.9 %collective-permute-start.4 = (bf16[96,256]{1,0:T(8,128)(2,1)S(1)}, bf16[96,256]{1,0:T(8,128)(2,1)S(1)}, u32[]{:S(2)}, u32[]{:S(2)}) collective-permute-start(bf16[96,256]{1,0:T(8,128)(2,1)S(1)} %get-tuple-element.54), channel_id=1, source_target_pairs={{4,0},{5,1},{6,2},{7,3},{0,4},{1,5},{2,6},{3,7},{12,8},{13,9},{14,... | collective-permute-start | bytes 147464 | tf_op jit(solution)/shard_map/ppermute | solution.py:340
  12.4 5.9 %collective-permute-start.5 = (bf16[96,256]{1,0:T(8,128)(2,1)S(1)}, bf16[96,256]{1,0:T(8,128)(2,1)S(1)}, u32[]{:S(2)}, u32[]{:S(2)}) collective-permute-start(bf16[96,256]{1,0:T(8,128)(2,1)S(1)} %get-tuple-element.55), channel_id=1, source_target_pairs={{6,0},{7,1},{4,2},{5,3},{2,4},{3,5},{0,6},{1,7},{14,8},{15,9},{12,... | collective-permute-start | bytes 147464 | tf_op jit(solution)/shard_map/ppermute | solution.py:340
  12.5 15.1 %collective-permute-start.6 = (bf16[272,512]{1,0:T(8,128)(2,1)S(1)}, bf16[272,512]{1,0:T(8,128)(2,1)S(1)}, u32[]{:S(2)}, u32[]{:S(2)}) collective-permute-start(bf16[272,512]{1,0:T(8,128)(2,1)S(1)} %collective-permute-done.1.first_ref.refs_3_), channel_id=1, source_target_pairs={{16,0},{24,8},{0,16},{8,24},{17,1},{25,9},{1,17},{9,25},{18,2},{26... | collective-permute-start | bytes 835592 | tf_op jit(solution)/shard_map/ppermute | solution.py:340
  18.3 9.2 %collective-permute-start.7 = (bf16[256,512]{1,0:T(8,128)(2,1)S(1)}, bf16[256,512]{1,0:T(8,128)(2,1)S(1)}, u32[]{:S(2)}, u32[]{:S(2)}) collective-permute-start(bf16[256,512]{1,0:T(8,128)(2,1)S(1)} %collective-permute-done.refs_4_), channel_id=1, source_target_pairs={{16,0},{24,8},{0,16},{8,24},{17,1},{25,9},{1,17},{9,25},{18,2},{26... | collective-permute-start | bytes 786440 | tf_op jit(solution)/shard_map/ppermute | solution.py:340
  19.9 6.3 %collective-permute-start.8 = (bf16[64,256]{1,0:T(8,128)(2,1)S(1)}, bf16[64,256]{1,0:T(8,128)(2,1)S(1)}, u32[]{:S(2)}, u32[]{:S(2)}) collective-permute-start(bf16[64,256]{1,0:T(8,128)(2,1)S(1)} %shard_map.99.refs_0_), channel_id=1, source_target_pairs={{6,0},{7,1},{4,2},{5,3},{2,4},{3,5},{0,6},{1,7},{14,8},{15,9},{12,... | collective-permute-start | bytes 98312 | tf_op jit(solution)/shard_map/ppermute | solution.py:340
  22.7 4.8 %collective-permute-start.9 = (bf16[64,256]{1,0:T(8,128)(2,1)S(1)}, bf16[64,256]{1,0:T(8,128)(2,1)S(1)}, u32[]{:S(2)}, u32[]{:S(2)}) collective-permute-start(bf16[64,256]{1,0:T(8,128)(2,1)S(1)} %shard_map.99.refs_0_), channel_id=1, source_target_pairs={{4,0},{5,1},{6,2},{7,3},{0,4},{1,5},{2,6},{3,7},{12,8},{13,9},{14,... | collective-permute-start | bytes 98312 | tf_op jit(solution)/shard_map/ppermute | solution.py:340
  22.8 4.8 %collective-permute-start.10 = (bf16[64,256]{1,0:T(8,128)(2,1)S(1)}, bf16[64,256]{1,0:T(8,128)(2,1)S(1)}, u32[]{:S(2)}, u32[]{:S(2)}) collective-permute-start(bf16[64,256]{1,0:T(8,128)(2,1)S(1)} %shard_map.99.refs_0_), channel_id=1, source_target_pairs={{2,0},{3,1},{0,2},{1,3},{6,4},{7,5},{4,6},{5,7},{10,8},{11,9},{8,1... | collective-permute-start | bytes 98312 | tf_op jit(solution)/shard_map/ppermute | solution.py:340
  28.4 1.4 %collective-permute-start.11 = (bf16[256,256]{1,0:T(8,128)(2,1)S(1)}, bf16[256,256]{1,0:T(8,128)(2,1)S(1)}, u32[]{:S(2)}, u32[]{:S(2)}) collective-permute-start(bf16[256,256]{1,0:T(8,128)(2,1)S(1)} %get-tuple-element.72), channel_id=1, source_target_pairs={{1,0},{0,1},{3,2},{2,3},{5,4},{4,5},{7,6},{6,7},{9,8},{8,9},{11,10... | collective-permute-start | bytes 393224 | tf_op jit(solution)/shard_map/ppermute | solution.py:340
  28.6 8.3 %collective-permute-start.15 = (bf16[256,256]{1,0:T(8,128)(2,1)S(1)}, bf16[256,256]{1,0:T(8,128)(2,1)S(1)}, u32[]{:S(2)}, u32[]{:S(2)}) collective-permute-start(bf16[256,256]{1,0:T(8,128)(2,1)S(1)} %shard_map.105.own_ref), channel_id=1, source_target_pairs={{1,0},{0,1},{3,2},{2,3},{5,4},{4,5},{7,6},{6,7},{9,8},{8,9},{11,10... | collective-permute-start | bytes 393224 | tf_op jit(solution)/shard_map/ppermute | solution.py:340
  29.9 8.0 %collective-permute-start.12 = (bf16[256,256]{1,0:T(8,128)(2,1)S(1)}, bf16[256,256]{1,0:T(8,128)(2,1)S(1)}, u32[]{:S(2)}, u32[]{:S(2)}) collective-permute-start(bf16[256,256]{1,0:T(8,128)(2,1)S(1)} %shard_map.101.refs_0_), channel_id=1, source_target_pairs={{2,0},{3,1},{0,2},{1,3},{6,4},{7,5},{4,6},{5,7},{10,8},{11,9},{8,1... | collective-permute-start | bytes 393224 | tf_op jit(solution)/shard_map/ppermute | solution.py:340
  30.6 12.9 %collective-permute-start.13 = (bf16[256,256]{1,0:T(8,128)(2,1)S(1)}, bf16[256,256]{1,0:T(8,128)(2,1)S(1)}, u32[]{:S(2)}, u32[]{:S(2)}) collective-permute-start(bf16[256,256]{1,0:T(8,128)(2,1)S(1)} %shard_map.101.refs_0_), channel_id=1, source_target_pairs={{4,0},{5,1},{6,2},{7,3},{0,4},{1,5},{2,6},{3,7},{12,8},{13,9},{14,... | collective-permute-start | bytes 393224 | tf_op jit(solution)/shard_map/ppermute | solution.py:340
  32.7 10.8 %collective-permute-start.14 = (bf16[256,256]{1,0:T(8,128)(2,1)S(1)}, bf16[256,256]{1,0:T(8,128)(2,1)S(1)}, u32[]{:S(2)}, u32[]{:S(2)}) collective-permute-start(bf16[256,256]{1,0:T(8,128)(2,1)S(1)} %shard_map.101.refs_0_), channel_id=1, source_target_pairs={{6,0},{7,1},{4,2},{5,3},{2,4},{3,5},{0,6},{1,7},{14,8},{15,9},{12,... | collective-permute-start | bytes 393224 | tf_op jit(solution)/shard_map/ppermute | solution.py:340
  43.6 1.4 %collective-permute-start.16 = (bf16[256,256]{1,0:T(8,128)(2,1)S(1)}, bf16[256,256]{1,0:T(8,128)(2,1)S(1)}, u32[]{:S(2)}, u32[]{:S(2)}) collective-permute-start(bf16[256,256]{1,0:T(8,128)(2,1)S(1)} %shard_map.102.own_ref), channel_id=1, source_target_pairs={{1,0},{0,1},{3,2},{2,3},{5,4},{4,5},{7,6},{6,7},{9,8},{8,9},{11,10... | collective-permute-start | bytes 393224 | tf_op jit(solution)/shard_map/ppermute | solution.py:340

commit v5 on v4

--- a/solution.py
+++ b/solution.py
@@ -401,6 +401,7 @@
     messages = [swapped(m, 2 * k + 2) for k, m in enumerate(messages)]
     onward[0], messages[0] = lax.optimization_barrier((onward[0], messages[0]))
     second = [permuted(onward[0], "blk", routes[-1])]
+    order = sorted(range(1, chips), key=lambda k: (k < 2, k))
     onward[1], messages = lax.optimization_barrier((onward[1], messages))
     second += [permuted(c, "blk", routes[-1]) for c in onward[1:]]
     (omega_piece,) = call(piece_body, [((piece, middle), BF16)], mine, *messages)
@@ -431,8 +432,8 @@
         first[HEADED],
         second[HEADED],
     )
-    second[-1], omega_pieces = lax.optimization_barrier((second[-1], omega_pieces[::-1]))
-    omega_pieces = omega_pieces[::-1]
+    second[-1], held = lax.optimization_barrier((second[-1], [omega_pieces[k] for k in order]))
+    omega_pieces[1:] = [held[order.index(k)] for k in range(1, chips)]
     kept, given = call(
         share_body,
         [((skel_rank, middle), F32), ((skel_rank, middle), BF16)],
@@ -456,6 +457,7 @@
         *first,
         *second,
     )
+    messages = [messages[k] for k in sorted(range(chips), key=lambda k: (k % 2, k))]
     (total,) = call(total_body, [((skel_rank, middle), BF16)], *messages)
     total, sample, top_omega = lax.optimization_barrier((total, sample, top_omega))
     (top_samples,) = call(join_body, [((skel_rank, sample_count), F32)], total, swapped(total, 1))

time: 46 us -> 44.8 us (0.974)
  starting transfers between devices: 21 us -> 20.1 us
  waiting for transfers between devices: 14.5 us -> 13.9 us
    ppermute x17, starting transfers between devices: 21 us -> 20.1 us  [permuted(): lax.ppermute(block, axis, [(route(i), i) for i in range(lax.axis_size(axi...]
    ppermute x17, waiting for transfers between devices: 14.5 us -> 13.9 us  [permuted(): lax.ppermute(block, axis, [(route(i), i) for i in range(lax.axis_size(axi...]
  transfers between devices with their start and end apart: 17 -> 17, of which waited for: 9 -> 10; matrix products, arithmetic and copies ran while one was open for 0% -> 0% of each run, Pallas kernels for 14% -> 14%
where the time goes in v5:
time: 44.8 us; the launch traced here: 44.3 us
  starting transfers between devices  20.1 us (45%)
  waiting for transfers between devices  13.9 us (31%)
  Pallas kernels  9.56 us (21%)
  between operations  0.74 us (2%)
    ppermute x17, starting transfers between devices, permuted(): lax.ppermute(block, axis, [(route(i), i) for i in range(lax.axis_size(axi...  20.1 us
    ppermute x17, waiting for transfers between devices, permuted(): lax.ppermute(block, axis, [(route(i), i) for i in range(lax.axis_size(axi...  13.9 us
    pallas_call x13, Pallas kernels, call(): pl.pallas_call(body, out_shape=[jax.ShapeDtypeStruct(s, d) for s, d in ou...  8.19 us
    pallas_call x1, Pallas kernels, on_device(): pl.pallas_call(load_body, out_shape=[jax.ShapeDtypeStruct((HEIGHT + half,...  1.37 us
  transfers between devices with their start and end apart: 17, of which 10 were waited for; matrix products, arithmetic and copies ran while one was open for 0% of the time, Pallas kernels for 14%

profile of v5, /device:TPU:0, one launch (start us, length us, event | category | flops | bytes accessed | tf_op | source)
XLA Modules:
  0.0 44.3 jit_solution(12954177530031357289)
XLA Ops:
  0.6 1.4 %shard_map.94 = (bf16[272,512]{1,0:T(8,128)(2,1)S(1)}, bf16[256,512]{1,0:T(8,128)(2,1)S(1)}, bf16[3,256,256]{2,1,0:T(8,128)(2,1)S(1)}, s32[2,5]{1,0:T(2,128)S(1)...) custom-call(bf16[3,512]{1,0:T(4,128)(2,1)} %refs_0_.1, bf16[512,512]{1,0:T(8,128)(2,1)} %refs_1_.1, ...), custom_call_target="tpu_custom_call" | custom-call | tf_op jit(solution)/shard_map/pallas_call | solution.py:368
  2.0 3.0 %collective-permute-start.1 = (bf16[272,512]{1,0:T(8,128)(2,1)S(1)}, bf16[272,512]{1,0:T(8,128)(2,1)S(1)}, u32[]{:S(2)}, u32[]{:S(2)}) collective-permute-start(bf16[272,512]{1,0:T(8,128)(2,1)S(1)} %get-tuple-element.43.refs_0_.own_ref), channel_id=1, source_target_pairs={{8,0},{0,8},{24,16},{16,24},{9,1},{1,9},{25,17},{17,25},{10,2},{2,... | collective-permute-start | bytes 835592 | tf_op jit(solution)/shard_map/ppermute | solution.py:340
  5.0 0.1 collective-permute-start
  5.1 1.2 %shard_map.95 = (bf16[272,256]{1,0:T(8,128)(2,1)S(1)}, f32[256,256]{1,0:T(8,128)S(1)}, bf16[768,512]{1,0:T(8,128)(2,1)S(1)}, bf16[768,512]{1,0:T(8,128)(2,1)S(1)...) custom-call(bf16[272,512]{1,0:T(8,128)(2,1)S(1)} %get-tuple-element.43.refs_0_.own_ref, ...), custom_call_target="tpu_custom_call" | custom-call | tf_op jit(solution)/shard_map/pallas_call | solution.py:22
  6.3 0.1 collective-permute-start.2
  6.4 1.3 %collective-permute-done.2.got_ref.refs_4_ = bf16[272,256]{1,0:T(8,128)(2,1)S(1)} collective-permute-done((bf16[272,256]{1,0:T(8,128)(2,1)S(1)}, bf16[272,256]{1,0:T(8,128)(2,1)S(1)}, u32[]{:S(2)}, u32[]{:S(2)}) %collective-permute-start.2) | collective-permute-done | bytes 139296 | tf_op jit(solution)/shard_map/ppermute | solution.py:340
  7.7 2.1 %collective-permute-start.3 = (bf16[96,256]{1,0:T(8,128)(2,1)S(1)}, bf16[96,256]{1,0:T(8,128)(2,1)S(1)}, u32[]{:S(2)}, u32[]{:S(2)}) collective-permute-start(bf16[96,256]{1,0:T(8,128)(2,1)S(1)} %get-tuple-element.51), channel_id=1, source_target_pairs={{2,0},{3,1},{0,2},{1,3},{6,4},{7,5},{4,6},{5,7},{10,8},{11,9},{8,1... | collective-permute-start | bytes 147464 | tf_op jit(solution)/shard_map/ppermute | solution.py:340
  9.8 2.6 %collective-permute-start.4 = (bf16[96,256]{1,0:T(8,128)(2,1)S(1)}, bf16[96,256]{1,0:T(8,128)(2,1)S(1)}, u32[]{:S(2)}, u32[]{:S(2)}) collective-permute-start(bf16[96,256]{1,0:T(8,128)(2,1)S(1)} %get-tuple-element.53), channel_id=1, source_target_pairs={{4,0},{5,1},{6,2},{7,3},{0,4},{1,5},{2,6},{3,7},{12,8},{13,9},{14,... | collective-permute-start | bytes 147464 | tf_op jit(solution)/shard_map/ppermute | solution.py:340
  12.4 0.0 collective-permute-start.5
  12.4 0.0 collective-permute-done.3.refs_0_.refs_1_
  12.4 0.1 collective-permute-done.1.first_ref.refs_3_
  12.5 2.1 %collective-permute-start.6 = (bf16[272,512]{1,0:T(8,128)(2,1)S(1)}, bf16[272,512]{1,0:T(8,128)(2,1)S(1)}, u32[]{:S(2)}, u32[]{:S(2)}) collective-permute-start(bf16[272,512]{1,0:T(8,128)(2,1)S(1)} %collective-permute-done.1.first_ref.refs_3_), channel_id=1, source_target_pairs={{16,0},{24,8},{0,16},{8,24},{17,1},{25,9},{1,17},{9,25},{18,2},{26... | collective-permute-start | bytes 835592 | tf_op jit(solution)/shard_map/ppermute | solution.py:340
  14.6 1.1 %collective-permute-done.4.refs_1_.refs_2_ = bf16[96,256]{1,0:T(8,128)(2,1)S(1)} collective-permute-done((bf16[96,256]{1,0:T(8,128)(2,1)S(1)}, bf16[96,256]{1,0:T(8,128)(2,1)S(1)}, u32[]{:S(2)}, u32[]{:S(2)}) %collective-permute-start.4) | collective-permute-done | bytes 49184 | tf_op jit(solution)/shard_map/ppermute | solution.py:340
  15.7 2.6 %collective-permute-done.5.refs_2_.refs_3_ = bf16[96,256]{1,0:T(8,128)(2,1)S(1)} collective-permute-done((bf16[96,256]{1,0:T(8,128)(2,1)S(1)}, bf16[96,256]{1,0:T(8,128)(2,1)S(1)}, u32[]{:S(2)}, u32[]{:S(2)}) %collective-permute-start.5) | collective-permute-done | bytes 49184 | tf_op jit(solution)/shard_map/ppermute | solution.py:340
  18.3 0.0 collective-permute-done.refs_4_
  18.3 1.5 %collective-permute-start.7 = (bf16[256,512]{1,0:T(8,128)(2,1)S(1)}, bf16[256,512]{1,0:T(8,128)(2,1)S(1)}, u32[]{:S(2)}, u32[]{:S(2)}) collective-permute-start(bf16[256,512]{1,0:T(8,128)(2,1)S(1)} %collective-permute-done.refs_4_), channel_id=1, source_target_pairs={{16,0},{24,8},{0,16},{8,24},{17,1},{25,9},{1,17},{9,25},{18,2},{26... | collective-permute-start | bytes 786440 | tf_op jit(solution)/shard_map/ppermute | solution.py:340
  19.9 1.9 %collective-permute-start.8 = (bf16[64,256]{1,0:T(8,128)(2,1)S(1)}, bf16[64,256]{1,0:T(8,128)(2,1)S(1)}, u32[]{:S(2)}, u32[]{:S(2)}) collective-permute-start(bf16[64,256]{1,0:T(8,128)(2,1)S(1)} %shard_map.99.refs_0_), channel_id=1, source_target_pairs={{4,0},{5,1},{6,2},{7,3},{0,4},{1,5},{2,6},{3,7},{12,8},{13,9},{14,... | collective-permute-start | bytes 98312 | tf_op jit(solution)/shard_map/ppermute | solution.py:340
  21.7 1.3 %collective-permute-start.9 = (bf16[64,256]{1,0:T(8,128)(2,1)S(1)}, bf16[64,256]{1,0:T(8,128)(2,1)S(1)}, u32[]{:S(2)}, u32[]{:S(2)}) collective-permute-start(bf16[64,256]{1,0:T(8,128)(2,1)S(1)} %shard_map.99.refs_0_), channel_id=1, source_target_pairs={{6,0},{7,1},{4,2},{5,3},{2,4},{3,5},{0,6},{1,7},{14,8},{15,9},{12,... | collective-permute-start | bytes 98312 | tf_op jit(solution)/shard_map/ppermute | solution.py:340
  23.1 0.3 collective-permute-start.10
  23.4 1.8 %shard_map.97 = (f32[16,256]{1,0:T(8,128)S(1)}, f32[256,512]{1,0:T(8,128)S(1)}) custom-call(bf16[96,256]{1,0:T(8,128)(2,1)S(1)} %collective-permute-done.3.refs_0_.refs_1_, bf16[96,256]{1,0:T(8,128)(2,1)S(1)} %collective-permute-done.4.refs_1_.refs_2_, bf16[96,256]{1,0:T(8,128)(2,1)S(1)} %collective-permute-done.5.refs_2_.refs_3_, ...), custom_call_target="tpu_custom_call" | custom-call | tf_op jit(solution)/shard_map/pallas_call | solution.py:22
  25.2 0.2 collective-permute-done.8.refs_2_
  25.4 2.0 %collective-permute-done.9.refs_3_ = bf16[64,256]{1,0:T(8,128)(2,1)S(1)} collective-permute-done((bf16[64,256]{1,0:T(8,128)(2,1)S(1)}, bf16[64,256]{1,0:T(8,128)(2,1)S(1)}, u32[]{:S(2)}, u32[]{:S(2)}) %collective-permute-start.9) | collective-permute-done | bytes 32800 | tf_op jit(solution)/shard_map/ppermute | solution.py:340
  27.4 0.0 collective-permute-done.10.refs_1_
  27.5 0.0 collective-permute-done.7.refs_6_
  27.5 0.0 collective-permute-done.6.second_ref.refs_5_
  27.5 0.4 shard_map.98
  27.9 0.4 shard_map.100
  28.3 0.1 collective-permute-start.11
  28.4 0.5 %collective-permute-start.15 = (bf16[256,256]{1,0:T(8,128)(2,1)S(1)}, bf16[256,256]{1,0:T(8,128)(2,1)S(1)}, u32[]{:S(2)}, u32[]{:S(2)}) collective-permute-start(bf16[256,256]{1,0:T(8,128)(2,1)S(1)} %shard_map.105.own_ref), channel_id=1, source_target_pairs={{1,0},{0,1},{3,2},{2,3},{5,4},{4,5},{7,6},{6,7},{9,8},{8,9},{11,10... | collective-permute-start | bytes 393224 | tf_op jit(solution)/shard_map/ppermute | solution.py:340
  29.0 0.8 %collective-permute-done.11.got_ref = bf16[256,256]{1,0:T(8,128)(2,1)S(1)} collective-permute-done((bf16[256,256]{1,0:T(8,128)(2,1)S(1)}, bf16[256,256]{1,0:T(8,128)(2,1)S(1)}, u32[]{:S(2)}, u32[]{:S(2)}) %collective-permute-start.11) | collective-permute-done | bytes 131104 | tf_op jit(solution)/shard_map/ppermute | solution.py:340
  29.8 1.3 %collective-permute-start.12 = (bf16[256,256]{1,0:T(8,128)(2,1)S(1)}, bf16[256,256]{1,0:T(8,128)(2,1)S(1)}, u32[]{:S(2)}, u32[]{:S(2)}) collective-permute-start(bf16[256,256]{1,0:T(8,128)(2,1)S(1)} %shard_map.101.refs_0_), channel_id=1, source_target_pairs={{4,0},{5,1},{6,2},{7,3},{0,4},{1,5},{2,6},{3,7},{12,8},{13,9},{14,... | collective-permute-start | bytes 393224 | tf_op jit(solution)/shard_map/ppermute | solution.py:340
  31.1 1.6 %collective-permute-start.13 = (bf16[256,256]{1,0:T(8,128)(2,1)S(1)}, bf16[256,256]{1,0:T(8,128)(2,1)S(1)}, u32[]{:S(2)}, u32[]{:S(2)}) collective-permute-start(bf16[256,256]{1,0:T(8,128)(2,1)S(1)} %shard_map.101.refs_0_), channel_id=1, source_target_pairs={{2,0},{3,1},{0,2},{1,3},{6,4},{7,5},{4,6},{5,7},{10,8},{11,9},{8,1... | collective-permute-start | bytes 393224 | tf_op jit(solution)/shard_map/ppermute | solution.py:340
  32.7 1.5 %collective-permute-start.14 = (bf16[256,256]{1,0:T(8,128)(2,1)S(1)}, bf16[256,256]{1,0:T(8,128)(2,1)S(1)}, u32[]{:S(2)}, u32[]{:S(2)}) collective-permute-start(bf16[256,256]{1,0:T(8,128)(2,1)S(1)} %shard_map.101.refs_0_), channel_id=1, source_target_pairs={{6,0},{7,1},{4,2},{5,3},{2,4},{3,5},{0,6},{1,7},{14,8},{15,9},{12,... | collective-permute-start | bytes 393224 | tf_op jit(solution)/shard_map/ppermute | solution.py:340
  34.2 1.0 %shard_map.103 = (bf16[512,512]{1,0:T(8,128)(2,1)S(1)}, bf16[512,512]{1,0:T(8,128)(2,1)S(1)}, f32[512,512]{1,0:T(8,128)S(1)}) custom-call(f32[12,128]{1,0:T(8,128)S(1)} %get-tuple-element.62.table_ref, bf16[272,512]{1,0:T(8,128)(2,1)S(1)} %collective-permute-done.1.first_ref.refs_3_, bf16[272,512]{1,0:T(8,128)(2,1)S(1)} %collective-permute-done.6.second_ref.refs_5_, ...), custom_call_target="tpu_custom_call" | custom-call | tf_op jit(solution)/shard_map/pallas_call | solution.py:22
  35.2 1.5 %shard_map.104 = bf16[512,512]{1,0:T(8,128)(2,1)} custom-call(f32[512,512]{1,0:T(8,128)S(1)} %get-tuple-element.72.refs_0_, bf16[512,512]{1,0:T(8,128)(2,1)S(1)} %get-tuple-element.73.refs_1_, bf16[512,512]{1,0:T(8,128)(2,1)S(1)} %get-tuple-element.74.refs_2_, bf16[272,512]{1,0:T(8,128)(2,1)S(1)} %collective-permute-done.1.first_ref.refs_3_, ...), custom_call_target="tpu_custom_call" | custom-call | tf_op jit(solution)/shard_map/pallas_call | solution.py:22
  36.7 0.0 collective-permute-done.15.other_ref
  36.7 0.9 %shard_map.106 = f32[256,512]{1,0:T(8,128)} custom-call(bf16[256,256]{1,0:T(8,128)(2,1)S(1)} %shard_map.105.own_ref, bf16[256,256]{1,0:T(8,128)(2,1)S(1)} %collective-permute-done.15.other_ref), custom_call_target="tpu_custom_call" | custom-call | tf_op jit(solution)/shard_map/pallas_call | solution.py:22
  37.6 1.8 %collective-permute-done.12.refs_1_ = bf16[256,256]{1,0:T(8,128)(2,1)S(1)} collective-permute-done((bf16[256,256]{1,0:T(8,128)(2,1)S(1)}, bf16[256,256]{1,0:T(8,128)(2,1)S(1)}, u32[]{:S(2)}, u32[]{:S(2)}) %collective-permute-start.12) | collective-permute-done | bytes 131104 | tf_op jit(solution)/shard_map/ppermute | solution.py:340
  39.4 2.6 %collective-permute-done.13.refs_2_ = bf16[256,256]{1,0:T(8,128)(2,1)S(1)} collective-permute-done((bf16[256,256]{1,0:T(8,128)(2,1)S(1)}, bf16[256,256]{1,0:T(8,128)(2,1)S(1)}, u32[]{:S(2)}, u32[]{:S(2)}) %collective-permute-start.13) | collective-permute-done | bytes 131104 | tf_op jit(solution)/shard_map/ppermute | solution.py:340
  42.0 0.0 collective-permute-done.14.refs_3_
  42.0 0.1 shard_map.102.own_ref
  42.0 0.1 collective-permute-start.16
  42.1 1.3 %collective-permute-done.16.other_ref = bf16[256,256]{1,0:T(8,128)(2,1)S(1)} collective-permute-done((bf16[256,256]{1,0:T(8,128)(2,1)S(1)}, bf16[256,256]{1,0:T(8,128)(2,1)S(1)}, u32[]{:S(2)}, u32[]{:S(2)}) %collective-permute-start.16) | collective-permute-done | bytes 131104 | tf_op jit(solution)/shard_map/ppermute | solution.py:340
  43.4 0.9 %shard_map.107 = f32[256,512]{1,0:T(8,128)} custom-call(bf16[256,256]{1,0:T(8,128)(2,1)S(1)} %shard_map.102.own_ref, bf16[256,256]{1,0:T(8,128)(2,1)S(1)} %collective-permute-done.16.other_ref), custom_call_target="tpu_custom_call" | custom-call | tf_op jit(solution)/shard_map/pallas_call | solution.py:22
  (4 shorter events, 0.1 us)
Async XLA Ops:
  2.0 10.5 %collective-permute-start.1 = (bf16[272,512]{1,0:T(8,128)(2,1)S(1)}, bf16[272,512]{1,0:T(8,128)(2,1)S(1)}, u32[]{:S(2)}, u32[]{:S(2)}) collective-permute-start(bf16[272,512]{1,0:T(8,128)(2,1)S(1)} %get-tuple-element.43.refs_0_.own_ref), channel_id=1, source_target_pairs={{8,0},{0,8},{24,16},{16,24},{9,1},{1,9},{25,17},{17,25},{10,2},{2,... | collective-permute-start | bytes 835592 | tf_op jit(solution)/shard_map/ppermute | solution.py:340
  5.0 13.3 %collective-permute-start = (bf16[256,512]{1,0:T(8,128)(2,1)S(1)}, bf16[256,512]{1,0:T(8,128)(2,1)S(1)}, u32[]{:S(2)}, u32[]{:S(2)}) collective-permute-start(bf16[256,512]{1,0:T(8,128)(2,1)S(1)} %get-tuple-element.42.refs_1_.own_late_ref), channel_id=1, source_target_pairs={{8,0},{0,8},{24,16},{16,24},{9,1},{1,9},{25,17},{17,25},{10,2},{2,... | collective-permute-start | bytes 786440 | tf_op jit(solution)/shard_map/ppermute | solution.py:340
  6.3 1.4 %collective-permute-start.2 = (bf16[272,256]{1,0:T(8,128)(2,1)S(1)}, bf16[272,256]{1,0:T(8,128)(2,1)S(1)}, u32[]{:S(2)}, u32[]{:S(2)}) collective-permute-start(bf16[272,256]{1,0:T(8,128)(2,1)S(1)} %get-tuple-element.50.sent_ref.refs_3_), channel_id=1, source_target_pairs={{1,0},{0,1},{3,2},{2,3},{5,4},{4,5},{7,6},{6,7},{9,8},{8,9},{11,10... | collective-permute-start | bytes 417800 | tf_op jit(solution)/shard_map/ppermute | solution.py:340
  7.7 4.7 %collective-permute-start.3 = (bf16[96,256]{1,0:T(8,128)(2,1)S(1)}, bf16[96,256]{1,0:T(8,128)(2,1)S(1)}, u32[]{:S(2)}, u32[]{:S(2)}) collective-permute-start(bf16[96,256]{1,0:T(8,128)(2,1)S(1)} %get-tuple-element.51), channel_id=1, source_target_pairs={{2,0},{3,1},{0,2},{1,3},{6,4},{7,5},{4,6},{5,7},{10,8},{11,9},{8,1... | collective-permute-start | bytes 147464 | tf_op jit(solution)/shard_map/ppermute | solution.py:340
  9.8 5.9 %collective-permute-start.4 = (bf16[96,256]{1,0:T(8,128)(2,1)S(1)}, bf16[96,256]{1,0:T(8,128)(2,1)S(1)}, u32[]{:S(2)}, u32[]{:S(2)}) collective-permute-start(bf16[96,256]{1,0:T(8,128)(2,1)S(1)} %get-tuple-element.53), channel_id=1, source_target_pairs={{4,0},{5,1},{6,2},{7,3},{0,4},{1,5},{2,6},{3,7},{12,8},{13,9},{14,... | collective-permute-start | bytes 147464 | tf_op jit(solution)/shard_map/ppermute | solution.py:340
  12.4 5.9 %collective-permute-start.5 = (bf16[96,256]{1,0:T(8,128)(2,1)S(1)}, bf16[96,256]{1,0:T(8,128)(2,1)S(1)}, u32[]{:S(2)}, u32[]{:S(2)}) collective-permute-start(bf16[96,256]{1,0:T(8,128)(2,1)S(1)} %get-tuple-element.54), channel_id=1, source_target_pairs={{6,0},{7,1},{4,2},{5,3},{2,4},{3,5},{0,6},{1,7},{14,8},{15,9},{12,... | collective-permute-start | bytes 147464 | tf_op jit(solution)/shard_map/ppermute | solution.py:340
  12.5 15.0 %collective-permute-start.6 = (bf16[272,512]{1,0:T(8,128)(2,1)S(1)}, bf16[272,512]{1,0:T(8,128)(2,1)S(1)}, u32[]{:S(2)}, u32[]{:S(2)}) collective-permute-start(bf16[272,512]{1,0:T(8,128)(2,1)S(1)} %collective-permute-done.1.first_ref.refs_3_), channel_id=1, source_target_pairs={{16,0},{24,8},{0,16},{8,24},{17,1},{25,9},{1,17},{9,25},{18,2},{26... | collective-permute-start | bytes 835592 | tf_op jit(solution)/shard_map/ppermute | solution.py:340
  18.3 9.1 %collective-permute-start.7 = (bf16[256,512]{1,0:T(8,128)(2,1)S(1)}, bf16[256,512]{1,0:T(8,128)(2,1)S(1)}, u32[]{:S(2)}, u32[]{:S(2)}) collective-permute-start(bf16[256,512]{1,0:T(8,128)(2,1)S(1)} %collective-permute-done.refs_4_), channel_id=1, source_target_pairs={{16,0},{24,8},{0,16},{8,24},{17,1},{25,9},{1,17},{9,25},{18,2},{26... | collective-permute-start | bytes 786440 | tf_op jit(solution)/shard_map/ppermute | solution.py:340
  19.9 5.6 %collective-permute-start.8 = (bf16[64,256]{1,0:T(8,128)(2,1)S(1)}, bf16[64,256]{1,0:T(8,128)(2,1)S(1)}, u32[]{:S(2)}, u32[]{:S(2)}) collective-permute-start(bf16[64,256]{1,0:T(8,128)(2,1)S(1)} %shard_map.99.refs_0_), channel_id=1, source_target_pairs={{4,0},{5,1},{6,2},{7,3},{0,4},{1,5},{2,6},{3,7},{12,8},{13,9},{14,... | collective-permute-start | bytes 98312 | tf_op jit(solution)/shard_map/ppermute | solution.py:340
  21.7 5.7 %collective-permute-start.9 = (bf16[64,256]{1,0:T(8,128)(2,1)S(1)}, bf16[64,256]{1,0:T(8,128)(2,1)S(1)}, u32[]{:S(2)}, u32[]{:S(2)}) collective-permute-start(bf16[64,256]{1,0:T(8,128)(2,1)S(1)} %shard_map.99.refs_0_), channel_id=1, source_target_pairs={{6,0},{7,1},{4,2},{5,3},{2,4},{3,5},{0,6},{1,7},{14,8},{15,9},{12,... | collective-permute-start | bytes 98312 | tf_op jit(solution)/shard_map/ppermute | solution.py:340
  23.1 4.4 %collective-permute-start.10 = (bf16[64,256]{1,0:T(8,128)(2,1)S(1)}, bf16[64,256]{1,0:T(8,128)(2,1)S(1)}, u32[]{:S(2)}, u32[]{:S(2)}) collective-permute-start(bf16[64,256]{1,0:T(8,128)(2,1)S(1)} %shard_map.99.refs_0_), channel_id=1, source_target_pairs={{2,0},{3,1},{0,2},{1,3},{6,4},{7,5},{4,6},{5,7},{10,8},{11,9},{8,1... | collective-permute-start | bytes 98312 | tf_op jit(solution)/shard_map/ppermute | solution.py:340
  28.3 1.4 %collective-permute-start.11 = (bf16[256,256]{1,0:T(8,128)(2,1)S(1)}, bf16[256,256]{1,0:T(8,128)(2,1)S(1)}, u32[]{:S(2)}, u32[]{:S(2)}) collective-permute-start(bf16[256,256]{1,0:T(8,128)(2,1)S(1)} %get-tuple-element.71), channel_id=1, source_target_pairs={{1,0},{0,1},{3,2},{2,3},{5,4},{4,5},{7,6},{6,7},{9,8},{8,9},{11,10... | collective-permute-start | bytes 393224 | tf_op jit(solution)/shard_map/ppermute | solution.py:340
  28.4 8.3 %collective-permute-start.15 = (bf16[256,256]{1,0:T(8,128)(2,1)S(1)}, bf16[256,256]{1,0:T(8,128)(2,1)S(1)}, u32[]{:S(2)}, u32[]{:S(2)}) collective-permute-start(bf16[256,256]{1,0:T(8,128)(2,1)S(1)} %shard_map.105.own_ref), channel_id=1, source_target_pairs={{1,0},{0,1},{3,2},{2,3},{5,4},{4,5},{7,6},{6,7},{9,8},{8,9},{11,10... | collective-permute-start | bytes 393224 | tf_op jit(solution)/shard_map/ppermute | solution.py:340
  29.8 9.6 %collective-permute-start.12 = (bf16[256,256]{1,0:T(8,128)(2,1)S(1)}, bf16[256,256]{1,0:T(8,128)(2,1)S(1)}, u32[]{:S(2)}, u32[]{:S(2)}) collective-permute-start(bf16[256,256]{1,0:T(8,128)(2,1)S(1)} %shard_map.101.refs_0_), channel_id=1, source_target_pairs={{4,0},{5,1},{6,2},{7,3},{0,4},{1,5},{2,6},{3,7},{12,8},{13,9},{14,... | collective-permute-start | bytes 393224 | tf_op jit(solution)/shard_map/ppermute | solution.py:340
  31.1 10.9 %collective-permute-start.13 = (bf16[256,256]{1,0:T(8,128)(2,1)S(1)}, bf16[256,256]{1,0:T(8,128)(2,1)S(1)}, u32[]{:S(2)}, u32[]{:S(2)}) collective-permute-start(bf16[256,256]{1,0:T(8,128)(2,1)S(1)} %shard_map.101.refs_0_), channel_id=1, source_target_pairs={{2,0},{3,1},{0,2},{1,3},{6,4},{7,5},{4,6},{5,7},{10,8},{11,9},{8,1... | collective-permute-start | bytes 393224 | tf_op jit(solution)/shard_map/ppermute | solution.py:340
  32.7 9.3 %collective-permute-start.14 = (bf16[256,256]{1,0:T(8,128)(2,1)S(1)}, bf16[256,256]{1,0:T(8,128)(2,1)S(1)}, u32[]{:S(2)}, u32[]{:S(2)}) collective-permute-start(bf16[256,256]{1,0:T(8,128)(2,1)S(1)} %shard_map.101.refs_0_), channel_id=1, source_target_pairs={{6,0},{7,1},{4,2},{5,3},{2,4},{3,5},{0,6},{1,7},{14,8},{15,9},{12,... | collective-permute-start | bytes 393224 | tf_op jit(solution)/shard_map/ppermute | solution.py:340
  42.0 1.4 %collective-permute-start.16 = (bf16[256,256]{1,0:T(8,128)(2,1)S(1)}, bf16[256,256]{1,0:T(8,128)(2,1)S(1)}, u32[]{:S(2)}, u32[]{:S(2)}) collective-permute-start(bf16[256,256]{1,0:T(8,128)(2,1)S(1)} %shard_map.102.own_ref), channel_id=1, source_target_pairs={{1,0},{0,1},{3,2},{2,3},{5,4},{4,5},{7,6},{6,7},{9,8},{8,9},{11,10... | collective-permute-start | bytes 393224 | tf_op jit(solution)/shard_map/ppermute | solution.py:340

commit v6 on v5

--- a/solution.py
+++ b/solution.py
@@ -298,9 +298,16 @@
     refs[-1][...] = near_product(*refs[:-1]).astype(BF16)
 
 
-def share_body(*refs):
-    *ins, kept_ref, given_ref = refs
-    total = near_product(*ins)
+def partial_body(start_ref, first_ref, second_ref, early_ref, late_ref, upper_ref, out_ref):
+    cut = early_ref.shape[0] - HEIGHT
+    total = start_ref[...] + dot(first_ref[:, :cut], early_ref[HEIGHT:, :])
+    total += dot(first_ref[:, cut:], late_ref[...])
+    out_ref[...] = total + dot(second_ref[:, :cut], upper_ref[HEIGHT:, :])
+
+
+def share_body(start_ref, second_ref, lower_ref, kept_ref, given_ref):
+    cut = second_ref.shape[1] - lower_ref.shape[0]
+    total = start_ref[...] + dot(second_ref[:, cut:], lower_ref[...])
     second = bit_of(lax.axis_index("leaf"), 0) == 1
     middle = total.shape[1] // 2
     low, high = total[:, :middle], total[:, middle:]
@@ -432,16 +439,17 @@
         first[HEADED],
         second[HEADED],
     )
+    (partial,) = call(
+        partial_body, [((skel_rank, sample_count), F32)], far_part, top_first, top_second, *first, second[0]
+    )
     second[-1], held = lax.optimization_barrier((second[-1], [omega_pieces[k] for k in order]))
     omega_pieces[1:] = [held[order.index(k)] for k in range(1, chips)]
     kept, given = call(
         share_body,
         [((skel_rank, middle), F32), ((skel_rank, middle), BF16)],
-        far_part,
-        top_first,
+        partial,
         top_second,
-        *first,
-        *second,
+        second[-1],
     )
     got = swapped(given, 1)
     (message,) = call(pair_body, [((skel_rank, middle), BF16)], kept, got)

time: 44.8 us -> 45 us (level)
    pallas_call x13 -> x14, Pallas kernels: 8.19 us -> 8.35 us  [call(): pl.pallas_call(body, out_shape=[jax.ShapeDtypeStruct(s, d) for s, d in ou...]
where the time goes in v6:
time: 45 us; the launch traced here: 44.5 us
  starting transfers between devices  20.1 us (45%)
  waiting for transfers between devices  13.9 us (31%)
  Pallas kernels  9.72 us (22%)
  between operations  0.75 us (2%)
    ppermute x17, starting transfers between devices, permuted(): lax.ppermute(block, axis, [(route(i), i) for i in range(lax.axis_size(axi...  20.1 us
    ppermute x17, waiting for transfers between devices, permuted(): lax.ppermute(block, axis, [(route(i), i) for i in range(lax.axis_size(axi...  13.9 us
    pallas_call x14, Pallas kernels, call(): pl.pallas_call(body, out_shape=[jax.ShapeDtypeStruct(s, d) for s, d in ou...  8.35 us
    pallas_call x1, Pallas kernels, on_device(): pl.pallas_call(load_body, out_shape=[jax.ShapeDtypeStruct((HEIGHT + half,...  1.37 us
  transfers between devices with their start and end apart: 17, of which 10 were waited for; matrix products, arithmetic and copies ran while one was open for 0% of the time, Pallas kernels for 14%

profile of v6, /device:TPU:0, one launch (start us, length us, event | category | flops | bytes accessed | tf_op | source)
XLA Modules:
  0.0 44.5 jit_solution(4498507290421482530)
XLA Ops:
  0.6 1.4 %shard_map.94 = (bf16[272,512]{1,0:T(8,128)(2,1)S(1)}, bf16[256,512]{1,0:T(8,128)(2,1)S(1)}, bf16[3,256,256]{2,1,0:T(8,128)(2,1)S(1)}, s32[2,5]{1,0:T(2,128)S(1)...) custom-call(bf16[3,512]{1,0:T(4,128)(2,1)} %refs_0_.1, bf16[512,512]{1,0:T(8,128)(2,1)} %refs_1_.1, ...), custom_call_target="tpu_custom_call" | custom-call | tf_op jit(solution)/shard_map/pallas_call | solution.py:375
  2.0 3.0 %collective-permute-start.1 = (bf16[272,512]{1,0:T(8,128)(2,1)S(1)}, bf16[272,512]{1,0:T(8,128)(2,1)S(1)}, u32[]{:S(2)}, u32[]{:S(2)}) collective-permute-start(bf16[272,512]{1,0:T(8,128)(2,1)S(1)} %get-tuple-element.43.refs_0_.own_ref), channel_id=1, source_target_pairs={{8,0},{0,8},{24,16},{16,24},{9,1},{1,9},{25,17},{17,25},{10,2},{2,... | collective-permute-start | bytes 835592 | tf_op jit(solution)/shard_map/ppermute | solution.py:347
  5.0 0.1 collective-permute-start
  5.1 1.2 %shard_map.95 = (bf16[272,256]{1,0:T(8,128)(2,1)S(1)}, f32[256,256]{1,0:T(8,128)S(1)}, bf16[768,512]{1,0:T(8,128)(2,1)S(1)}, bf16[768,512]{1,0:T(8,128)(2,1)S(1)...) custom-call(bf16[272,512]{1,0:T(8,128)(2,1)S(1)} %get-tuple-element.43.refs_0_.own_ref, ...), custom_call_target="tpu_custom_call" | custom-call | tf_op jit(solution)/shard_map/pallas_call | solution.py:22
  6.3 0.1 collective-permute-start.2
  6.4 1.3 %collective-permute-done.2.got_ref.refs_4_ = bf16[272,256]{1,0:T(8,128)(2,1)S(1)} collective-permute-done((bf16[272,256]{1,0:T(8,128)(2,1)S(1)}, bf16[272,256]{1,0:T(8,128)(2,1)S(1)}, u32[]{:S(2)}, u32[]{:S(2)}) %collective-permute-start.2) | collective-permute-done | bytes 139296 | tf_op jit(solution)/shard_map/ppermute | solution.py:347
  7.7 2.1 %collective-permute-start.3 = (bf16[96,256]{1,0:T(8,128)(2,1)S(1)}, bf16[96,256]{1,0:T(8,128)(2,1)S(1)}, u32[]{:S(2)}, u32[]{:S(2)}) collective-permute-start(bf16[96,256]{1,0:T(8,128)(2,1)S(1)} %get-tuple-element.51), channel_id=1, source_target_pairs={{2,0},{3,1},{0,2},{1,3},{6,4},{7,5},{4,6},{5,7},{10,8},{11,9},{8,1... | collective-permute-start | bytes 147464 | tf_op jit(solution)/shard_map/ppermute | solution.py:347
  9.8 2.6 %collective-permute-start.4 = (bf16[96,256]{1,0:T(8,128)(2,1)S(1)}, bf16[96,256]{1,0:T(8,128)(2,1)S(1)}, u32[]{:S(2)}, u32[]{:S(2)}) collective-permute-start(bf16[96,256]{1,0:T(8,128)(2,1)S(1)} %get-tuple-element.53), channel_id=1, source_target_pairs={{4,0},{5,1},{6,2},{7,3},{0,4},{1,5},{2,6},{3,7},{12,8},{13,9},{14,... | collective-permute-start | bytes 147464 | tf_op jit(solution)/shard_map/ppermute | solution.py:347
  12.4 0.0 collective-permute-start.5
  12.4 0.0 collective-permute-done.3.refs_0_.refs_1_
  12.4 0.1 collective-permute-done.1.first_ref.early_ref.refs_3_
  12.5 2.1 %collective-permute-start.6 = (bf16[272,512]{1,0:T(8,128)(2,1)S(1)}, bf16[272,512]{1,0:T(8,128)(2,1)S(1)}, u32[]{:S(2)}, u32[]{:S(2)}) collective-permute-start(bf16[272,512]{1,0:T(8,128)(2,1)S(1)} %collective-permute-done.1.first_ref.early_ref.refs_3_), channel_id=1, source_target_pairs={{16,0},{24,8},{0,16},{8,24},{17,1},{25,9},{1,17},{9,25},{18,2},{26... | collective-permute-start | bytes 835592 | tf_op jit(solution)/shard_map/ppermute | solution.py:347
  14.6 1.1 %collective-permute-done.4.refs_1_.refs_2_ = bf16[96,256]{1,0:T(8,128)(2,1)S(1)} collective-permute-done((bf16[96,256]{1,0:T(8,128)(2,1)S(1)}, bf16[96,256]{1,0:T(8,128)(2,1)S(1)}, u32[]{:S(2)}, u32[]{:S(2)}) %collective-permute-start.4) | collective-permute-done | bytes 49184 | tf_op jit(solution)/shard_map/ppermute | solution.py:347
  15.7 2.6 %collective-permute-done.5.refs_2_.refs_3_ = bf16[96,256]{1,0:T(8,128)(2,1)S(1)} collective-permute-done((bf16[96,256]{1,0:T(8,128)(2,1)S(1)}, bf16[96,256]{1,0:T(8,128)(2,1)S(1)}, u32[]{:S(2)}, u32[]{:S(2)}) %collective-permute-start.5) | collective-permute-done | bytes 49184 | tf_op jit(solution)/shard_map/ppermute | solution.py:347
  18.3 0.0 collective-permute-done.late_ref.refs_4_
  18.3 1.5 %collective-permute-start.7 = (bf16[256,512]{1,0:T(8,128)(2,1)S(1)}, bf16[256,512]{1,0:T(8,128)(2,1)S(1)}, u32[]{:S(2)}, u32[]{:S(2)}) collective-permute-start(bf16[256,512]{1,0:T(8,128)(2,1)S(1)} %collective-permute-done.late_ref.refs_4_), channel_id=1, source_target_pairs={{16,0},{24,8},{0,16},{8,24},{17,1},{25,9},{1,17},{9,25},{18,2},{26... | collective-permute-start | bytes 786440 | tf_op jit(solution)/shard_map/ppermute | solution.py:347
  19.9 1.9 %collective-permute-start.8 = (bf16[64,256]{1,0:T(8,128)(2,1)S(1)}, bf16[64,256]{1,0:T(8,128)(2,1)S(1)}, u32[]{:S(2)}, u32[]{:S(2)}) collective-permute-start(bf16[64,256]{1,0:T(8,128)(2,1)S(1)} %shard_map.100.refs_0_), channel_id=1, source_target_pairs={{4,0},{5,1},{6,2},{7,3},{0,4},{1,5},{2,6},{3,7},{12,8},{13,9},{14,... | collective-permute-start | bytes 98312 | tf_op jit(solution)/shard_map/ppermute | solution.py:347
  21.7 1.3 %collective-permute-start.9 = (bf16[64,256]{1,0:T(8,128)(2,1)S(1)}, bf16[64,256]{1,0:T(8,128)(2,1)S(1)}, u32[]{:S(2)}, u32[]{:S(2)}) collective-permute-start(bf16[64,256]{1,0:T(8,128)(2,1)S(1)} %shard_map.100.refs_0_), channel_id=1, source_target_pairs={{6,0},{7,1},{4,2},{5,3},{2,4},{3,5},{0,6},{1,7},{14,8},{15,9},{12,... | collective-permute-start | bytes 98312 | tf_op jit(solution)/shard_map/ppermute | solution.py:347
  23.1 0.3 collective-permute-start.10
  23.4 1.8 %shard_map.97 = (f32[16,256]{1,0:T(8,128)S(1)}, f32[256,512]{1,0:T(8,128)S(1)}) custom-call(bf16[96,256]{1,0:T(8,128)(2,1)S(1)} %collective-permute-done.3.refs_0_.refs_1_, bf16[96,256]{1,0:T(8,128)(2,1)S(1)} %collective-permute-done.4.refs_1_.refs_2_, bf16[96,256]{1,0:T(8,128)(2,1)S(1)} %collective-permute-done.5.refs_2_.refs_3_, ...), custom_call_target="tpu_custom_call" | custom-call | tf_op jit(solution)/shard_map/pallas_call | solution.py:22
  25.2 0.2 collective-permute-done.8.refs_2_
  25.4 2.0 %collective-permute-done.9.refs_3_ = bf16[64,256]{1,0:T(8,128)(2,1)S(1)} collective-permute-done((bf16[64,256]{1,0:T(8,128)(2,1)S(1)}, bf16[64,256]{1,0:T(8,128)(2,1)S(1)}, u32[]{:S(2)}, u32[]{:S(2)}) %collective-permute-start.9) | collective-permute-done | bytes 32800 | tf_op jit(solution)/shard_map/ppermute | solution.py:347
  27.4 0.0 collective-permute-done.10.refs_1_
  27.5 0.0 collective-permute-done.7.lower_ref.refs_6_
  27.5 0.0 collective-permute-done.6.second_ref.upper_ref.refs_5_
  27.5 0.4 shard_map.98
  27.9 0.4 shard_map.99.start_ref
  28.3 0.2 shard_map.101
  28.5 0.1 collective-permute-start.11
  28.6 0.5 %collective-permute-start.15 = (bf16[256,256]{1,0:T(8,128)(2,1)S(1)}, bf16[256,256]{1,0:T(8,128)(2,1)S(1)}, u32[]{:S(2)}, u32[]{:S(2)}) collective-permute-start(bf16[256,256]{1,0:T(8,128)(2,1)S(1)} %shard_map.106.own_ref), channel_id=1, source_target_pairs={{1,0},{0,1},{3,2},{2,3},{5,4},{4,5},{7,6},{6,7},{9,8},{8,9},{11,10... | collective-permute-start | bytes 393224 | tf_op jit(solution)/shard_map/ppermute | solution.py:347
  29.1 0.8 %collective-permute-done.11.got_ref = bf16[256,256]{1,0:T(8,128)(2,1)S(1)} collective-permute-done((bf16[256,256]{1,0:T(8,128)(2,1)S(1)}, bf16[256,256]{1,0:T(8,128)(2,1)S(1)}, u32[]{:S(2)}, u32[]{:S(2)}) %collective-permute-start.11) | collective-permute-done | bytes 131104 | tf_op jit(solution)/shard_map/ppermute | solution.py:347
  29.9 1.3 %collective-permute-start.12 = (bf16[256,256]{1,0:T(8,128)(2,1)S(1)}, bf16[256,256]{1,0:T(8,128)(2,1)S(1)}, u32[]{:S(2)}, u32[]{:S(2)}) collective-permute-start(bf16[256,256]{1,0:T(8,128)(2,1)S(1)} %shard_map.102.refs_0_), channel_id=1, source_target_pairs={{4,0},{5,1},{6,2},{7,3},{0,4},{1,5},{2,6},{3,7},{12,8},{13,9},{14,... | collective-permute-start | bytes 393224 | tf_op jit(solution)/shard_map/ppermute | solution.py:347
  31.2 1.6 %collective-permute-start.13 = (bf16[256,256]{1,0:T(8,128)(2,1)S(1)}, bf16[256,256]{1,0:T(8,128)(2,1)S(1)}, u32[]{:S(2)}, u32[]{:S(2)}) collective-permute-start(bf16[256,256]{1,0:T(8,128)(2,1)S(1)} %shard_map.102.refs_0_), channel_id=1, source_target_pairs={{2,0},{3,1},{0,2},{1,3},{6,4},{7,5},{4,6},{5,7},{10,8},{11,9},{8,1... | collective-permute-start | bytes 393224 | tf_op jit(solution)/shard_map/ppermute | solution.py:347
  32.9 1.5 %collective-permute-start.14 = (bf16[256,256]{1,0:T(8,128)(2,1)S(1)}, bf16[256,256]{1,0:T(8,128)(2,1)S(1)}, u32[]{:S(2)}, u32[]{:S(2)}) collective-permute-start(bf16[256,256]{1,0:T(8,128)(2,1)S(1)} %shard_map.102.refs_0_), channel_id=1, source_target_pairs={{6,0},{7,1},{4,2},{5,3},{2,4},{3,5},{0,6},{1,7},{14,8},{15,9},{12,... | collective-permute-start | bytes 393224 | tf_op jit(solution)/shard_map/ppermute | solution.py:347
  34.4 1.0 %shard_map.104 = (bf16[512,512]{1,0:T(8,128)(2,1)S(1)}, bf16[512,512]{1,0:T(8,128)(2,1)S(1)}, f32[512,512]{1,0:T(8,128)S(1)}) custom-call(f32[12,128]{1,0:T(8,128)S(1)} %get-tuple-element.62.table_ref, bf16[272,512]{1,0:T(8,128)(2,1)S(1)} %collective-permute-done.1.first_ref.early_ref.refs_3_, ...), custom_call_target="tpu_custom_call" | custom-call | tf_op jit(solution)/shard_map/pallas_call | solution.py:22
  35.4 1.5 %shard_map.105 = bf16[512,512]{1,0:T(8,128)(2,1)} custom-call(f32[512,512]{1,0:T(8,128)S(1)} %get-tuple-element.72.refs_0_, bf16[512,512]{1,0:T(8,128)(2,1)S(1)} %get-tuple-element.73.refs_1_, bf16[512,512]{1,0:T(8,128)(2,1)S(1)} %get-tuple-element.74.refs_2_, bf16[272,512]{1,0:T(8,128)(2,1)S(1)} %collective-permute-done.1.first_ref.early_ref.refs_3_, ...), custom_call_target="tpu_custom_call" | custom-call | tf_op jit(solution)/shard_map/pallas_call | solution.py:22
  36.9 0.0 collective-permute-done.15.other_ref
  36.9 0.9 %shard_map.107 = f32[256,512]{1,0:T(8,128)} custom-call(bf16[256,256]{1,0:T(8,128)(2,1)S(1)} %shard_map.106.own_ref, bf16[256,256]{1,0:T(8,128)(2,1)S(1)} %collective-permute-done.15.other_ref), custom_call_target="tpu_custom_call" | custom-call | tf_op jit(solution)/shard_map/pallas_call | solution.py:22
  37.7 1.8 %collective-permute-done.12.refs_1_ = bf16[256,256]{1,0:T(8,128)(2,1)S(1)} collective-permute-done((bf16[256,256]{1,0:T(8,128)(2,1)S(1)}, bf16[256,256]{1,0:T(8,128)(2,1)S(1)}, u32[]{:S(2)}, u32[]{:S(2)}) %collective-permute-start.12) | collective-permute-done | bytes 131104 | tf_op jit(solution)/shard_map/ppermute | solution.py:347
  39.5 2.6 %collective-permute-done.13.refs_2_ = bf16[256,256]{1,0:T(8,128)(2,1)S(1)} collective-permute-done((bf16[256,256]{1,0:T(8,128)(2,1)S(1)}, bf16[256,256]{1,0:T(8,128)(2,1)S(1)}, u32[]{:S(2)}, u32[]{:S(2)}) %collective-permute-start.13) | collective-permute-done | bytes 131104 | tf_op jit(solution)/shard_map/ppermute | solution.py:347
  42.1 0.0 collective-permute-done.14.refs_3_
  42.1 0.1 shard_map.103.own_ref
  42.2 0.1 collective-permute-start.16
  42.3 1.3 %collective-permute-done.16.other_ref = bf16[256,256]{1,0:T(8,128)(2,1)S(1)} collective-permute-done((bf16[256,256]{1,0:T(8,128)(2,1)S(1)}, bf16[256,256]{1,0:T(8,128)(2,1)S(1)}, u32[]{:S(2)}, u32[]{:S(2)}) %collective-permute-start.16) | collective-permute-done | bytes 131104 | tf_op jit(solution)/shard_map/ppermute | solution.py:347
  43.6 0.9 %shard_map.108 = f32[256,512]{1,0:T(8,128)} custom-call(bf16[256,256]{1,0:T(8,128)(2,1)S(1)} %shard_map.103.own_ref, bf16[256,256]{1,0:T(8,128)(2,1)S(1)} %collective-permute-done.16.other_ref), custom_call_target="tpu_custom_call" | custom-call | tf_op jit(solution)/shard_map/pallas_call | solution.py:22
  (4 shorter events, 0.1 us)
Async XLA Ops:
  2.0 10.5 %collective-permute-start.1 = (bf16[272,512]{1,0:T(8,128)(2,1)S(1)}, bf16[272,512]{1,0:T(8,128)(2,1)S(1)}, u32[]{:S(2)}, u32[]{:S(2)}) collective-permute-start(bf16[272,512]{1,0:T(8,128)(2,1)S(1)} %get-tuple-element.43.refs_0_.own_ref), channel_id=1, source_target_pairs={{8,0},{0,8},{24,16},{16,24},{9,1},{1,9},{25,17},{17,25},{10,2},{2,... | collective-permute-start | bytes 835592 | tf_op jit(solution)/shard_map/ppermute | solution.py:347
  5.0 13.3 %collective-permute-start = (bf16[256,512]{1,0:T(8,128)(2,1)S(1)}, bf16[256,512]{1,0:T(8,128)(2,1)S(1)}, u32[]{:S(2)}, u32[]{:S(2)}) collective-permute-start(bf16[256,512]{1,0:T(8,128)(2,1)S(1)} %get-tuple-element.42.refs_1_.own_late_ref), channel_id=1, source_target_pairs={{8,0},{0,8},{24,16},{16,24},{9,1},{1,9},{25,17},{17,25},{10,2},{2,... | collective-permute-start | bytes 786440 | tf_op jit(solution)/shard_map/ppermute | solution.py:347
  6.3 1.4 %collective-permute-start.2 = (bf16[272,256]{1,0:T(8,128)(2,1)S(1)}, bf16[272,256]{1,0:T(8,128)(2,1)S(1)}, u32[]{:S(2)}, u32[]{:S(2)}) collective-permute-start(bf16[272,256]{1,0:T(8,128)(2,1)S(1)} %get-tuple-element.50.sent_ref.refs_3_), channel_id=1, source_target_pairs={{1,0},{0,1},{3,2},{2,3},{5,4},{4,5},{7,6},{6,7},{9,8},{8,9},{11,10... | collective-permute-start | bytes 417800 | tf_op jit(solution)/shard_map/ppermute | solution.py:347
  7.7 4.7 %collective-permute-start.3 = (bf16[96,256]{1,0:T(8,128)(2,1)S(1)}, bf16[96,256]{1,0:T(8,128)(2,1)S(1)}, u32[]{:S(2)}, u32[]{:S(2)}) collective-permute-start(bf16[96,256]{1,0:T(8,128)(2,1)S(1)} %get-tuple-element.51), channel_id=1, source_target_pairs={{2,0},{3,1},{0,2},{1,3},{6,4},{7,5},{4,6},{5,7},{10,8},{11,9},{8,1... | collective-permute-start | bytes 147464 | tf_op jit(solution)/shard_map/ppermute | solution.py:347
  9.8 5.9 %collective-permute-start.4 = (bf16[96,256]{1,0:T(8,128)(2,1)S(1)}, bf16[96,256]{1,0:T(8,128)(2,1)S(1)}, u32[]{:S(2)}, u32[]{:S(2)}) collective-permute-start(bf16[96,256]{1,0:T(8,128)(2,1)S(1)} %get-tuple-element.53), channel_id=1, source_target_pairs={{4,0},{5,1},{6,2},{7,3},{0,4},{1,5},{2,6},{3,7},{12,8},{13,9},{14,... | collective-permute-start | bytes 147464 | tf_op jit(solution)/shard_map/ppermute | solution.py:347
  12.4 5.9 %collective-permute-start.5 = (bf16[96,256]{1,0:T(8,128)(2,1)S(1)}, bf16[96,256]{1,0:T(8,128)(2,1)S(1)}, u32[]{:S(2)}, u32[]{:S(2)}) collective-permute-start(bf16[96,256]{1,0:T(8,128)(2,1)S(1)} %get-tuple-element.54), channel_id=1, source_target_pairs={{6,0},{7,1},{4,2},{5,3},{2,4},{3,5},{0,6},{1,7},{14,8},{15,9},{12,... | collective-permute-start | bytes 147464 | tf_op jit(solution)/shard_map/ppermute | solution.py:347
  12.5 15.0 %collective-permute-start.6 = (bf16[272,512]{1,0:T(8,128)(2,1)S(1)}, bf16[272,512]{1,0:T(8,128)(2,1)S(1)}, u32[]{:S(2)}, u32[]{:S(2)}) collective-permute-start(bf16[272,512]{1,0:T(8,128)(2,1)S(1)} %collective-permute-done.1.first_ref.early_ref.refs_3_), channel_id=1, source_target_pairs={{16,0},{24,8},{0,16},{8,24},{17,1},{25,9},{1,17},{9,25},{18,2},{26... | collective-permute-start | bytes 835592 | tf_op jit(solution)/shard_map/ppermute | solution.py:347
  18.3 9.1 %collective-permute-start.7 = (bf16[256,512]{1,0:T(8,128)(2,1)S(1)}, bf16[256,512]{1,0:T(8,128)(2,1)S(1)}, u32[]{:S(2)}, u32[]{:S(2)}) collective-permute-start(bf16[256,512]{1,0:T(8,128)(2,1)S(1)} %collective-permute-done.late_ref.refs_4_), channel_id=1, source_target_pairs={{16,0},{24,8},{0,16},{8,24},{17,1},{25,9},{1,17},{9,25},{18,2},{26... | collective-permute-start | bytes 786440 | tf_op jit(solution)/shard_map/ppermute | solution.py:347
  19.9 5.6 %collective-permute-start.8 = (bf16[64,256]{1,0:T(8,128)(2,1)S(1)}, bf16[64,256]{1,0:T(8,128)(2,1)S(1)}, u32[]{:S(2)}, u32[]{:S(2)}) collective-permute-start(bf16[64,256]{1,0:T(8,128)(2,1)S(1)} %shard_map.100.refs_0_), channel_id=1, source_target_pairs={{4,0},{5,1},{6,2},{7,3},{0,4},{1,5},{2,6},{3,7},{12,8},{13,9},{14,... | collective-permute-start | bytes 98312 | tf_op jit(solution)/shard_map/ppermute | solution.py:347
  21.7 5.7 %collective-permute-start.9 = (bf16[64,256]{1,0:T(8,128)(2,1)S(1)}, bf16[64,256]{1,0:T(8,128)(2,1)S(1)}, u32[]{:S(2)}, u32[]{:S(2)}) collective-permute-start(bf16[64,256]{1,0:T(8,128)(2,1)S(1)} %shard_map.100.refs_0_), channel_id=1, source_target_pairs={{6,0},{7,1},{4,2},{5,3},{2,4},{3,5},{0,6},{1,7},{14,8},{15,9},{12,... | collective-permute-start | bytes 98312 | tf_op jit(solution)/shard_map/ppermute | solution.py:347
  23.1 4.4 %collective-permute-start.10 = (bf16[64,256]{1,0:T(8,128)(2,1)S(1)}, bf16[64,256]{1,0:T(8,128)(2,1)S(1)}, u32[]{:S(2)}, u32[]{:S(2)}) collective-permute-start(bf16[64,256]{1,0:T(8,128)(2,1)S(1)} %shard_map.100.refs_0_), channel_id=1, source_target_pairs={{2,0},{3,1},{0,2},{1,3},{6,4},{7,5},{4,6},{5,7},{10,8},{11,9},{8,1... | collective-permute-start | bytes 98312 | tf_op jit(solution)/shard_map/ppermute | solution.py:347
  28.5 1.4 %collective-permute-start.11 = (bf16[256,256]{1,0:T(8,128)(2,1)S(1)}, bf16[256,256]{1,0:T(8,128)(2,1)S(1)}, u32[]{:S(2)}, u32[]{:S(2)}) collective-permute-start(bf16[256,256]{1,0:T(8,128)(2,1)S(1)} %get-tuple-element.71), channel_id=1, source_target_pairs={{1,0},{0,1},{3,2},{2,3},{5,4},{4,5},{7,6},{6,7},{9,8},{8,9},{11,10... | collective-permute-start | bytes 393224 | tf_op jit(solution)/shard_map/ppermute | solution.py:347
  28.6 8.3 %collective-permute-start.15 = (bf16[256,256]{1,0:T(8,128)(2,1)S(1)}, bf16[256,256]{1,0:T(8,128)(2,1)S(1)}, u32[]{:S(2)}, u32[]{:S(2)}) collective-permute-start(bf16[256,256]{1,0:T(8,128)(2,1)S(1)} %shard_map.106.own_ref), channel_id=1, source_target_pairs={{1,0},{0,1},{3,2},{2,3},{5,4},{4,5},{7,6},{6,7},{9,8},{8,9},{11,10... | collective-permute-start | bytes 393224 | tf_op jit(solution)/shard_map/ppermute | solution.py:347
  29.9 9.6 %collective-permute-start.12 = (bf16[256,256]{1,0:T(8,128)(2,1)S(1)}, bf16[256,256]{1,0:T(8,128)(2,1)S(1)}, u32[]{:S(2)}, u32[]{:S(2)}) collective-permute-start(bf16[256,256]{1,0:T(8,128)(2,1)S(1)} %shard_map.102.refs_0_), channel_id=1, source_target_pairs={{4,0},{5,1},{6,2},{7,3},{0,4},{1,5},{2,6},{3,7},{12,8},{13,9},{14,... | collective-permute-start | bytes 393224 | tf_op jit(solution)/shard_map/ppermute | solution.py:347
  31.2 10.9 %collective-permute-start.13 = (bf16[256,256]{1,0:T(8,128)(2,1)S(1)}, bf16[256,256]{1,0:T(8,128)(2,1)S(1)}, u32[]{:S(2)}, u32[]{:S(2)}) collective-permute-start(bf16[256,256]{1,0:T(8,128)(2,1)S(1)} %shard_map.102.refs_0_), channel_id=1, source_target_pairs={{2,0},{3,1},{0,2},{1,3},{6,4},{7,5},{4,6},{5,7},{10,8},{11,9},{8,1... | collective-permute-start | bytes 393224 | tf_op jit(solution)/shard_map/ppermute | solution.py:347
  32.9 9.3 %collective-permute-start.14 = (bf16[256,256]{1,0:T(8,128)(2,1)S(1)}, bf16[256,256]{1,0:T(8,128)(2,1)S(1)}, u32[]{:S(2)}, u32[]{:S(2)}) collective-permute-start(bf16[256,256]{1,0:T(8,128)(2,1)S(1)} %shard_map.102.refs_0_), channel_id=1, source_target_pairs={{6,0},{7,1},{4,2},{5,3},{2,4},{3,5},{0,6},{1,7},{14,8},{15,9},{12,... | collective-permute-start | bytes 393224 | tf_op jit(solution)/shard_map/ppermute | solution.py:347
  42.2 1.4 %collective-permute-start.16 = (bf16[256,256]{1,0:T(8,128)(2,1)S(1)}, bf16[256,256]{1,0:T(8,128)(2,1)S(1)}, u32[]{:S(2)}, u32[]{:S(2)}) collective-permute-start(bf16[256,256]{1,0:T(8,128)(2,1)S(1)} %shard_map.103.own_ref), channel_id=1, source_target_pairs={{1,0},{0,1},{3,2},{2,3},{5,4},{4,5},{7,6},{6,7},{9,8},{8,9},{11,10... | collective-permute-start | bytes 393224 | tf_op jit(solution)/shard_map/ppermute | solution.py:347
